TPU v7x, 256 devices: a whole 4x4x8 slice. The times are simulated.
256 devices in a mesh: ctx: 64 (over x_lo, z, y), fsdp: 4 (over x_hi, core).
Axes of the slice: x: 4 (x_hi: 2, x_lo: 2; x = x_hi * 2 + x_lo), y: 4, z: 8, core: 2. Of those that a mesh axis runs over, the one named last changes fastest.
Arguments:
- q_raw: bfloat16 [8192, 2560], P('ctx', 'fsdp'), may hold values from -3000 to 3000
- k_raw: bfloat16 [8192, 2560], P('ctx', 'fsdp'), may hold values from -3000 to 3000
- values: bfloat16 [8192, 2560], P('ctx', 'fsdp'), may hold values from -6 to 6
- positions: int32 [8192, 3], P('ctx'), may hold values from 0 to 79, as said below
- cotangent: bfloat16 [8192, 5120], P('ctx'), may hold values from -6 to 6
- out_weight: bfloat16 [2560, 5120], P('fsdp'), may hold values from -0.078125 to 0.078125
- modulation: float32 [50, 5120], replicated, may hold values from -4 to 4
- step_index: int32 [1], replicated, may hold values from 0 to 49
Outputs:
- query_grad: bfloat16 [8192, 2560], P('ctx', 'fsdp')
- key_grad: bfloat16 [8192, 2560], P('ctx', 'fsdp')
- value_grad: bfloat16 [8192, 2560], P('ctx', 'fsdp')
Inputs may be any that keep to these rules, and one draw needn't show every extreme that they name: `positions`: frame, row and column coordinates of each token in the latent grid.
All inputs are finite; a program needn't handle non-finite values.
Results may differ from a plain program's by a relative error of at most 0.034.
Values may be sent and summed in bfloat16 or wider, within the bound.
No kernel may reach another device: no remote copies, remote signals or barrier semaphores. Data moves between devices by JAX's collectives and lax.ppermute only.
A program may use at most 192 MiB of HBM per device.

v0:
```python
import functools
import math

import jax
import jax.numpy as jnp
import numpy as np
from jax import lax
from jax.experimental import pallas as pl
from jax.experimental.pallas import tpu as pltpu
from jax.sharding import Mesh
from jax.sharding import PartitionSpec as P

HEAD_DIM = 128
EPSILON = 1e-06
LOG2E = math.log2(math.e)
SCALING = 1.0 / math.sqrt(HEAD_DIM)
TOKENS_AXES = ("xl", "z", "y")
HEADS_AXES = ("xh", "c")
VMEM_LIMIT = 58 * 1024 * 1024
NT = (((1,), (1,)), ((), ()))
TN = (((0,), (0,)), ((), ()))


def angle_table(head_size):
    side_dim = 2 * (head_size // 6)
    first_dim = head_size - 2 * side_dim
    freq_table = np.zeros((3, head_size // 2), np.float32)
    column = 0
    for axis_number, group_dim in enumerate([first_dim, side_dim, side_dim]):
        for pair_index in range(group_dim // 2):
            freq_table[axis_number, column] = 10000.0 ** (-2.0 * pair_index / group_dim)
            column += 1
    return freq_table


def rotation(positions, heads_count):
    angles = jnp.dot(
        positions.astype(jnp.float32),
        jnp.asarray(np.repeat(angle_table(HEAD_DIM), 2, axis=1)),
        precision=lax.Precision.HIGHEST,
    )
    parity = jnp.tile(jnp.array([-1.0, 1.0], jnp.float32), HEAD_DIM // 2)
    cosine = jnp.cos(angles)
    signed_sine = jnp.sin(angles) * parity[None, :]
    return jnp.tile(cosine, (1, heads_count)), jnp.tile(signed_sine, (1, heads_count))


def rotate(source, cosine, signed_sine, direction):
    column_ids = jnp.arange(source.shape[1])
    partner = jnp.where(
        column_ids % 2 == 0, jnp.roll(source, -1, axis=1), jnp.roll(source, 1, axis=1)
    )
    return source * cosine + direction * partner * signed_sine


def shift(x, axis, distance):
    size = lax.axis_size(axis)
    return lax.ppermute(x, axis, [(i, (i + distance) % size) for i in range(size)])


def flip(x, axis):
    return lax.ppermute(x, axis, [(0, 1), (1, 0)])


def sum_heads_axes(x):
    total = x
    for mask in (1, 2, 3):
        total = total + lax.ppermute(x, HEADS_AXES, [(i, i ^ mask) for i in range(4)])
    return total


def ring_gather(x):
    half = x.shape[0] // 2
    left, right = x, x
    from_left, from_right = [], []
    for _ in range(3):
        left, right = shift(left, "z", 1), shift(right, "z", -1)
        from_left.append(left)
        from_right.append(right)
    far = [shift(left[:half], "z", 1), shift(right[half:], "z", -1)]
    return [[x], *[[b] for b in from_left], far, *[[b] for b in from_right[::-1]]]


def ring_reduce(blocks):
    half = blocks[4].shape[0] // 2
    low, high = shift(blocks[4][:half], "z", -1), shift(blocks[4][half:], "z", 1)
    left = blocks[3] + jnp.concatenate([low, jnp.zeros_like(low)], axis=0)
    right = blocks[5] + jnp.concatenate([jnp.zeros_like(high), high], axis=0)
    for near in (2, 1):
        left = blocks[near] + shift(left, "z", -1)
        right = blocks[8 - near] + shift(right, "z", 1)
    f32 = jnp.float32
    return (
        blocks[0].astype(f32)
        + shift(left, "z", -1).astype(f32)
        + shift(right, "z", 1).astype(f32)
    )


def plane_gather(x):
    rows = x.shape[0]
    pair = jnp.concatenate([x, flip(x, "xl")], axis=0)
    left, right = shift(pair, "y", 1), shift(pair, "y", -1)
    low, high = shift(left[:rows], "y", 1), shift(right[rows:], "y", -1)
    return [pair, left, low, high, right]


def fill(target, refs):
    row = 0
    for ref in refs:
        count = ref.shape[0]
        target[row : row + count, :] = ref[...]
        row += count


def owner_of(index_ref, place):
    return lax.rem(index_ref[0] + 8 - place, 8)


def key_owner_of(index_ref, place):
    d, a = divmod(place, 2)
    return 4 * lax.rem(index_ref[2] + a, 2) + lax.rem(index_ref[1] + 4 - d, 4)


def split(refs, counts):
    out, first = [], 0
    for count in counts:
        out.append(refs[first : first + count])
        first += count
    return out, refs[first:]


def stats_kernel(places, counts, heads, index_ref, *refs):
    sides, (stats_ref, *scratch) = split(refs, counts)
    for target, side in zip(scratch, sides):
        fill(target, side)
    q_ref, c_ref, k_ref, v_ref = scratch
    h = pl.program_id(0)
    for t in range(0, len(places), 2):
        cols = slice(t * 128, t * 128 + 256)
        s = lax.dot_general(k_ref[...], q_ref[cols, :], NT, preferred_element_type=jnp.float32)
        g = lax.dot_general(v_ref[...], c_ref[cols, :], NT, preferred_element_type=jnp.float32)
        s = s * (SCALING * LOG2E)
        top = jnp.max(s, axis=0, keepdims=True)
        e = jnp.exp2(s - top)
        total = jnp.sum(e, axis=0, keepdims=True)
        weight = jnp.sum(e * g, axis=0, keepdims=True)
        for side in (0, 1):
            owner = owner_of(index_ref, places[t + side])
            part = slice(side * 128, side * 128 + 128)
            for kind, row in enumerate((top, total, weight)):
                stats_ref[owner, pl.ds(heads * kind + h, 1), :] = row[:, part]


def grads_kernel(places, counts, heads, index_ref, *refs):
    sides, (totals_ref, *rest) = split(refs, counts)
    dq_refs, dkv_ref, scratch, (dk_ref, dv_ref) = rest[:8], rest[8], rest[9:13], rest[13:]
    for target, side in zip(scratch, sides):
        fill(target, side)
    q_ref, c_ref, k_ref, v_ref = scratch
    k_turned = k_ref[...].astype(jnp.float32).T.astype(jnp.bfloat16)
    h = pl.program_id(0)
    for t in range(0, len(places), 2):
        cols = slice(t * 128, t * 128 + 256)
        owners = [owner_of(index_ref, place) for place in places[t : t + 2]]
        log_total, delta = (
            jnp.concatenate(
                [totals_ref[owner, pl.ds(heads * kind + h, 1), :] for owner in owners], axis=1
            )
            for kind in (0, 1)
        )
        s = lax.dot_general(k_ref[...], q_ref[cols, :], NT, preferred_element_type=jnp.float32)
        g = lax.dot_general(v_ref[...], c_ref[cols, :], NT, preferred_element_type=jnp.float32)
        p = jnp.exp2(s * (SCALING * LOG2E) - log_total)
        ds = (p * (g - delta)).astype(jnp.bfloat16)
        dv = jnp.dot(p.astype(jnp.bfloat16), c_ref[cols, :], preferred_element_type=jnp.float32)
        dk = jnp.dot(ds, q_ref[cols, :], preferred_element_type=jnp.float32)
        if t == 0:
            dv_ref[...] = dv
            dk_ref[...] = dk
        else:
            dv_ref[...] += dv
            dk_ref[...] += dk
        dq = jnp.dot(k_turned, ds, preferred_element_type=jnp.float32)
        dq = (dq * SCALING).T.astype(jnp.bfloat16)
        dq_refs[t][...] = dq[:128]
        dq_refs[t + 1][...] = dq[128:]
    for place in range(8):
        owner = key_owner_of(index_ref, place)
        rows = slice(place * 128, place * 128 + 128)
        dkv_ref[owner, 0] = (dk_ref[rows, :] * SCALING).astype(jnp.bfloat16)
        dkv_ref[owner, 1] = dv_ref[rows, :].astype(jnp.bfloat16)


SMEM_SPEC = pl.BlockSpec(memory_space=pltpu.SMEM)
ROWS_SPEC = pl.BlockSpec((8, 16, 128), lambda h: (0, 0, 0))


def side_specs(pieces, first):
    return [
        pl.BlockSpec((piece.shape[0], HEAD_DIM), lambda h: (0, first + h)) for piece in pieces
    ]


def sides_of(blocks, keys, heads):
    pieces = [piece for block in blocks for piece in block]
    operands = [*pieces, *pieces, *keys, *keys]
    specs = []
    for side in (pieces, keys):
        for first in (0, heads):
            specs += side_specs(side, first)
    return operands, specs, [len(pieces)] * 2 + [len(keys)] * 2


def block_stats(index, places, blocks, keys, heads):
    operands, specs, counts = sides_of(blocks, keys, heads)
    rows = 128 * len(blocks)
    return pl.pallas_call(
        functools.partial(stats_kernel, places, counts, heads),
        grid=(heads,),
        out_shape=jax.ShapeDtypeStruct((8, 16, 128), jnp.float32),
        in_specs=[SMEM_SPEC, *specs],
        out_specs=ROWS_SPEC,
        scratch_shapes=[pltpu.VMEM((rows, HEAD_DIM), jnp.bfloat16)] * 2
        + [pltpu.VMEM((1024, HEAD_DIM), jnp.bfloat16)] * 2,
        compiler_params=pltpu.CompilerParams(vmem_limit_bytes=VMEM_LIMIT),
        cost_estimate=pl.CostEstimate(
            flops=heads * rows * 2**17 * 16, bytes_accessed=2**23, transcendentals=heads * rows * 2**10
        ),
        name="block_stats",
    )(index, *operands)


def block_grads(index, places, blocks, keys, totals, heads):
    operands, specs, counts = sides_of(blocks, keys, heads)
    rows = 128 * len(blocks)
    width = heads * HEAD_DIM
    outs = pl.pallas_call(
        functools.partial(grads_kernel, places, counts, heads),
        grid=(heads,),
        out_shape=[jax.ShapeDtypeStruct((128, width), jnp.bfloat16)] * 8
        + [jax.ShapeDtypeStruct((8, 2, 128, width), jnp.bfloat16)],
        in_specs=[SMEM_SPEC, *specs, ROWS_SPEC],
        out_specs=[pl.BlockSpec((128, HEAD_DIM), lambda h: (0, h))] * 8
        + [pl.BlockSpec((8, 2, 128, HEAD_DIM), lambda h: (0, 0, 0, h))],
        scratch_shapes=[pltpu.VMEM((rows, HEAD_DIM), jnp.bfloat16)] * 2
        + [pltpu.VMEM((1024, HEAD_DIM), jnp.bfloat16)] * 2
        + [pltpu.VMEM((1024, HEAD_DIM), jnp.float32)] * 2,
        compiler_params=pltpu.CompilerParams(vmem_limit_bytes=VMEM_LIMIT),
        cost_estimate=pl.CostEstimate(
            flops=heads * rows * 2**17 * 20, bytes_accessed=2**24, transcendentals=heads * rows * 2**10
        ),
        name="block_grads",
    )(index, *operands, totals)
    return outs[:8], outs[8]


def merge(parts, heads):
    kinds = [
        [part[:, first * heads : (first + 1) * heads] for first in range(3)] for part in parts
    ]
    top = functools.reduce(jnp.maximum, [kind[0] for kind in kinds])
    total = weight = 0.0
    for kind in kinds:
        factor = jnp.exp2(kind[0] - top)
        total = total + kind[1] * factor
        weight = weight + kind[2] * factor
    return top, total, weight


def with_padding(rows):
    used = sum(row.shape[1] for row in rows)
    return jnp.concatenate([*rows, jnp.zeros((8, 16 - used, 128), jnp.float32)], axis=1)


def shards(q_raw, k_raw, values, positions, cotangent, out_weight, modulation, step_index):
    width = q_raw.shape[1]
    heads = width // HEAD_DIM
    inner_width = width * 4
    f32 = jnp.float32
    q_float = q_raw.astype(f32)
    k_float = k_raw.astype(f32)
    squares = jnp.stack(
        [jnp.sum(q_float * q_float, axis=1), jnp.sum(k_float * k_float, axis=1)]
    )
    inverse = lax.rsqrt(sum_heads_axes(squares) / inner_width + EPSILON)
    cosine, signed_sine = rotation(positions, heads)
    q_normed = q_float * inverse[0][:, None]
    k_normed = k_float * inverse[1][:, None]
    q_rot = rotate(q_normed, cosine, signed_sine, 1.0).astype(jnp.bfloat16)
    k_rot = rotate(k_normed, cosine, signed_sine, 1.0).astype(jnp.bfloat16)
    gate_row = lax.dynamic_slice_in_dim(modulation, step_index[0], 1, 0)
    gated_cot = (gate_row * cotangent.astype(f32)).astype(jnp.bfloat16)
    attn_cot = lax.dot_general(
        gated_cot, out_weight, NT, preferred_element_type=f32
    ).astype(jnp.bfloat16)

    index = jnp.stack([lax.axis_index("z"), lax.axis_index("y"), lax.axis_index("xl")])
    queries = ring_gather(jnp.concatenate([q_rot, attn_cot], axis=1))
    keys = plane_gather(jnp.concatenate([k_rot, values], axis=1))

    places = list(range(8))
    stats = block_stats(index, places, queries, keys, heads)
    stats = with_padding(merge([stats, shift(stats, "z", 1)], heads))
    top, total, weight = merge([stats] + [shift(stats, "z", d) for d in (2, -2, 4)], heads)
    totals = with_padding([top + jnp.log2(total), weight / total])

    dq, dkv = block_grads(index, places, queries, keys, totals, heads)
    dq_sum = ring_reduce(dq)
    dkv_sum = jnp.sum(lax.all_to_all(dkv, ("xl", "y"), 0, 0, tiled=True).astype(f32), axis=0)

    dq_normed = rotate(dq_sum, cosine, signed_sine, -1.0)
    dk_normed = rotate(dkv_sum[0], cosine, signed_sine, -1.0)
    slopes = jnp.stack(
        [jnp.sum(dq_normed * q_normed, axis=1), jnp.sum(dk_normed * k_normed, axis=1)]
    )
    slopes = sum_heads_axes(slopes) / inner_width
    query_grad = inverse[0][:, None] * (dq_normed - q_normed * slopes[0][:, None])
    key_grad = inverse[1][:, None] * (dk_normed - k_normed * slopes[1][:, None])
    return (
        query_grad.astype(jnp.bfloat16),
        key_grad.astype(jnp.bfloat16),
        dkv_sum[1].astype(jnp.bfloat16),
    )


def solution(mesh):
    axes = ("xl", "z", "y", "xh", "c")
    fine = Mesh(np.asarray(mesh.devices).reshape(2, 8, 4, 2, 2), axes)
    split = P(TOKENS_AXES, HEADS_AXES)
    rows = P(TOKENS_AXES, None)
    return jax.shard_map(
        shards,
        mesh=fine,
        in_specs=(split, split, split, rows, rows, P(HEADS_AXES, None), P(), P()),
        out_specs=(split, split, split),
        check_vma=False,
    )
```

profile of v0, /device:TPU:1, one launch (start us, length us, event | category | flops | bytes accessed | tf_op | source)
XLA Modules:
  0.0 149.1 jit_solution(2059288683009497769)
XLA Ops:
  2.9 3.7 %collective-permute-start.1 = (f32[2,128]{1,0:T(2,128)S(1)}, f32[2,128]{1,0:T(2,128)S(1)}, u32[]{:S(2)}, u32[]{:S(2)}) collective-permute-start(f32[2,128]{1,0:T(2,128)S(1)} %pad_maximum_fusion.3), channel_id=1, source_target_pairs={{0,2},{1,3},{2,0},{3,1},{4,6},{5,7},{6,4},{7,5},{8,10},{9,11},{10,... | collective-permute-start | bytes 3080 | tf_op jit(solution)/shard_map/ppermute | solution.py:68
  6.6 2.8 %collective-permute-start.2 = (f32[2,128]{1,0:T(2,128)S(1)}, f32[2,128]{1,0:T(2,128)S(1)}, u32[]{:S(2)}, u32[]{:S(2)}) collective-permute-start(f32[2,128]{1,0:T(2,128)S(1)} %pad_maximum_fusion.3), channel_id=1, source_target_pairs={{0,3},{1,2},{2,1},{3,0},{4,7},{5,6},{6,5},{7,4},{8,11},{9,10},{10,... | collective-permute-start | bytes 3080 | tf_op jit(solution)/shard_map/ppermute | solution.py:68
  15.6 1.8 %copy-done.1 = bf16[640,5120]{1,0:T(8,128)(2,1)S(1)} copy-done((bf16[640,5120]{1,0:T(8,128)(2,1)S(1)}, bf16[640,5120]{1,0:T(8,128)(2,1)}, u32[]{:S(2)}) %copy-start.1) | copy-done | bytes 6553624
  17.4 2.1 %fusion.2 = bf16[128,640]{1,0:T(8,128)(2,1)S(1)} fusion(bf16[640,5120]{1,0:T(8,128)(2,1)S(1)} %copy-done.1, bf16[128,5120]{1,0:T(8,128)(2,1)S(1)} %copy-done.4, f32[5120]{0:T(1024)S(1)} %bitcast.38), kind=kOutput, calls=%fused_computation.4 | convolution fusion | flops 840908800 | bytes 8048640 | tf_op jit(solution)/shard_map/dot_general | solution.py:294
  19.6 3.9 %collective-permute-start.7 = (bf16[128,1280]{1,0:T(8,128)(2,1)S(1)}, bf16[128,1280]{1,0:T(8,128)(2,1)S(1)}, u32[]{:S(2)}, u32[]{:S(2)}) collective-permute-start(bf16[128,1280]{1,0:T(8,128)(2,1)S(1)} %pad_maximum_fusion.1.refs_0_.refs_9_), channel_id=1, source_target_pairs={{0,112},{16,0},{32,16},{48,32},{64,48},{80,64},{96,80},{112,96},{1... | collective-permute-start | bytes 983048 | tf_op jit(solution)/shard_map/ppermute | solution.py:58
  24.4 2.0 %collective-permute-start.14 = (bf16[256,1280]{1,0:T(8,128)(2,1)S(1)}, bf16[256,1280]{1,0:T(8,128)(2,1)S(1)}, u32[]{:S(2)}, u32[]{:S(2)}) collective-permute-start(bf16[256,1280]{1,0:T(8,128)(2,1)S(1)} %pad_maximum_fusion.refs_18_.refs_23_), channel_id=1, source_target_pairs={{0,12},{4,0},{8,4},{12,8},{1,13},{5,1},{9,5},{13,9},{2,14},{6,2},{... | collective-permute-start | bytes 1966088 | tf_op jit(solution)/shard_map/ppermute | solution.py:58
  26.4 3.7 %collective-permute-done.7.refs_8_.refs_17_ = bf16[128,1280]{1,0:T(8,128)(2,1)S(1)} collective-permute-done((bf16[128,1280]{1,0:T(8,128)(2,1)S(1)}, bf16[128,1280]{1,0:T(8,128)(2,1)S(1)}, u32[]{:S(2)}, u32[]{:S(2)}) %collective-permute-start.7) | collective-permute-done | bytes 327712 | tf_op jit(solution)/shard_map/ppermute | solution.py:58
  30.1 3.4 %collective-permute-start.8 = (bf16[128,1280]{1,0:T(8,128)(2,1)S(1)}, bf16[128,1280]{1,0:T(8,128)(2,1)S(1)}, u32[]{:S(2)}, u32[]{:S(2)}) collective-permute-start(bf16[128,1280]{1,0:T(8,128)(2,1)S(1)} %collective-permute-done.7.refs_8_.refs_17_), channel_id=1, source_target_pairs={{0,112},{16,0},{32,16},{48,32},{64,48},{80,64},{96,80},{112,96},{1... | collective-permute-start | bytes 983048 | tf_op jit(solution)/shard_map/ppermute | solution.py:58
  33.5 5.6 %collective-permute-done.8.refs_7_.refs_16_ = bf16[128,1280]{1,0:T(8,128)(2,1)S(1)} collective-permute-done((bf16[128,1280]{1,0:T(8,128)(2,1)S(1)}, bf16[128,1280]{1,0:T(8,128)(2,1)S(1)}, u32[]{:S(2)}, u32[]{:S(2)}) %collective-permute-start.8) | collective-permute-done | bytes 327712 | tf_op jit(solution)/shard_map/ppermute | solution.py:58
  39.1 3.4 %collective-permute-start.9 = (bf16[128,1280]{1,0:T(8,128)(2,1)S(1)}, bf16[128,1280]{1,0:T(8,128)(2,1)S(1)}, u32[]{:S(2)}, u32[]{:S(2)}) collective-permute-start(bf16[128,1280]{1,0:T(8,128)(2,1)S(1)} %collective-permute-done.8.refs_7_.refs_16_), channel_id=1, source_target_pairs={{0,112},{16,0},{32,16},{48,32},{64,48},{80,64},{96,80},{112,96},{1... | collective-permute-start | bytes 983048 | tf_op jit(solution)/shard_map/ppermute | solution.py:58
  42.6 3.0 %collective-permute-start.15 = (bf16[128,1280]{1,0:T(8,128)(2,1)S(1)}, bf16[128,1280]{1,0:T(8,128)(2,1)}, u32[]{:S(2)}, u32[]{:S(2)}) collective-permute-start(bf16[128,1280]{1,0:T(8,128)(2,1)S(1)} %slice.190), channel_id=1, source_target_pairs={{0,12},{4,0},{8,4},{12,8},{1,13},{5,1},{9,5},{13,9},{2,14},{6,2},{... | collective-permute-start | bytes 983048 | tf_op jit(solution)/shard_map/ppermute | solution.py:58
  47.3 3.5 %collective-permute-start.10 = (bf16[64,1280]{1,0:T(8,128)(2,1)S(1)}, bf16[64,1280]{1,0:T(8,128)(2,1)}, u32[]{:S(2)}, u32[]{:S(2)}) collective-permute-start(bf16[64,1280]{1,0:T(8,128)(2,1)S(1)} %slice.184), channel_id=1, source_target_pairs={{0,112},{16,0},{32,16},{48,32},{64,48},{80,64},{96,80},{112,96},{1... | collective-permute-start | bytes 491528 | tf_op jit(solution)/shard_map/ppermute | solution.py:58
  53.0 3.6 %collective-permute-done.6.refs_4_.refs_13_ = bf16[64,1280]{1,0:T(8,128)(2,1)} collective-permute-done((bf16[64,1280]{1,0:T(8,128)(2,1)S(1)}, bf16[64,1280]{1,0:T(8,128)(2,1)}, u32[]{:S(2)}, u32[]{:S(2)}) %collective-permute-start.6) | collective-permute-done | bytes 163872 | tf_op jit(solution)/shard_map/ppermute | solution.py:58
  56.6 12.1 %block_stats.1 = f32[8,16,128]{2,1,0:T(8,128)} custom-call(s32[3]{0:T(128)} %pad_add_fusion.2.index_ref, bf16[128,1280]{1,0:T(8,128)(2,1)} %copy-done.7, bf16[128,1280]{1,0:T(8,128)(2,1)} %copy-done.21, bf16[128,1280]{1,0:T(8,128)(2,1)} %copy-done.23, bf16[128,1280]{1,0:T(8,128)(2,1)} %copy-done.19, ...), custom_call_target="tpu_custom_call" | custom-call | flops 10737418240 | bytes 8388608 | tf_op jit(solution)/shard_map/block_stats/pallas_call | solution.py:218
  68.9 4.4 %collective-permute-done.16 = f32[8,16,128]{2,1,0:T(8,128)S(1)} collective-permute-done((f32[8,16,128]{2,1,0:T(8,128)}, f32[8,16,128]{2,1,0:T(8,128)S(1)}, u32[]{:S(2)}, u32[]{:S(2)}) %collective-permute-start.16) | collective-permute-done | bytes 65568 | tf_op jit(solution)/shard_map/ppermute | solution.py:58
  75.1 2.0 %collective-permute-start.19 = (f32[8,16,128]{2,1,0:T(8,128)S(1)}, f32[8,16,128]{2,1,0:T(8,128)S(1)}, u32[]{:S(2)}, u32[]{:S(2)}) collective-permute-start(f32[8,16,128]{2,1,0:T(8,128)S(1)} %maximum_maximum_fusion), channel_id=1, source_target_pairs={{0,64},{16,80},{32,96},{48,112},{64,0},{80,16},{96,32},{112,48},{1... | collective-permute-start | bytes 196616 | tf_op jit(solution)/shard_map/ppermute | solution.py:58
  77.2 2.4 %collective-permute-start.17 = (f32[8,16,128]{2,1,0:T(8,128)S(1)}, f32[8,16,128]{2,1,0:T(8,128)S(1)}, u32[]{:S(2)}, u32[]{:S(2)}) collective-permute-start(f32[8,16,128]{2,1,0:T(8,128)S(1)} %maximum_maximum_fusion), channel_id=1, source_target_pairs={{0,32},{16,48},{32,64},{48,80},{64,96},{80,112},{96,0},{112,16},{1... | collective-permute-start | bytes 196616 | tf_op jit(solution)/shard_map/ppermute | solution.py:58
  79.6 2.7 %collective-permute-done.19 = f32[8,16,128]{2,1,0:T(8,128)S(1)} collective-permute-done((f32[8,16,128]{2,1,0:T(8,128)S(1)}, f32[8,16,128]{2,1,0:T(8,128)S(1)}, u32[]{:S(2)}, u32[]{:S(2)}) %collective-permute-start.19) | collective-permute-done | bytes 65568 | tf_op jit(solution)/shard_map/ppermute | solution.py:58
  82.4 1.9 %collective-permute-done.17 = f32[8,16,128]{2,1,0:T(8,128)S(1)} collective-permute-done((f32[8,16,128]{2,1,0:T(8,128)S(1)}, f32[8,16,128]{2,1,0:T(8,128)S(1)}, u32[]{:S(2)}, u32[]{:S(2)}) %collective-permute-start.17) | collective-permute-done | bytes 65568 | tf_op jit(solution)/shard_map/ppermute | solution.py:58
  85.0 16.4 %block_grads.1 = (bf16[128,640]{1,0:T(8,128)(2,1)}, bf16[128,640]{1,0:T(8,128)(2,1)}, bf16[128,640]{1,0:T(8,128)(2,1)}, bf16[128,640]{1,0:T(8,128)(2,1)}, bf16[1...) custom-call(s32[3]{0:T(128)} %pad_add_fusion.2.index_ref, ...), custom_call_target="tpu_custom_call" | custom-call | flops 13421772800 | bytes 16777216 | tf_op jit(solution)/shard_map/block_grads/pallas_call | solution.py:238
  101.5 4.9 %all-to-all-start = ((bf16[8,2,128,640]{3,2,1,0:T(8,128)(2,1)}), bf16[8,2,128,640]{3,2,1,0:T(8,128)(2,1)}, u32[]{:S(2)}, u32[]{:S(2)}) async-start(bf16[8,2,128,640]{3,2,1,0:T(8,128)(2,1)} %get-tuple-element.20), calls=%async_computation | async-start | bytes 5242880 | tf_op jit(solution)/shard_map/all_to_all | solution.py:310
  106.6 2.7 %collective-permute-start.20 = (bf16[64,640]{1,0:T(8,128)(2,1)S(1)}, bf16[64,640]{1,0:T(8,128)(2,1)S(1)}, u32[]{:S(2)}, u32[]{:S(2)}) collective-permute-start(bf16[64,640]{1,0:T(8,128)(2,1)S(1)} %get-tuple-element.49), channel_id=1, source_target_pairs={{0,112},{16,0},{32,16},{48,32},{64,48},{80,64},{96,80},{112,96},{1... | collective-permute-start | bytes 245768 | tf_op jit(solution)/shard_map/ppermute | solution.py:58
  111.5 2.7 %collective-permute-start.21 = (bf16[128,640]{1,0:T(8,128)(2,1)S(1)}, bf16[128,640]{1,0:T(8,128)(2,1)S(1)}, u32[]{:S(2)}, u32[]{:S(2)}) collective-permute-start(bf16[128,640]{1,0:T(8,128)(2,1)S(1)} %pad_add_fusion.1), channel_id=1, source_target_pairs={{0,112},{16,0},{32,16},{48,32},{64,48},{80,64},{96,80},{112,96},{1... | collective-permute-start | bytes 491528 | tf_op jit(solution)/shard_map/ppermute | solution.py:58
  114.2 2.6 %collective-permute-done.25 = bf16[128,640]{1,0:T(8,128)(2,1)S(1)} collective-permute-done((bf16[128,640]{1,0:T(8,128)(2,1)S(1)}, bf16[128,640]{1,0:T(8,128)(2,1)S(1)}, u32[]{:S(2)}, u32[]{:S(2)}) %collective-permute-start.25) | collective-permute-done | bytes 163872 | tf_op jit(solution)/shard_map/ppermute | solution.py:58
  117.0 3.1 %collective-permute-start.22 = (bf16[128,640]{1,0:T(8,128)(2,1)S(1)}, bf16[128,640]{1,0:T(8,128)(2,1)S(1)}, u32[]{:S(2)}, u32[]{:S(2)}) collective-permute-start(bf16[128,640]{1,0:T(8,128)(2,1)S(1)} %add.131), channel_id=1, source_target_pairs={{0,112},{16,0},{32,16},{48,32},{64,48},{80,64},{96,80},{112,96},{1... | collective-permute-start | bytes 491528 | tf_op jit(solution)/shard_map/ppermute | solution.py:58
  120.1 2.6 %collective-permute-done.26 = bf16[128,640]{1,0:T(8,128)(2,1)S(1)} collective-permute-done((bf16[128,640]{1,0:T(8,128)(2,1)S(1)}, bf16[128,640]{1,0:T(8,128)(2,1)S(1)}, u32[]{:S(2)}, u32[]{:S(2)}) %collective-permute-start.26) | collective-permute-done | bytes 163872 | tf_op jit(solution)/shard_map/ppermute | solution.py:58
  122.9 3.1 %collective-permute-start.23 = (bf16[128,640]{1,0:T(8,128)(2,1)S(1)}, bf16[128,640]{1,0:T(8,128)(2,1)S(1)}, u32[]{:S(2)}, u32[]{:S(2)}) collective-permute-start(bf16[128,640]{1,0:T(8,128)(2,1)S(1)} %add.132), channel_id=1, source_target_pairs={{0,112},{16,0},{32,16},{48,32},{64,48},{80,64},{96,80},{112,96},{1... | collective-permute-start | bytes 491528 | tf_op jit(solution)/shard_map/ppermute | solution.py:58
  126.0 2.6 %collective-permute-done.27 = bf16[128,640]{1,0:T(8,128)(2,1)S(1)} collective-permute-done((bf16[128,640]{1,0:T(8,128)(2,1)S(1)}, bf16[128,640]{1,0:T(8,128)(2,1)S(1)}, u32[]{:S(2)}, u32[]{:S(2)}) %collective-permute-start.27) | collective-permute-done | bytes 163872 | tf_op jit(solution)/shard_map/ppermute | solution.py:58
  128.9 8.4 %all-to-all-done = bf16[8,2,128,640]{3,2,1,0:T(8,128)(2,1)} async-done(((bf16[8,2,128,640]{3,2,1,0:T(8,128)(2,1)}), bf16[8,2,128,640]{3,2,1,0:T(8,128)(2,1)}, u32[]{:S(2)}, u32[]{:S(2)}) %all-to-all-start) | async-done | bytes 2621472 | tf_op jit(solution)/shard_map/all_to_all | solution.py:310
  137.3 2.2 %convert_reduce_fusion = f32[2,128,640]{2,1,0:T(8,128)S(1)} fusion(bf16[8,2,128,640]{3,2,1,0:T(8,128)(2,1)} %all-to-all-done), kind=kLoop, calls=%fused_computation | loop fusion | flops 2457600 | bytes 3276800 | tf_op jit(solution)/shard_map/reduce_sum | solution.py:310
  140.4 2.6 %collective-permute-start.29 = (f32[2,128]{1,0:T(2,128)S(1)}, f32[2,128]{1,0:T(2,128)S(1)}, u32[]{:S(2)}, u32[]{:S(2)}) collective-permute-start(f32[2,128]{1,0:T(2,128)S(1)} %pad_maximum_fusion.4), channel_id=1, source_target_pairs={{0,2},{1,3},{2,0},{3,1},{4,6},{5,7},{6,4},{7,5},{8,10},{9,11},{10,... | collective-permute-start | bytes 3080 | tf_op jit(solution)/shard_map/ppermute | solution.py:68
  142.9 2.7 %collective-permute-start.30 = (f32[2,128]{1,0:T(2,128)S(1)}, f32[2,128]{1,0:T(2,128)S(1)}, u32[]{:S(2)}, u32[]{:S(2)}) collective-permute-start(f32[2,128]{1,0:T(2,128)S(1)} %pad_maximum_fusion.4), channel_id=1, source_target_pairs={{0,3},{1,2},{2,1},{3,0},{4,7},{5,6},{6,5},{7,4},{8,11},{9,10},{10,... | collective-permute-start | bytes 3080 | tf_op jit(solution)/shard_map/ppermute | solution.py:68
  (140 shorter events, 22.4 us)
Async XLA Ops:
  2.9 11.4 %collective-permute-start.1 = (f32[2,128]{1,0:T(2,128)S(1)}, f32[2,128]{1,0:T(2,128)S(1)}, u32[]{:S(2)}, u32[]{:S(2)}) collective-permute-start(f32[2,128]{1,0:T(2,128)S(1)} %pad_maximum_fusion.3), channel_id=1, source_target_pairs={{0,2},{1,3},{2,0},{3,1},{4,6},{5,7},{6,4},{7,5},{8,10},{9,11},{10,... | collective-permute-start | bytes 3080 | tf_op jit(solution)/shard_map/ppermute | solution.py:68
  6.6 7.8 %collective-permute-start.2 = (f32[2,128]{1,0:T(2,128)S(1)}, f32[2,128]{1,0:T(2,128)S(1)}, u32[]{:S(2)}, u32[]{:S(2)}) collective-permute-start(f32[2,128]{1,0:T(2,128)S(1)} %pad_maximum_fusion.3), channel_id=1, source_target_pairs={{0,3},{1,2},{2,1},{3,0},{4,7},{5,6},{6,5},{7,4},{8,11},{9,10},{10,... | collective-permute-start | bytes 3080 | tf_op jit(solution)/shard_map/ppermute | solution.py:68
  9.4 5.0 %collective-permute-start = (f32[2,128]{1,0:T(2,128)S(1)}, f32[2,128]{1,0:T(2,128)S(1)}, u32[]{:S(2)}, u32[]{:S(2)}) collective-permute-start(f32[2,128]{1,0:T(2,128)S(1)} %pad_maximum_fusion.3), channel_id=1, source_target_pairs={{0,1},{1,0},{2,3},{3,2},{4,5},{5,4},{6,7},{7,6},{8,9},{9,8},{10,11... | collective-permute-start | bytes 3080 | tf_op jit(solution)/shard_map/ppermute | solution.py:68
  15.4 8.9 %collective-permute-start.11 = (bf16[128,1280]{1,0:T(8,128)(2,1)S(1)}, bf16[128,1280]{1,0:T(8,128)(2,1)S(1)}, u32[]{:S(2)}, u32[]{:S(2)}) collective-permute-start(bf16[128,1280]{1,0:T(8,128)(2,1)S(1)} %pad_maximum_fusion.2), channel_id=1, source_target_pairs={{0,128},{128,0},{1,129},{129,1},{2,130},{130,2},{3,131},{131,3},{4... | collective-permute-start | bytes 983048 | tf_op jit(solution)/shard_map/ppermute | solution.py:62
  19.6 10.5 %collective-permute-start.7 = (bf16[128,1280]{1,0:T(8,128)(2,1)S(1)}, bf16[128,1280]{1,0:T(8,128)(2,1)S(1)}, u32[]{:S(2)}, u32[]{:S(2)}) collective-permute-start(bf16[128,1280]{1,0:T(8,128)(2,1)S(1)} %pad_maximum_fusion.1.refs_0_.refs_9_), channel_id=1, source_target_pairs={{0,112},{16,0},{32,16},{48,32},{64,48},{80,64},{96,80},{112,96},{1... | collective-permute-start | bytes 983048 | tf_op jit(solution)/shard_map/ppermute | solution.py:58
  23.5 10.0 %collective-permute-start.3 = (bf16[128,1280]{1,0:T(8,128)(2,1)S(1)}, bf16[128,1280]{1,0:T(8,128)(2,1)S(1)}, u32[]{:S(2)}, u32[]{:S(2)}) collective-permute-start(bf16[128,1280]{1,0:T(8,128)(2,1)S(1)} %pad_maximum_fusion.1.refs_0_.refs_9_), channel_id=1, source_target_pairs={{0,16},{16,32},{32,48},{48,64},{64,80},{80,96},{96,112},{112,0},{1... | collective-permute-start | bytes 983048 | tf_op jit(solution)/shard_map/ppermute | solution.py:58
  24.4 18.2 %collective-permute-start.14 = (bf16[256,1280]{1,0:T(8,128)(2,1)S(1)}, bf16[256,1280]{1,0:T(8,128)(2,1)S(1)}, u32[]{:S(2)}, u32[]{:S(2)}) collective-permute-start(bf16[256,1280]{1,0:T(8,128)(2,1)S(1)} %pad_maximum_fusion.refs_18_.refs_23_), channel_id=1, source_target_pairs={{0,12},{4,0},{8,4},{12,8},{1,13},{5,1},{9,5},{13,9},{2,14},{6,2},{... | collective-permute-start | bytes 1966088 | tf_op jit(solution)/shard_map/ppermute | solution.py:58
  26.4 19.2 %collective-permute-start.12 = (bf16[256,1280]{1,0:T(8,128)(2,1)S(1)}, bf16[256,1280]{1,0:T(8,128)(2,1)S(1)}, u32[]{:S(2)}, u32[]{:S(2)}) collective-permute-start(bf16[256,1280]{1,0:T(8,128)(2,1)S(1)} %pad_maximum_fusion.refs_18_.refs_23_), channel_id=1, source_target_pairs={{0,4},{4,8},{8,12},{12,0},{1,5},{5,9},{9,13},{13,1},{2,6},{6,10},{... | collective-permute-start | bytes 1966088 | tf_op jit(solution)/shard_map/ppermute | solution.py:58
  30.1 9.0 %collective-permute-start.8 = (bf16[128,1280]{1,0:T(8,128)(2,1)S(1)}, bf16[128,1280]{1,0:T(8,128)(2,1)S(1)}, u32[]{:S(2)}, u32[]{:S(2)}) collective-permute-start(bf16[128,1280]{1,0:T(8,128)(2,1)S(1)} %collective-permute-done.7.refs_8_.refs_17_), channel_id=1, source_target_pairs={{0,112},{16,0},{32,16},{48,32},{64,48},{80,64},{96,80},{112,96},{1... | collective-permute-start | bytes 983048 | tf_op jit(solution)/shard_map/ppermute | solution.py:58
  33.5 9.0 %collective-permute-start.4 = (bf16[128,1280]{1,0:T(8,128)(2,1)S(1)}, bf16[128,1280]{1,0:T(8,128)(2,1)S(1)}, u32[]{:S(2)}, u32[]{:S(2)}) collective-permute-start(bf16[128,1280]{1,0:T(8,128)(2,1)S(1)} %collective-permute-done.3.refs_1_.refs_10_), channel_id=1, source_target_pairs={{0,16},{16,32},{32,48},{48,64},{64,80},{80,96},{96,112},{112,0},{1... | collective-permute-start | bytes 983048 | tf_op jit(solution)/shard_map/ppermute | solution.py:58
  39.1 8.1 %collective-permute-start.9 = (bf16[128,1280]{1,0:T(8,128)(2,1)S(1)}, bf16[128,1280]{1,0:T(8,128)(2,1)S(1)}, u32[]{:S(2)}, u32[]{:S(2)}) collective-permute-start(bf16[128,1280]{1,0:T(8,128)(2,1)S(1)} %collective-permute-done.8.refs_7_.refs_16_), channel_id=1, source_target_pairs={{0,112},{16,0},{32,16},{48,32},{64,48},{80,64},{96,80},{112,96},{1... | collective-permute-start | bytes 983048 | tf_op jit(solution)/shard_map/ppermute | solution.py:58
  42.5 8.2 %collective-permute-start.5 = (bf16[128,1280]{1,0:T(8,128)(2,1)S(1)}, bf16[128,1280]{1,0:T(8,128)(2,1)S(1)}, u32[]{:S(2)}, u32[]{:S(2)}) collective-permute-start(bf16[128,1280]{1,0:T(8,128)(2,1)S(1)} %collective-permute-done.4.refs_2_.refs_11_), channel_id=1, source_target_pairs={{0,16},{16,32},{32,48},{48,64},{64,80},{80,96},{96,112},{112,0},{1... | collective-permute-start | bytes 983048 | tf_op jit(solution)/shard_map/ppermute | solution.py:58
  42.6 14.0 %collective-permute-start.15 = (bf16[128,1280]{1,0:T(8,128)(2,1)S(1)}, bf16[128,1280]{1,0:T(8,128)(2,1)}, u32[]{:S(2)}, u32[]{:S(2)}) collective-permute-start(bf16[128,1280]{1,0:T(8,128)(2,1)S(1)} %slice.190), channel_id=1, source_target_pairs={{0,12},{4,0},{8,4},{12,8},{1,13},{5,1},{9,5},{13,9},{2,14},{6,2},{... | collective-permute-start | bytes 983048 | tf_op jit(solution)/shard_map/ppermute | solution.py:58
  46.4 10.2 %collective-permute-start.13 = (bf16[128,1280]{1,0:T(8,128)(2,1)}, bf16[128,1280]{1,0:T(8,128)(2,1)}, u32[]{:S(2)}, u32[]{:S(2)}) collective-permute-start(bf16[128,1280]{1,0:T(8,128)(2,1)} %slice.189), channel_id=1, source_target_pairs={{0,4},{4,8},{8,12},{12,0},{1,5},{5,9},{9,13},{13,1},{2,6},{6,10},{... | collective-permute-start | bytes 983048 | tf_op jit(solution)/shard_map/ppermute | solution.py:58
  47.3 5.8 %collective-permute-start.10 = (bf16[64,1280]{1,0:T(8,128)(2,1)S(1)}, bf16[64,1280]{1,0:T(8,128)(2,1)}, u32[]{:S(2)}, u32[]{:S(2)}) collective-permute-start(bf16[64,1280]{1,0:T(8,128)(2,1)S(1)} %slice.184), channel_id=1, source_target_pairs={{0,112},{16,0},{32,16},{48,32},{64,48},{80,64},{96,80},{112,96},{1... | collective-permute-start | bytes 491528 | tf_op jit(solution)/shard_map/ppermute | solution.py:58
  50.8 5.9 %collective-permute-start.6 = (bf16[64,1280]{1,0:T(8,128)(2,1)S(1)}, bf16[64,1280]{1,0:T(8,128)(2,1)}, u32[]{:S(2)}, u32[]{:S(2)}) collective-permute-start(bf16[64,1280]{1,0:T(8,128)(2,1)S(1)} %slice.183), channel_id=1, source_target_pairs={{0,16},{16,32},{32,48},{48,64},{64,80},{80,96},{96,112},{112,0},{1... | collective-permute-start | bytes 491528 | tf_op jit(solution)/shard_map/ppermute | solution.py:58
  68.8 4.6 %collective-permute-start.16 = (f32[8,16,128]{2,1,0:T(8,128)}, f32[8,16,128]{2,1,0:T(8,128)S(1)}, u32[]{:S(2)}, u32[]{:S(2)}) collective-permute-start(f32[8,16,128]{2,1,0:T(8,128)} %block_stats.1), channel_id=1, source_target_pairs={{0,16},{16,32},{32,48},{48,64},{64,80},{80,96},{96,112},{112,0},{1... | collective-permute-start | bytes 196616 | tf_op jit(solution)/shard_map/ppermute | solution.py:58
  75.1 7.2 %collective-permute-start.19 = (f32[8,16,128]{2,1,0:T(8,128)S(1)}, f32[8,16,128]{2,1,0:T(8,128)S(1)}, u32[]{:S(2)}, u32[]{:S(2)}) collective-permute-start(f32[8,16,128]{2,1,0:T(8,128)S(1)} %maximum_maximum_fusion), channel_id=1, source_target_pairs={{0,64},{16,80},{32,96},{48,112},{64,0},{80,16},{96,32},{112,48},{1... | collective-permute-start | bytes 196616 | tf_op jit(solution)/shard_map/ppermute | solution.py:58
  77.2 5.2 %collective-permute-start.18 = (f32[8,16,128]{2,1,0:T(8,128)S(1)}, f32[8,16,128]{2,1,0:T(8,128)S(1)}, u32[]{:S(2)}, u32[]{:S(2)}) collective-permute-start(f32[8,16,128]{2,1,0:T(8,128)S(1)} %maximum_maximum_fusion), channel_id=1, source_target_pairs={{0,96},{16,112},{32,0},{48,16},{64,32},{80,48},{96,64},{112,80},{1... | collective-permute-start | bytes 196616 | tf_op jit(solution)/shard_map/ppermute | solution.py:58
  77.2 7.1 %collective-permute-start.17 = (f32[8,16,128]{2,1,0:T(8,128)S(1)}, f32[8,16,128]{2,1,0:T(8,128)S(1)}, u32[]{:S(2)}, u32[]{:S(2)}) collective-permute-start(f32[8,16,128]{2,1,0:T(8,128)S(1)} %maximum_maximum_fusion), channel_id=1, source_target_pairs={{0,32},{16,48},{32,64},{48,80},{64,96},{80,112},{96,0},{112,16},{1... | collective-permute-start | bytes 196616 | tf_op jit(solution)/shard_map/ppermute | solution.py:58
  101.5 35.8 %all-to-all-start = ((bf16[8,2,128,640]{3,2,1,0:T(8,128)(2,1)}), bf16[8,2,128,640]{3,2,1,0:T(8,128)(2,1)}, u32[]{:S(2)}, u32[]{:S(2)}) async-start(bf16[8,2,128,640]{3,2,1,0:T(8,128)(2,1)} %get-tuple-element.20), calls=%async_computation | async-start | bytes 5242880 | tf_op jit(solution)/shard_map/all_to_all | solution.py:310
  106.5 4.6 %collective-permute-start.24 = (bf16[64,640]{1,0:T(8,128)(2,1)S(1)}, bf16[64,640]{1,0:T(8,128)(2,1)S(1)}, u32[]{:S(2)}, u32[]{:S(2)}) collective-permute-start(bf16[64,640]{1,0:T(8,128)(2,1)S(1)} %get-tuple-element.50), channel_id=1, source_target_pairs={{0,16},{16,32},{32,48},{48,64},{64,80},{80,96},{96,112},{112,0},{1... | collective-permute-start | bytes 245768 | tf_op jit(solution)/shard_map/ppermute | solution.py:58
  106.6 4.8 %collective-permute-start.20 = (bf16[64,640]{1,0:T(8,128)(2,1)S(1)}, bf16[64,640]{1,0:T(8,128)(2,1)S(1)}, u32[]{:S(2)}, u32[]{:S(2)}) collective-permute-start(bf16[64,640]{1,0:T(8,128)(2,1)S(1)} %get-tuple-element.49), channel_id=1, source_target_pairs={{0,112},{16,0},{32,16},{48,32},{64,48},{80,64},{96,80},{112,96},{1... | collective-permute-start | bytes 245768 | tf_op jit(solution)/shard_map/ppermute | solution.py:58
  111.1 5.7 %collective-permute-start.25 = (bf16[128,640]{1,0:T(8,128)(2,1)S(1)}, bf16[128,640]{1,0:T(8,128)(2,1)S(1)}, u32[]{:S(2)}, u32[]{:S(2)}) collective-permute-start(bf16[128,640]{1,0:T(8,128)(2,1)S(1)} %pad_add_fusion), channel_id=1, source_target_pairs={{0,16},{16,32},{32,48},{48,64},{64,80},{80,96},{96,112},{112,0},{1... | collective-permute-start | bytes 491528 | tf_op jit(solution)/shard_map/ppermute | solution.py:58
  111.5 5.5 %collective-permute-start.21 = (bf16[128,640]{1,0:T(8,128)(2,1)S(1)}, bf16[128,640]{1,0:T(8,128)(2,1)S(1)}, u32[]{:S(2)}, u32[]{:S(2)}) collective-permute-start(bf16[128,640]{1,0:T(8,128)(2,1)S(1)} %pad_add_fusion.1), channel_id=1, source_target_pairs={{0,112},{16,0},{32,16},{48,32},{64,48},{80,64},{96,80},{112,96},{1... | collective-permute-start | bytes 491528 | tf_op jit(solution)/shard_map/ppermute | solution.py:58
  116.9 5.9 %collective-permute-start.26 = (bf16[128,640]{1,0:T(8,128)(2,1)S(1)}, bf16[128,640]{1,0:T(8,128)(2,1)S(1)}, u32[]{:S(2)}, u32[]{:S(2)}) collective-permute-start(bf16[128,640]{1,0:T(8,128)(2,1)S(1)} %add.135), channel_id=1, source_target_pairs={{0,16},{16,32},{32,48},{48,64},{64,80},{80,96},{96,112},{112,0},{1... | collective-permute-start | bytes 491528 | tf_op jit(solution)/shard_map/ppermute | solution.py:58
  117.0 5.8 %collective-permute-start.22 = (bf16[128,640]{1,0:T(8,128)(2,1)S(1)}, bf16[128,640]{1,0:T(8,128)(2,1)S(1)}, u32[]{:S(2)}, u32[]{:S(2)}) collective-permute-start(bf16[128,640]{1,0:T(8,128)(2,1)S(1)} %add.131), channel_id=1, source_target_pairs={{0,112},{16,0},{32,16},{48,32},{64,48},{80,64},{96,80},{112,96},{1... | collective-permute-start | bytes 491528 | tf_op jit(solution)/shard_map/ppermute | solution.py:58
  122.8 5.9 %collective-permute-start.27 = (bf16[128,640]{1,0:T(8,128)(2,1)S(1)}, bf16[128,640]{1,0:T(8,128)(2,1)S(1)}, u32[]{:S(2)}, u32[]{:S(2)}) collective-permute-start(bf16[128,640]{1,0:T(8,128)(2,1)S(1)} %add.136), channel_id=1, source_target_pairs={{0,16},{16,32},{32,48},{48,64},{64,80},{80,96},{96,112},{112,0},{1... | collective-permute-start | bytes 491528 | tf_op jit(solution)/shard_map/ppermute | solution.py:58
  122.9 5.7 %collective-permute-start.23 = (bf16[128,640]{1,0:T(8,128)(2,1)S(1)}, bf16[128,640]{1,0:T(8,128)(2,1)S(1)}, u32[]{:S(2)}, u32[]{:S(2)}) collective-permute-start(bf16[128,640]{1,0:T(8,128)(2,1)S(1)} %add.132), channel_id=1, source_target_pairs={{0,112},{16,0},{32,16},{48,32},{64,48},{80,64},{96,80},{112,96},{1... | collective-permute-start | bytes 491528 | tf_op jit(solution)/shard_map/ppermute | solution.py:58
  140.4 5.9 %collective-permute-start.29 = (f32[2,128]{1,0:T(2,128)S(1)}, f32[2,128]{1,0:T(2,128)S(1)}, u32[]{:S(2)}, u32[]{:S(2)}) collective-permute-start(f32[2,128]{1,0:T(2,128)S(1)} %pad_maximum_fusion.4), channel_id=1, source_target_pairs={{0,2},{1,3},{2,0},{3,1},{4,6},{5,7},{6,4},{7,5},{8,10},{9,11},{10,... | collective-permute-start | bytes 3080 | tf_op jit(solution)/shard_map/ppermute | solution.py:68
  142.9 4.5 %collective-permute-start.30 = (f32[2,128]{1,0:T(2,128)S(1)}, f32[2,128]{1,0:T(2,128)S(1)}, u32[]{:S(2)}, u32[]{:S(2)}) collective-permute-start(f32[2,128]{1,0:T(2,128)S(1)} %pad_maximum_fusion.4), channel_id=1, source_target_pairs={{0,3},{1,2},{2,1},{3,0},{4,7},{5,6},{6,5},{7,4},{8,11},{9,10},{10,... | collective-permute-start | bytes 3080 | tf_op jit(solution)/shard_map/ppermute | solution.py:68
  145.6 1.8 %collective-permute-start.28 = (f32[2,128]{1,0:T(2,128)S(1)}, f32[2,128]{1,0:T(2,128)S(1)}, u32[]{:S(2)}, u32[]{:S(2)}) collective-permute-start(f32[2,128]{1,0:T(2,128)S(1)} %pad_maximum_fusion.4), channel_id=1, source_target_pairs={{0,1},{1,0},{2,3},{3,2},{4,5},{5,4},{6,7},{7,6},{8,9},{9,8},{10,11... | collective-permute-start | bytes 3080 | tf_op jit(solution)/shard_map/ppermute | solution.py:68
  (24 other events, 256.8 us)
where the time goes:
time: 151 us; the launch traced here: 149 us
  starting transfers between devices  52.7 us (35%)
  waiting for transfers between devices  43.7 us (29%)
  Pallas kernels  28.6 us (19%)
  other arithmetic  10.6 us (7%)
  local copies, waits for them, and re-layouts  8.19 us (5%)
  matrix products  3.36 us (2%)
  between operations  1.87 us (1%)
    ppermute x24, starting transfers between devices, shift(): lax.ppermute(x, axis, [(i, (i + distance) % size) for i in range(size)])  36 us
    ppermute x24, waiting for transfers between devices, shift(): lax.ppermute(x, axis, [(i, (i + distance) % size) for i in range(size)])  33.4 us
    pallas_call x1, Pallas kernels, block_grads(): pl.pallas_call(functools.partial(grads_kernel, places, counts, heads), gr...  16.4 us
    pallas_call x1, Pallas kernels, block_stats(): pl.pallas_call(functools.partial(stats_kernel, places, counts, heads), gr...  12.1 us
    ppermute x6, starting transfers between devices, sum_heads_axes(): lax.ppermute(x, HEADS_AXES, [(i, i ^ mask) for i in range(4)])  11.7 us
    all_to_all x1, waiting for transfers between devices, shards(): lax.all_to_all(dkv, ('xl', 'y'), 0, 0, tiled=True).astype(f32)  8.39 us
    all_to_all x1, starting transfers between devices, shards(): lax.all_to_all(dkv, ('xl', 'y'), 0, 0, tiled=True).astype(f32)  4.94 us
  transfers between devices with their start and end apart: 32, of which 15 were waited for; matrix products, arithmetic and copies ran while one was open for 6% of the time, Pallas kernels for 0%

commit v1 on v0

--- a/solution.py
+++ b/solution.py
@@ -34,15 +34,25 @@
 
 
 def rotation(positions, heads_count):
-    angles = jnp.dot(
-        positions.astype(jnp.float32),
-        jnp.asarray(np.repeat(angle_table(HEAD_DIM), 2, axis=1)),
-        precision=lax.Precision.HIGHEST,
-    )
-    parity = jnp.tile(jnp.array([-1.0, 1.0], jnp.float32), HEAD_DIM // 2)
-    cosine = jnp.cos(angles)
-    signed_sine = jnp.sin(angles) * parity[None, :]
-    return jnp.tile(cosine, (1, heads_count)), jnp.tile(signed_sine, (1, heads_count))
+    table = np.repeat(angle_table(HEAD_DIM), 2, axis=1)
+    place = positions.astype(jnp.float32)
+    angles = sum(place[:, axis : axis + 1] * jnp.asarray(table[axis])[None, :] for axis in range(3))
+    parity = jnp.asarray(np.tile(np.array([-1.0, 1.0], np.float32), HEAD_DIM // 2))
+    cosine, signed_sine = lax.optimization_barrier(
+        (jnp.cos(angles), jnp.sin(angles) * parity[None, :])
+    )
+    return (
+        jnp.concatenate([cosine] * heads_count, axis=1),
+        jnp.concatenate([signed_sine] * heads_count, axis=1),
+    )
+
+
+def partner_of(source):
+    columns = np.arange(source.shape[1])
+    exchange = (columns[:, None] == (columns ^ 1)[None, :]).astype(np.float32)
+    return jnp.dot(
+        source, jnp.asarray(exchange, dtype=jnp.bfloat16), preferred_element_type=jnp.float32
+    )
 
 
 def rotate(source, cosine, signed_sine, direction):
@@ -136,16 +146,15 @@
         fill(target, side)
     q_ref, c_ref, k_ref, v_ref = scratch
     h = pl.program_id(0)
-    for t in range(0, len(places), 2):
-        cols = slice(t * 128, t * 128 + 256)
+    for t in range(0, len(places), 4):
+        cols = slice(t * 128, t * 128 + 512)
         s = lax.dot_general(k_ref[...], q_ref[cols, :], NT, preferred_element_type=jnp.float32)
         g = lax.dot_general(v_ref[...], c_ref[cols, :], NT, preferred_element_type=jnp.float32)
-        s = s * (SCALING * LOG2E)
         top = jnp.max(s, axis=0, keepdims=True)
         e = jnp.exp2(s - top)
         total = jnp.sum(e, axis=0, keepdims=True)
         weight = jnp.sum(e * g, axis=0, keepdims=True)
-        for side in (0, 1):
+        for side in range(4):
             owner = owner_of(index_ref, places[t + side])
             part = slice(side * 128, side * 128 + 128)
             for kind, row in enumerate((top, total, weight)):
@@ -171,7 +180,7 @@
         )
         s = lax.dot_general(k_ref[...], q_ref[cols, :], NT, preferred_element_type=jnp.float32)
         g = lax.dot_general(v_ref[...], c_ref[cols, :], NT, preferred_element_type=jnp.float32)
-        p = jnp.exp2(s * (SCALING * LOG2E) - log_total)
+        p = jnp.exp2(s - log_total)
         ds = (p * (g - delta)).astype(jnp.bfloat16)
         dv = jnp.dot(p.astype(jnp.bfloat16), c_ref[cols, :], preferred_element_type=jnp.float32)
         dk = jnp.dot(ds, q_ref[cols, :], preferred_element_type=jnp.float32)
@@ -182,7 +191,7 @@
             dv_ref[...] += dv
             dk_ref[...] += dk
         dq = jnp.dot(k_turned, ds, preferred_element_type=jnp.float32)
-        dq = (dq * SCALING).T.astype(jnp.bfloat16)
+        dq = (dq / LOG2E).T.astype(jnp.bfloat16)
         dq_refs[t][...] = dq[:128]
         dq_refs[t + 1][...] = dq[128:]
     for place in range(8):
@@ -280,15 +289,21 @@
     f32 = jnp.float32
     q_float = q_raw.astype(f32)
     k_float = k_raw.astype(f32)
-    squares = jnp.stack(
-        [jnp.sum(q_float * q_float, axis=1), jnp.sum(k_float * k_float, axis=1)]
-    )
-    inverse = lax.rsqrt(sum_heads_axes(squares) / inner_width + EPSILON)
+    both = jnp.stack([q_raw, k_raw]).astype(f32)
+    squares = jnp.sum(both * both, axis=2)
     cosine, signed_sine = rotation(positions, heads)
+    squares = squares + flip(squares, "c")
+    squares, cotangent = lax.optimization_barrier((squares, cotangent))
+    inverse = lax.rsqrt((squares + flip(squares, "xh")) / inner_width + EPSILON)
     q_normed = q_float * inverse[0][:, None]
     k_normed = k_float * inverse[1][:, None]
-    q_rot = rotate(q_normed, cosine, signed_sine, 1.0).astype(jnp.bfloat16)
-    k_rot = rotate(k_normed, cosine, signed_sine, 1.0).astype(jnp.bfloat16)
+    q_rot, k_rot = (
+        (
+            (factor * inverse[row])[:, None]
+            * (raw.astype(f32) * cosine + partner_of(raw) * signed_sine)
+        ).astype(jnp.bfloat16)
+        for row, (raw, factor) in enumerate(((q_raw, 1.0), (k_raw, SCALING * LOG2E)))
+    )
     gate_row = lax.dynamic_slice_in_dim(modulation, step_index[0], 1, 0)
     gated_cot = (gate_row * cotangent.astype(f32)).astype(jnp.bfloat16)
     attn_cot = lax.dot_general(

time: 151 us -> 146 us (0.967); the launches traced: 149 us -> 146 us
  local copies, waits for them, and re-layouts: 8.19 us -> 2.91 us
  matrix products: 3.36 us -> 5.71 us
  starting transfers between devices: 52.7 us -> 54.5 us
    ppermute x6 -> x3, starting transfers between devices: 11.7 us -> 5.76 us  [sum_heads_axes(): lax.ppermute(x, HEADS_AXES, [(i, i ^ mask) for i in range(4)])]
    ppermute x1 -> x3, starting transfers between devices: 0.09 us -> 4.82 us  [flip(): return lax.ppermute(x, axis, [(0, 1), (1, 0)])]
    ppermute x24, starting transfers between devices: 36 us -> 39.3 us  [shift(): lax.ppermute(x, axis, [(i, (i + distance) % size) for i in range(size)])]
    ppermute x24, waiting for transfers between devices: 33.4 us -> 30.1 us  [shift(): lax.ppermute(x, axis, [(i, (i + distance) % size) for i in range(size)])]
    dot_general x1, matrix products: 2.15 us -> 5.08 us  [shards(): lax.dot_general(gated_cot, out_weight, NT, preferred_element_type=f32)]
    another operation x5 -> x0, local copies, waits for them, and re-layouts: 2.84 us -> none  [the longest x2 2 us: rotation(): jnp.tile(signed_sine, (1, heads_count))]
    unnamed x48 -> x56, local copies, waits for them, and re-layouts: 2.5 us -> 0.66 us
    ppermute x1 -> x3, waiting for transfers between devices: 0.8 us -> 2.59 us  [flip(): return lax.ppermute(x, axis, [(0, 1), (1, 0)])]
  transfers between devices with their start and end apart: 32 -> 31, of which waited for: 15 -> 16; matrix products, arithmetic and copies ran while one was open for 6% -> 7% of each run, Pallas kernels for 0% -> 0%
where the time goes in v1:
time: 146 us
  starting transfers between devices  54.5 us (37%)
  waiting for transfers between devices  42.6 us (29%)
  Pallas kernels  28 us (19%)
  other arithmetic  10.2 us (7%)
  matrix products  5.71 us (4%)
  local copies, waits for them, and re-layouts  2.91 us (2%)
  between operations  1.87 us (1%)
    ppermute x24, starting transfers between devices, shift(): lax.ppermute(x, axis, [(i, (i + distance) % size) for i in range(size)])  39.3 us
    ppermute x24, waiting for transfers between devices, shift(): lax.ppermute(x, axis, [(i, (i + distance) % size) for i in range(size)])  30.1 us
    pallas_call x1, Pallas kernels, block_grads(): pl.pallas_call(functools.partial(grads_kernel, places, counts, heads), gr...  16.4 us
    pallas_call x1, Pallas kernels, block_stats(): pl.pallas_call(functools.partial(stats_kernel, places, counts, heads), gr...  11.5 us
    all_to_all x1, waiting for transfers between devices, shards(): lax.all_to_all(dkv, ('xl', 'y'), 0, 0, tiled=True).astype(f32)  8.43 us
    ppermute x3, starting transfers between devices, sum_heads_axes(): lax.ppermute(x, HEADS_AXES, [(i, i ^ mask) for i in range(4)])  5.76 us
    dot_general x1, matrix products, shards(): lax.dot_general(gated_cot, out_weight, NT, preferred_element_type=f32)  5.08 us
    ppermute x3, starting transfers between devices, flip(): return lax.ppermute(x, axis, [(0, 1), (1, 0)])  4.82 us
  transfers between devices with their start and end apart: 31, of which 16 were waited for; matrix products, arithmetic and copies ran while one was open for 7% of the time, Pallas kernels for 0%

profile of v1, /device:TPU:1, one launch (start us, length us, event | category | flops | bytes accessed | tf_op | source)
XLA Modules:
  0.0 145.7 jit_solution(14567097767568012898)
XLA Ops:
  1.9 3.3 %collective-permute-start = (f32[2,128]{1,0:T(2,128)S(1)}, f32[2,128]{1,0:T(2,128)S(1)}, u32[]{:S(2)}, u32[]{:S(2)}) collective-permute-start(f32[2,128]{1,0:T(2,128)S(1)} %multiply_reduce_fusion), channel_id=1, source_target_pairs={{0,1},{1,0},{2,3},{3,2},{4,5},{5,4},{6,7},{7,6},{8,9},{9,8},{10,11... | collective-permute-start | bytes 3080 | tf_op jit(solution)/shard_map/ppermute | solution.py:72
  9.0 5.1 %fusion.10 = bf16[128,640]{1,0:T(8,128)(2,1)S(1)} fusion(bf16[640,5120]{1,0:T(8,128)(2,1)} %param.19, bf16[128,5120]{1,0:T(8,128)(2,1)S(1)} %copy-done.4, f32[5120]{0:T(1024)S(1)} %bitcast.63), kind=kOutput, calls=%fused_computation.14 | convolution fusion | flops 840908800 | bytes 8048640 | tf_op jit(solution)/shard_map/dot_general | solution.py:309
  15.8 1.7 %collective-permute-start.2 = (bf16[128,1280]{1,0:T(8,128)(2,1)S(1)}, bf16[128,1280]{1,0:T(8,128)(2,1)S(1)}, u32[]{:S(2)}, u32[]{:S(2)}) collective-permute-start(bf16[128,1280]{1,0:T(8,128)(2,1)S(1)} %pad_maximum_fusion.1.refs_0_.refs_9_), channel_id=1, source_target_pairs={{0,16},{16,32},{32,48},{48,64},{64,80},{80,96},{96,112},{112,0},{1... | collective-permute-start | bytes 983048 | tf_op jit(solution)/shard_map/ppermute | solution.py:68
  17.5 4.0 %collective-permute-start.6 = (bf16[128,1280]{1,0:T(8,128)(2,1)S(1)}, bf16[128,1280]{1,0:T(8,128)(2,1)S(1)}, u32[]{:S(2)}, u32[]{:S(2)}) collective-permute-start(bf16[128,1280]{1,0:T(8,128)(2,1)S(1)} %pad_maximum_fusion.1.refs_0_.refs_9_), channel_id=1, source_target_pairs={{0,112},{16,0},{32,16},{48,32},{64,48},{80,64},{96,80},{112,96},{1... | collective-permute-start | bytes 983048 | tf_op jit(solution)/shard_map/ppermute | solution.py:68
  21.5 2.6 %collective-permute-done.10 = bf16[128,1280]{1,0:T(8,128)(2,1)S(1)} collective-permute-done((bf16[128,1280]{1,0:T(8,128)(2,1)S(1)}, bf16[128,1280]{1,0:T(8,128)(2,1)S(1)}, u32[]{:S(2)}, u32[]{:S(2)}) %collective-permute-start.10) | collective-permute-done | bytes 327712 | tf_op jit(solution)/shard_map/ppermute | solution.py:72
  27.1 1.9 %collective-permute-done.2.refs_1_.refs_10_ = bf16[128,1280]{1,0:T(8,128)(2,1)S(1)} collective-permute-done((bf16[128,1280]{1,0:T(8,128)(2,1)S(1)}, bf16[128,1280]{1,0:T(8,128)(2,1)S(1)}, u32[]{:S(2)}, u32[]{:S(2)}) %collective-permute-start.2) | collective-permute-done | bytes 327712 | tf_op jit(solution)/shard_map/ppermute | solution.py:68
  29.0 3.7 %collective-permute-start.7 = (bf16[128,1280]{1,0:T(8,128)(2,1)S(1)}, bf16[128,1280]{1,0:T(8,128)(2,1)S(1)}, u32[]{:S(2)}, u32[]{:S(2)}) collective-permute-start(bf16[128,1280]{1,0:T(8,128)(2,1)S(1)} %collective-permute-done.6.refs_8_.refs_17_), channel_id=1, source_target_pairs={{0,112},{16,0},{32,16},{48,32},{64,48},{80,64},{96,80},{112,96},{1... | collective-permute-start | bytes 983048 | tf_op jit(solution)/shard_map/ppermute | solution.py:68
  32.8 6.4 %collective-permute-done.3.refs_2_.refs_11_ = bf16[128,1280]{1,0:T(8,128)(2,1)S(1)} collective-permute-done((bf16[128,1280]{1,0:T(8,128)(2,1)S(1)}, bf16[128,1280]{1,0:T(8,128)(2,1)S(1)}, u32[]{:S(2)}, u32[]{:S(2)}) %collective-permute-start.3) | collective-permute-done | bytes 327712 | tf_op jit(solution)/shard_map/ppermute | solution.py:68
  39.2 2.7 %collective-permute-start.8 = (bf16[128,1280]{1,0:T(8,128)(2,1)S(1)}, bf16[128,1280]{1,0:T(8,128)(2,1)S(1)}, u32[]{:S(2)}, u32[]{:S(2)}) collective-permute-start(bf16[128,1280]{1,0:T(8,128)(2,1)S(1)} %collective-permute-done.7.refs_7_.refs_16_), channel_id=1, source_target_pairs={{0,112},{16,0},{32,16},{48,32},{64,48},{80,64},{96,80},{112,96},{1... | collective-permute-start | bytes 983048 | tf_op jit(solution)/shard_map/ppermute | solution.py:68
  43.2 2.2 %collective-permute-start.14 = (bf16[128,1280]{1,0:T(8,128)(2,1)}, bf16[128,1280]{1,0:T(8,128)(2,1)}, u32[]{:S(2)}, u32[]{:S(2)}) collective-permute-start(bf16[128,1280]{1,0:T(8,128)(2,1)} %slice.164), channel_id=1, source_target_pairs={{0,12},{4,0},{8,4},{12,8},{1,13},{5,1},{9,5},{13,9},{2,14},{6,2},{... | collective-permute-start | bytes 983048 | tf_op jit(solution)/shard_map/ppermute | solution.py:68
  45.4 2.0 %collective-permute-done.4.refs_3_.refs_12_ = bf16[128,1280]{1,0:T(8,128)(2,1)S(1)} collective-permute-done((bf16[128,1280]{1,0:T(8,128)(2,1)S(1)}, bf16[128,1280]{1,0:T(8,128)(2,1)S(1)}, u32[]{:S(2)}, u32[]{:S(2)}) %collective-permute-start.4) | collective-permute-done | bytes 327712 | tf_op jit(solution)/shard_map/ppermute | solution.py:68
  47.7 2.7 %collective-permute-start.9 = (bf16[64,1280]{1,0:T(8,128)(2,1)S(1)}, bf16[64,1280]{1,0:T(8,128)(2,1)}, u32[]{:S(2)}, u32[]{:S(2)}) collective-permute-start(bf16[64,1280]{1,0:T(8,128)(2,1)S(1)} %slice.162), channel_id=1, source_target_pairs={{0,112},{16,0},{32,16},{48,32},{64,48},{80,64},{96,80},{112,96},{1... | collective-permute-start | bytes 491528 | tf_op jit(solution)/shard_map/ppermute | solution.py:68
  51.1 2.0 %collective-permute-done.5.refs_4_.refs_13_ = bf16[64,1280]{1,0:T(8,128)(2,1)} collective-permute-done((bf16[64,1280]{1,0:T(8,128)(2,1)S(1)}, bf16[64,1280]{1,0:T(8,128)(2,1)}, u32[]{:S(2)}, u32[]{:S(2)}) %collective-permute-start.5) | collective-permute-done | bytes 163872 | tf_op jit(solution)/shard_map/ppermute | solution.py:68
  53.2 11.5 %block_stats.1 = f32[8,16,128]{2,1,0:T(8,128)} custom-call(s32[3]{0:T(128)} %pad_add_fusion.2.index_ref, bf16[128,1280]{1,0:T(8,128)(2,1)} %copy-done.7, bf16[128,1280]{1,0:T(8,128)(2,1)} %copy-done.20, bf16[128,1280]{1,0:T(8,128)(2,1)} %copy-done.22, bf16[128,1280]{1,0:T(8,128)(2,1)} %copy-done.18, ...), custom_call_target="tpu_custom_call" | custom-call | flops 10737418240 | bytes 8388608 | tf_op jit(solution)/shard_map/block_stats/pallas_call | solution.py:227
  64.9 4.8 %collective-permute-done.15 = f32[8,16,128]{2,1,0:T(8,128)S(1)} collective-permute-done((f32[8,16,128]{2,1,0:T(8,128)}, f32[8,16,128]{2,1,0:T(8,128)S(1)}, u32[]{:S(2)}, u32[]{:S(2)}) %collective-permute-start.15) | collective-permute-done | bytes 65568 | tf_op jit(solution)/shard_map/ppermute | solution.py:68
  71.5 3.8 %collective-permute-start.18 = (f32[8,16,128]{2,1,0:T(8,128)S(1)}, f32[8,16,128]{2,1,0:T(8,128)S(1)}, u32[]{:S(2)}, u32[]{:S(2)}) collective-permute-start(f32[8,16,128]{2,1,0:T(8,128)S(1)} %maximum_maximum_fusion), channel_id=1, source_target_pairs={{0,64},{16,80},{32,96},{48,112},{64,0},{80,16},{96,32},{112,48},{1... | collective-permute-start | bytes 196616 | tf_op jit(solution)/shard_map/ppermute | solution.py:68
  76.0 1.6 %collective-permute-start.16 = (f32[8,16,128]{2,1,0:T(8,128)S(1)}, f32[8,16,128]{2,1,0:T(8,128)S(1)}, u32[]{:S(2)}, u32[]{:S(2)}) collective-permute-start(f32[8,16,128]{2,1,0:T(8,128)S(1)} %maximum_maximum_fusion), channel_id=1, source_target_pairs={{0,32},{16,48},{32,64},{48,80},{64,96},{80,112},{96,0},{112,16},{1... | collective-permute-start | bytes 196616 | tf_op jit(solution)/shard_map/ppermute | solution.py:68
  79.5 1.9 %collective-permute-done.16 = f32[8,16,128]{2,1,0:T(8,128)S(1)} collective-permute-done((f32[8,16,128]{2,1,0:T(8,128)S(1)}, f32[8,16,128]{2,1,0:T(8,128)S(1)}, u32[]{:S(2)}, u32[]{:S(2)}) %collective-permute-start.16) | collective-permute-done | bytes 65568 | tf_op jit(solution)/shard_map/ppermute | solution.py:68
  82.2 16.4 %block_grads.1 = (bf16[128,640]{1,0:T(8,128)(2,1)}, bf16[128,640]{1,0:T(8,128)(2,1)}, bf16[128,640]{1,0:T(8,128)(2,1)}, bf16[128,640]{1,0:T(8,128)(2,1)}, bf16[1...) custom-call(s32[3]{0:T(128)} %pad_add_fusion.2.index_ref, ...), custom_call_target="tpu_custom_call" | custom-call | flops 13421772800 | bytes 16777216 | tf_op jit(solution)/shard_map/block_grads/pallas_call | solution.py:247
  98.6 4.5 %all-to-all-start = ((bf16[8,2,128,640]{3,2,1,0:T(8,128)(2,1)}), bf16[8,2,128,640]{3,2,1,0:T(8,128)(2,1)}, u32[]{:S(2)}, u32[]{:S(2)}) async-start(bf16[8,2,128,640]{3,2,1,0:T(8,128)(2,1)} %get-tuple-element.28), calls=%async_computation | async-start | bytes 5242880 | tf_op jit(solution)/shard_map/all_to_all | solution.py:325
  103.2 2.1 %collective-permute-start.23 = (bf16[64,640]{1,0:T(8,128)(2,1)S(1)}, bf16[64,640]{1,0:T(8,128)(2,1)S(1)}, u32[]{:S(2)}, u32[]{:S(2)}) collective-permute-start(bf16[64,640]{1,0:T(8,128)(2,1)S(1)} %get-tuple-element.48), channel_id=1, source_target_pairs={{0,16},{16,32},{32,48},{48,64},{64,80},{80,96},{96,112},{112,0},{1... | collective-permute-start | bytes 245768 | tf_op jit(solution)/shard_map/ppermute | solution.py:68
  106.0 1.8 %collective-permute-done.23 = bf16[64,640]{1,0:T(8,128)(2,1)S(1)} collective-permute-done((bf16[64,640]{1,0:T(8,128)(2,1)S(1)}, bf16[64,640]{1,0:T(8,128)(2,1)S(1)}, u32[]{:S(2)}, u32[]{:S(2)}) %collective-permute-start.23) | collective-permute-done | bytes 81952 | tf_op jit(solution)/shard_map/ppermute | solution.py:68
  108.8 2.1 %collective-permute-start.20 = (bf16[128,640]{1,0:T(8,128)(2,1)S(1)}, bf16[128,640]{1,0:T(8,128)(2,1)S(1)}, u32[]{:S(2)}, u32[]{:S(2)}) collective-permute-start(bf16[128,640]{1,0:T(8,128)(2,1)S(1)} %pad_add_fusion.1), channel_id=1, source_target_pairs={{0,112},{16,0},{32,16},{48,32},{64,48},{80,64},{96,80},{112,96},{1... | collective-permute-start | bytes 491528 | tf_op jit(solution)/shard_map/ppermute | solution.py:68
  110.9 2.4 %collective-permute-done.24 = bf16[128,640]{1,0:T(8,128)(2,1)S(1)} collective-permute-done((bf16[128,640]{1,0:T(8,128)(2,1)S(1)}, bf16[128,640]{1,0:T(8,128)(2,1)S(1)}, u32[]{:S(2)}, u32[]{:S(2)}) %collective-permute-start.24) | collective-permute-done | bytes 163872 | tf_op jit(solution)/shard_map/ppermute | solution.py:68
  113.5 3.2 %collective-permute-start.21 = (bf16[128,640]{1,0:T(8,128)(2,1)S(1)}, bf16[128,640]{1,0:T(8,128)(2,1)S(1)}, u32[]{:S(2)}, u32[]{:S(2)}) collective-permute-start(bf16[128,640]{1,0:T(8,128)(2,1)S(1)} %add.126), channel_id=1, source_target_pairs={{0,112},{16,0},{32,16},{48,32},{64,48},{80,64},{96,80},{112,96},{1... | collective-permute-start | bytes 491528 | tf_op jit(solution)/shard_map/ppermute | solution.py:68
  116.7 2.5 %collective-permute-done.25 = bf16[128,640]{1,0:T(8,128)(2,1)S(1)} collective-permute-done((bf16[128,640]{1,0:T(8,128)(2,1)S(1)}, bf16[128,640]{1,0:T(8,128)(2,1)S(1)}, u32[]{:S(2)}, u32[]{:S(2)}) %collective-permute-start.25) | collective-permute-done | bytes 163872 | tf_op jit(solution)/shard_map/ppermute | solution.py:68
  119.4 3.2 %collective-permute-start.22 = (bf16[128,640]{1,0:T(8,128)(2,1)S(1)}, bf16[128,640]{1,0:T(8,128)(2,1)S(1)}, u32[]{:S(2)}, u32[]{:S(2)}) collective-permute-start(bf16[128,640]{1,0:T(8,128)(2,1)S(1)} %add.127), channel_id=1, source_target_pairs={{0,112},{16,0},{32,16},{48,32},{64,48},{80,64},{96,80},{112,96},{1... | collective-permute-start | bytes 491528 | tf_op jit(solution)/shard_map/ppermute | solution.py:68
  122.6 2.5 %collective-permute-done.26 = bf16[128,640]{1,0:T(8,128)(2,1)S(1)} collective-permute-done((bf16[128,640]{1,0:T(8,128)(2,1)S(1)}, bf16[128,640]{1,0:T(8,128)(2,1)S(1)}, u32[]{:S(2)}, u32[]{:S(2)}) %collective-permute-start.26) | collective-permute-done | bytes 163872 | tf_op jit(solution)/shard_map/ppermute | solution.py:68
  125.5 8.4 %all-to-all-done = bf16[8,2,128,640]{3,2,1,0:T(8,128)(2,1)} async-done(((bf16[8,2,128,640]{3,2,1,0:T(8,128)(2,1)}), bf16[8,2,128,640]{3,2,1,0:T(8,128)(2,1)}, u32[]{:S(2)}, u32[]{:S(2)}) %all-to-all-start) | async-done | bytes 2621472 | tf_op jit(solution)/shard_map/all_to_all | solution.py:325
  133.9 2.2 %convert_reduce_fusion = f32[2,128,640]{2,1,0:T(8,128)S(1)} fusion(bf16[8,2,128,640]{3,2,1,0:T(8,128)(2,1)} %all-to-all-done), kind=kLoop, calls=%fused_computation | loop fusion | flops 2457600 | bytes 3276800 | tf_op jit(solution)/shard_map/reduce_sum | solution.py:325
  136.9 3.9 %collective-permute-start.29 = (f32[2,128]{1,0:T(2,128)S(1)}, f32[2,128]{1,0:T(2,128)S(1)}, u32[]{:S(2)}, u32[]{:S(2)}) collective-permute-start(f32[2,128]{1,0:T(2,128)S(1)} %pad_maximum_fusion.3), channel_id=1, source_target_pairs={{0,3},{1,2},{2,1},{3,0},{4,7},{5,6},{6,5},{7,4},{8,11},{9,10},{10,... | collective-permute-start | bytes 3080 | tf_op jit(solution)/shard_map/ppermute | solution.py:78
  140.9 1.8 %collective-permute-start.28 = (f32[2,128]{1,0:T(2,128)S(1)}, f32[2,128]{1,0:T(2,128)S(1)}, u32[]{:S(2)}, u32[]{:S(2)}) collective-permute-start(f32[2,128]{1,0:T(2,128)S(1)} %pad_maximum_fusion.3), channel_id=1, source_target_pairs={{0,2},{1,3},{2,0},{3,1},{4,6},{5,7},{6,4},{7,5},{8,10},{9,11},{10,... | collective-permute-start | bytes 3080 | tf_op jit(solution)/shard_map/ppermute | solution.py:78
  (139 shorter events, 22.6 us)
Async XLA Ops:
  1.9 5.9 %collective-permute-start = (f32[2,128]{1,0:T(2,128)S(1)}, f32[2,128]{1,0:T(2,128)S(1)}, u32[]{:S(2)}, u32[]{:S(2)}) collective-permute-start(f32[2,128]{1,0:T(2,128)S(1)} %multiply_reduce_fusion), channel_id=1, source_target_pairs={{0,1},{1,0},{2,3},{3,2},{4,5},{5,4},{6,7},{7,6},{8,9},{9,8},{10,11... | collective-permute-start | bytes 3080 | tf_op jit(solution)/shard_map/ppermute | solution.py:72
  7.9 6.2 %collective-permute-start.1 = (f32[2,128]{1,0:T(2,128)S(1)}, f32[2,128]{1,0:T(2,128)S(1)}, u32[]{:S(2)}, u32[]{:S(2)}) collective-permute-start(f32[2,128]{1,0:T(2,128)S(1)} %add.107), channel_id=1, source_target_pairs={{0,2},{2,0},{1,3},{3,1},{4,6},{6,4},{5,7},{7,5},{8,10},{10,8},{9,1... | collective-permute-start | bytes 3080 | tf_op jit(solution)/shard_map/ppermute | solution.py:72
  15.0 9.1 %collective-permute-start.10 = (bf16[128,1280]{1,0:T(8,128)(2,1)S(1)}, bf16[128,1280]{1,0:T(8,128)(2,1)S(1)}, u32[]{:S(2)}, u32[]{:S(2)}) collective-permute-start(bf16[128,1280]{1,0:T(8,128)(2,1)S(1)} %pad_maximum_fusion.2), channel_id=1, source_target_pairs={{0,128},{128,0},{1,129},{129,1},{2,130},{130,2},{3,131},{131,3},{4... | collective-permute-start | bytes 983048 | tf_op jit(solution)/shard_map/ppermute | solution.py:72
  15.8 13.2 %collective-permute-start.2 = (bf16[128,1280]{1,0:T(8,128)(2,1)S(1)}, bf16[128,1280]{1,0:T(8,128)(2,1)S(1)}, u32[]{:S(2)}, u32[]{:S(2)}) collective-permute-start(bf16[128,1280]{1,0:T(8,128)(2,1)S(1)} %pad_maximum_fusion.1.refs_0_.refs_9_), channel_id=1, source_target_pairs={{0,16},{16,32},{32,48},{48,64},{64,80},{80,96},{96,112},{112,0},{1... | collective-permute-start | bytes 983048 | tf_op jit(solution)/shard_map/ppermute | solution.py:68
  17.5 11.5 %collective-permute-start.6 = (bf16[128,1280]{1,0:T(8,128)(2,1)S(1)}, bf16[128,1280]{1,0:T(8,128)(2,1)S(1)}, u32[]{:S(2)}, u32[]{:S(2)}) collective-permute-start(bf16[128,1280]{1,0:T(8,128)(2,1)S(1)} %pad_maximum_fusion.1.refs_0_.refs_9_), channel_id=1, source_target_pairs={{0,112},{16,0},{32,16},{48,32},{64,48},{80,64},{96,80},{112,96},{1... | collective-permute-start | bytes 983048 | tf_op jit(solution)/shard_map/ppermute | solution.py:68
  24.2 29.0 %copy-start.6 = (bf16[256,1280]{1,0:T(8,128)(2,1)}, bf16[256,1280]{1,0:T(8,128)(2,1)S(1)}, u32[]{:S(2)}) copy-start(bf16[256,1280]{1,0:T(8,128)(2,1)S(1)} %pad_maximum_fusion.refs_18_.refs_23_) | copy-start | bytes 1966084
  24.2 17.7 %collective-permute-start.11 = (bf16[256,1280]{1,0:T(8,128)(2,1)S(1)}, bf16[256,1280]{1,0:T(8,128)(2,1)S(1)}, u32[]{:S(2)}, u32[]{:S(2)}) collective-permute-start(bf16[256,1280]{1,0:T(8,128)(2,1)S(1)} %pad_maximum_fusion.refs_18_.refs_23_), channel_id=1, source_target_pairs={{0,4},{4,8},{8,12},{12,0},{1,5},{5,9},{9,13},{13,1},{2,6},{6,10},{... | collective-permute-start | bytes 1966088 | tf_op jit(solution)/shard_map/ppermute | solution.py:68
  25.6 16.8 %collective-permute-start.13 = (bf16[256,1280]{1,0:T(8,128)(2,1)S(1)}, bf16[256,1280]{1,0:T(8,128)(2,1)S(1)}, u32[]{:S(2)}, u32[]{:S(2)}) collective-permute-start(bf16[256,1280]{1,0:T(8,128)(2,1)S(1)} %pad_maximum_fusion.refs_18_.refs_23_), channel_id=1, source_target_pairs={{0,12},{4,0},{8,4},{12,8},{1,13},{5,1},{9,5},{13,9},{2,14},{6,2},{... | collective-permute-start | bytes 1966088 | tf_op jit(solution)/shard_map/ppermute | solution.py:68
  29.0 10.2 %collective-permute-start.3 = (bf16[128,1280]{1,0:T(8,128)(2,1)S(1)}, bf16[128,1280]{1,0:T(8,128)(2,1)S(1)}, u32[]{:S(2)}, u32[]{:S(2)}) collective-permute-start(bf16[128,1280]{1,0:T(8,128)(2,1)S(1)} %collective-permute-done.2.refs_1_.refs_10_), channel_id=1, source_target_pairs={{0,16},{16,32},{32,48},{48,64},{64,80},{80,96},{96,112},{112,0},{1... | collective-permute-start | bytes 983048 | tf_op jit(solution)/shard_map/ppermute | solution.py:68
  29.0 10.1 %collective-permute-start.7 = (bf16[128,1280]{1,0:T(8,128)(2,1)S(1)}, bf16[128,1280]{1,0:T(8,128)(2,1)S(1)}, u32[]{:S(2)}, u32[]{:S(2)}) collective-permute-start(bf16[128,1280]{1,0:T(8,128)(2,1)S(1)} %collective-permute-done.6.refs_8_.refs_17_), channel_id=1, source_target_pairs={{0,112},{16,0},{32,16},{48,32},{64,48},{80,64},{96,80},{112,96},{1... | collective-permute-start | bytes 983048 | tf_op jit(solution)/shard_map/ppermute | solution.py:68
  39.2 8.2 %collective-permute-start.4 = (bf16[128,1280]{1,0:T(8,128)(2,1)S(1)}, bf16[128,1280]{1,0:T(8,128)(2,1)S(1)}, u32[]{:S(2)}, u32[]{:S(2)}) collective-permute-start(bf16[128,1280]{1,0:T(8,128)(2,1)S(1)} %collective-permute-done.3.refs_2_.refs_11_), channel_id=1, source_target_pairs={{0,16},{16,32},{32,48},{48,64},{64,80},{80,96},{96,112},{112,0},{1... | collective-permute-start | bytes 983048 | tf_op jit(solution)/shard_map/ppermute | solution.py:68
  39.2 8.5 %collective-permute-start.8 = (bf16[128,1280]{1,0:T(8,128)(2,1)S(1)}, bf16[128,1280]{1,0:T(8,128)(2,1)S(1)}, u32[]{:S(2)}, u32[]{:S(2)}) collective-permute-start(bf16[128,1280]{1,0:T(8,128)(2,1)S(1)} %collective-permute-done.7.refs_7_.refs_16_), channel_id=1, source_target_pairs={{0,112},{16,0},{32,16},{48,32},{64,48},{80,64},{96,80},{112,96},{1... | collective-permute-start | bytes 983048 | tf_op jit(solution)/shard_map/ppermute | solution.py:68
  41.9 11.3 %collective-permute-start.12 = (bf16[128,1280]{1,0:T(8,128)(2,1)S(1)}, bf16[128,1280]{1,0:T(8,128)(2,1)}, u32[]{:S(2)}, u32[]{:S(2)}) collective-permute-start(bf16[128,1280]{1,0:T(8,128)(2,1)S(1)} %slice.163), channel_id=1, source_target_pairs={{0,4},{4,8},{8,12},{12,0},{1,5},{5,9},{9,13},{13,1},{2,6},{6,10},{... | collective-permute-start | bytes 983048 | tf_op jit(solution)/shard_map/ppermute | solution.py:68
  43.2 10.0 %collective-permute-start.14 = (bf16[128,1280]{1,0:T(8,128)(2,1)}, bf16[128,1280]{1,0:T(8,128)(2,1)}, u32[]{:S(2)}, u32[]{:S(2)}) collective-permute-start(bf16[128,1280]{1,0:T(8,128)(2,1)} %slice.164), channel_id=1, source_target_pairs={{0,12},{4,0},{8,4},{12,8},{1,13},{5,1},{9,5},{13,9},{2,14},{6,2},{... | collective-permute-start | bytes 983048 | tf_op jit(solution)/shard_map/ppermute | solution.py:68
  47.4 5.7 %collective-permute-start.5 = (bf16[64,1280]{1,0:T(8,128)(2,1)S(1)}, bf16[64,1280]{1,0:T(8,128)(2,1)}, u32[]{:S(2)}, u32[]{:S(2)}) collective-permute-start(bf16[64,1280]{1,0:T(8,128)(2,1)S(1)} %slice.161), channel_id=1, source_target_pairs={{0,16},{16,32},{32,48},{48,64},{64,80},{80,96},{96,112},{112,0},{1... | collective-permute-start | bytes 491528 | tf_op jit(solution)/shard_map/ppermute | solution.py:68
  47.7 5.4 %collective-permute-start.9 = (bf16[64,1280]{1,0:T(8,128)(2,1)S(1)}, bf16[64,1280]{1,0:T(8,128)(2,1)}, u32[]{:S(2)}, u32[]{:S(2)}) collective-permute-start(bf16[64,1280]{1,0:T(8,128)(2,1)S(1)} %slice.162), channel_id=1, source_target_pairs={{0,112},{16,0},{32,16},{48,32},{64,48},{80,64},{96,80},{112,96},{1... | collective-permute-start | bytes 491528 | tf_op jit(solution)/shard_map/ppermute | solution.py:68
  64.7 5.0 %collective-permute-start.15 = (f32[8,16,128]{2,1,0:T(8,128)}, f32[8,16,128]{2,1,0:T(8,128)S(1)}, u32[]{:S(2)}, u32[]{:S(2)}) collective-permute-start(f32[8,16,128]{2,1,0:T(8,128)} %block_stats.1), channel_id=1, source_target_pairs={{0,16},{16,32},{32,48},{48,64},{64,80},{80,96},{96,112},{112,0},{1... | collective-permute-start | bytes 196616 | tf_op jit(solution)/shard_map/ppermute | solution.py:68
  71.5 7.1 %collective-permute-start.18 = (f32[8,16,128]{2,1,0:T(8,128)S(1)}, f32[8,16,128]{2,1,0:T(8,128)S(1)}, u32[]{:S(2)}, u32[]{:S(2)}) collective-permute-start(f32[8,16,128]{2,1,0:T(8,128)S(1)} %maximum_maximum_fusion), channel_id=1, source_target_pairs={{0,64},{16,80},{32,96},{48,112},{64,0},{80,16},{96,32},{112,48},{1... | collective-permute-start | bytes 196616 | tf_op jit(solution)/shard_map/ppermute | solution.py:68
  75.3 4.2 %collective-permute-start.17 = (f32[8,16,128]{2,1,0:T(8,128)S(1)}, f32[8,16,128]{2,1,0:T(8,128)S(1)}, u32[]{:S(2)}, u32[]{:S(2)}) collective-permute-start(f32[8,16,128]{2,1,0:T(8,128)S(1)} %maximum_maximum_fusion), channel_id=1, source_target_pairs={{0,96},{16,112},{32,0},{48,16},{64,32},{80,48},{96,64},{112,80},{1... | collective-permute-start | bytes 196616 | tf_op jit(solution)/shard_map/ppermute | solution.py:68
  76.0 5.4 %collective-permute-start.16 = (f32[8,16,128]{2,1,0:T(8,128)S(1)}, f32[8,16,128]{2,1,0:T(8,128)S(1)}, u32[]{:S(2)}, u32[]{:S(2)}) collective-permute-start(f32[8,16,128]{2,1,0:T(8,128)S(1)} %maximum_maximum_fusion), channel_id=1, source_target_pairs={{0,32},{16,48},{32,64},{48,80},{64,96},{80,112},{96,0},{112,16},{1... | collective-permute-start | bytes 196616 | tf_op jit(solution)/shard_map/ppermute | solution.py:68
  98.6 35.3 %all-to-all-start = ((bf16[8,2,128,640]{3,2,1,0:T(8,128)(2,1)}), bf16[8,2,128,640]{3,2,1,0:T(8,128)(2,1)}, u32[]{:S(2)}, u32[]{:S(2)}) async-start(bf16[8,2,128,640]{3,2,1,0:T(8,128)(2,1)} %get-tuple-element.28), calls=%async_computation | async-start | bytes 5242880 | tf_op jit(solution)/shard_map/all_to_all | solution.py:325
  103.2 4.6 %collective-permute-start.23 = (bf16[64,640]{1,0:T(8,128)(2,1)S(1)}, bf16[64,640]{1,0:T(8,128)(2,1)S(1)}, u32[]{:S(2)}, u32[]{:S(2)}) collective-permute-start(bf16[64,640]{1,0:T(8,128)(2,1)S(1)} %get-tuple-element.48), channel_id=1, source_target_pairs={{0,16},{16,32},{32,48},{48,64},{64,80},{80,96},{96,112},{112,0},{1... | collective-permute-start | bytes 245768 | tf_op jit(solution)/shard_map/ppermute | solution.py:68
  105.4 3.4 %collective-permute-start.19 = (bf16[64,640]{1,0:T(8,128)(2,1)S(1)}, bf16[64,640]{1,0:T(8,128)(2,1)S(1)}, u32[]{:S(2)}, u32[]{:S(2)}) collective-permute-start(bf16[64,640]{1,0:T(8,128)(2,1)S(1)} %get-tuple-element.47), channel_id=1, source_target_pairs={{0,112},{16,0},{32,16},{48,32},{64,48},{80,64},{96,80},{112,96},{1... | collective-permute-start | bytes 245768 | tf_op jit(solution)/shard_map/ppermute | solution.py:68
  107.9 5.5 %collective-permute-start.24 = (bf16[128,640]{1,0:T(8,128)(2,1)S(1)}, bf16[128,640]{1,0:T(8,128)(2,1)S(1)}, u32[]{:S(2)}, u32[]{:S(2)}) collective-permute-start(bf16[128,640]{1,0:T(8,128)(2,1)S(1)} %pad_add_fusion), channel_id=1, source_target_pairs={{0,16},{16,32},{32,48},{48,64},{64,80},{80,96},{96,112},{112,0},{1... | collective-permute-start | bytes 491528 | tf_op jit(solution)/shard_map/ppermute | solution.py:68
  108.8 4.6 %collective-permute-start.20 = (bf16[128,640]{1,0:T(8,128)(2,1)S(1)}, bf16[128,640]{1,0:T(8,128)(2,1)S(1)}, u32[]{:S(2)}, u32[]{:S(2)}) collective-permute-start(bf16[128,640]{1,0:T(8,128)(2,1)S(1)} %pad_add_fusion.1), channel_id=1, source_target_pairs={{0,112},{16,0},{32,16},{48,32},{64,48},{80,64},{96,80},{112,96},{1... | collective-permute-start | bytes 491528 | tf_op jit(solution)/shard_map/ppermute | solution.py:68
  113.4 5.9 %collective-permute-start.25 = (bf16[128,640]{1,0:T(8,128)(2,1)S(1)}, bf16[128,640]{1,0:T(8,128)(2,1)S(1)}, u32[]{:S(2)}, u32[]{:S(2)}) collective-permute-start(bf16[128,640]{1,0:T(8,128)(2,1)S(1)} %add.130), channel_id=1, source_target_pairs={{0,16},{16,32},{32,48},{48,64},{64,80},{80,96},{96,112},{112,0},{1... | collective-permute-start | bytes 491528 | tf_op jit(solution)/shard_map/ppermute | solution.py:68
  113.5 5.8 %collective-permute-start.21 = (bf16[128,640]{1,0:T(8,128)(2,1)S(1)}, bf16[128,640]{1,0:T(8,128)(2,1)S(1)}, u32[]{:S(2)}, u32[]{:S(2)}) collective-permute-start(bf16[128,640]{1,0:T(8,128)(2,1)S(1)} %add.126), channel_id=1, source_target_pairs={{0,112},{16,0},{32,16},{48,32},{64,48},{80,64},{96,80},{112,96},{1... | collective-permute-start | bytes 491528 | tf_op jit(solution)/shard_map/ppermute | solution.py:68
  119.3 5.9 %collective-permute-start.26 = (bf16[128,640]{1,0:T(8,128)(2,1)S(1)}, bf16[128,640]{1,0:T(8,128)(2,1)S(1)}, u32[]{:S(2)}, u32[]{:S(2)}) collective-permute-start(bf16[128,640]{1,0:T(8,128)(2,1)S(1)} %add.131), channel_id=1, source_target_pairs={{0,16},{16,32},{32,48},{48,64},{64,80},{80,96},{96,112},{112,0},{1... | collective-permute-start | bytes 491528 | tf_op jit(solution)/shard_map/ppermute | solution.py:68
  119.4 5.8 %collective-permute-start.22 = (bf16[128,640]{1,0:T(8,128)(2,1)S(1)}, bf16[128,640]{1,0:T(8,128)(2,1)S(1)}, u32[]{:S(2)}, u32[]{:S(2)}) collective-permute-start(bf16[128,640]{1,0:T(8,128)(2,1)S(1)} %add.127), channel_id=1, source_target_pairs={{0,112},{16,0},{32,16},{48,32},{64,48},{80,64},{96,80},{112,96},{1... | collective-permute-start | bytes 491528 | tf_op jit(solution)/shard_map/ppermute | solution.py:68
  136.9 6.5 %collective-permute-start.29 = (f32[2,128]{1,0:T(2,128)S(1)}, f32[2,128]{1,0:T(2,128)S(1)}, u32[]{:S(2)}, u32[]{:S(2)}) collective-permute-start(f32[2,128]{1,0:T(2,128)S(1)} %pad_maximum_fusion.3), channel_id=1, source_target_pairs={{0,3},{1,2},{2,1},{3,0},{4,7},{5,6},{6,5},{7,4},{8,11},{9,10},{10,... | collective-permute-start | bytes 3080 | tf_op jit(solution)/shard_map/ppermute | solution.py:78
  140.9 3.9 %collective-permute-start.28 = (f32[2,128]{1,0:T(2,128)S(1)}, f32[2,128]{1,0:T(2,128)S(1)}, u32[]{:S(2)}, u32[]{:S(2)}) collective-permute-start(f32[2,128]{1,0:T(2,128)S(1)} %pad_maximum_fusion.3), channel_id=1, source_target_pairs={{0,2},{1,3},{2,0},{3,1},{4,6},{5,7},{6,4},{7,5},{8,10},{9,11},{10,... | collective-permute-start | bytes 3080 | tf_op jit(solution)/shard_map/ppermute | solution.py:78
  142.7 2.1 %collective-permute-start.27 = (f32[2,128]{1,0:T(2,128)S(1)}, f32[2,128]{1,0:T(2,128)S(1)}, u32[]{:S(2)}, u32[]{:S(2)}) collective-permute-start(f32[2,128]{1,0:T(2,128)S(1)} %pad_maximum_fusion.3), channel_id=1, source_target_pairs={{0,1},{1,0},{2,3},{3,2},{4,5},{5,4},{6,7},{7,6},{8,9},{9,8},{10,11... | collective-permute-start | bytes 3080 | tf_op jit(solution)/shard_map/ppermute | solution.py:78
  (23 other events, 220.4 us)

commit v2 on v1

--- a/solution.py
+++ b/solution.py
@@ -68,6 +68,10 @@
     return lax.ppermute(x, axis, [(i, (i + distance) % size) for i in range(size)])
 
 
+def swap(x, axis, mask):
+    return lax.ppermute(x, axis, [(i, i ^ mask) for i in range(lax.axis_size(axis))])
+
+
 def flip(x, axis):
     return lax.ppermute(x, axis, [(0, 1), (1, 0)])
 
@@ -93,12 +97,19 @@
 
 def ring_reduce(blocks):
     half = blocks[4].shape[0] // 2
-    low, high = shift(blocks[4][:half], "z", -1), shift(blocks[4][half:], "z", 1)
-    left = blocks[3] + jnp.concatenate([low, jnp.zeros_like(low)], axis=0)
-    right = blocks[5] + jnp.concatenate([jnp.zeros_like(high), high], axis=0)
-    for near in (2, 1):
-        left = blocks[near] + shift(left, "z", -1)
-        right = blocks[8 - near] + shift(right, "z", 1)
+    low, high = shift(blocks[4][:half], "z", -2), shift(blocks[4][half:], "z", 2)
+    left = (
+        blocks[2]
+        + shift(blocks[3], "z", -1)
+        + jnp.concatenate([low, jnp.zeros_like(low)], axis=0)
+    )
+    right = (
+        blocks[6]
+        + shift(blocks[5], "z", 1)
+        + jnp.concatenate([jnp.zeros_like(high), high], axis=0)
+    )
+    left = blocks[1] + shift(left, "z", -1)
+    right = blocks[7] + shift(right, "z", 1)
     f32 = jnp.float32
     return (
         blocks[0].astype(f32)
@@ -107,9 +118,9 @@
     )
 
 
-def plane_gather(x):
+def plane_gather(x, flipped):
     rows = x.shape[0]
-    pair = jnp.concatenate([x, flip(x, "xl")], axis=0)
+    pair = jnp.concatenate([x, flipped], axis=0)
     left, right = shift(pair, "y", 1), shift(pair, "y", -1)
     low, high = shift(left[:rows], "y", 1), shift(right[rows:], "y", -1)
     return [pair, left, low, high, right]
@@ -265,21 +276,13 @@
 
 
 def merge(parts, heads):
-    kinds = [
-        [part[:, first * heads : (first + 1) * heads] for first in range(3)] for part in parts
+    tops = [
+        jnp.concatenate([part[:, :heads]] * 3 + [part[:, : 16 - 3 * heads]], axis=1)
+        for part in parts
     ]
-    top = functools.reduce(jnp.maximum, [kind[0] for kind in kinds])
-    total = weight = 0.0
-    for kind in kinds:
-        factor = jnp.exp2(kind[0] - top)
-        total = total + kind[1] * factor
-        weight = weight + kind[2] * factor
-    return top, total, weight
-
-
-def with_padding(rows):
-    used = sum(row.shape[1] for row in rows)
-    return jnp.concatenate([*rows, jnp.zeros((8, 16 - used, 128), jnp.float32)], axis=1)
+    top = functools.reduce(jnp.maximum, tops)
+    total = sum(part * jnp.exp2(own - top) for part, own in zip(parts, tops))
+    return jnp.where(jnp.arange(16)[None, :, None] < heads, top, total)
 
 
 def shards(q_raw, k_raw, values, positions, cotangent, out_weight, modulation, step_index):
@@ -289,6 +292,7 @@
     f32 = jnp.float32
     q_float = q_raw.astype(f32)
     k_float = k_raw.astype(f32)
+    values_flipped = flip(values, "xl")
     both = jnp.stack([q_raw, k_raw]).astype(f32)
     squares = jnp.sum(both * both, axis=2)
     cosine, signed_sine = rotation(positions, heads)
@@ -312,13 +316,18 @@
 
     index = jnp.stack([lax.axis_index("z"), lax.axis_index("y"), lax.axis_index("xl")])
     queries = ring_gather(jnp.concatenate([q_rot, attn_cot], axis=1))
-    keys = plane_gather(jnp.concatenate([k_rot, values], axis=1))
+    keys = plane_gather(
+        jnp.concatenate([k_rot, values], axis=1),
+        jnp.concatenate([flip(k_rot, "xl"), values_flipped], axis=1),
+    )
 
     places = list(range(8))
     stats = block_stats(index, places, queries, keys, heads)
-    stats = with_padding(merge([stats, shift(stats, "z", 1)], heads))
-    top, total, weight = merge([stats] + [shift(stats, "z", d) for d in (2, -2, 4)], heads)
-    totals = with_padding([top + jnp.log2(total), weight / total])
+    stats = merge([stats, swap(stats, "z", 1)], heads)
+    stats = merge([stats] + [swap(stats, "z", mask) for mask in (2, 4, 6)], heads)
+    top, total, weight = (stats[:, kind * heads : (kind + 1) * heads] for kind in range(3))
+    rest = jnp.zeros((8, 16 - 2 * heads, 128), f32)
+    totals = jnp.concatenate([top + jnp.log2(total), weight / total, rest], axis=1)
 
     dq, dkv = block_grads(index, places, queries, keys, totals, heads)
     dq_sum = ring_reduce(dq)

time: 146 us -> 142 us (0.973)
  waiting for transfers between devices: 42.6 us -> 37.7 us
  local copies, waits for them, and re-layouts: 2.91 us -> 4.41 us
    ppermute x24 -> x20, waiting for transfers between devices: 30.1 us -> 22.7 us  [shift(): lax.ppermute(x, axis, [(i, (i + distance) % size) for i in range(size)])]
    ppermute x24 -> x20, starting transfers between devices: 39.3 us -> 32.1 us  [shift(): lax.ppermute(x, axis, [(i, (i + distance) % size) for i in range(size)])]
    ppermute x0 -> x4, starting transfers between devices: none -> 5.84 us  [swap(): lax.ppermute(x, axis, [(i, i ^ mask) for i in range(lax.axis_size(axis))])]
    ppermute x0 -> x4, waiting for transfers between devices: none -> 5.6 us  [swap(): lax.ppermute(x, axis, [(i, i ^ mask) for i in range(lax.axis_size(axis))])]
    ppermute x3 -> x4, waiting for transfers between devices: 2.59 us -> 0.01 us  [flip(): return lax.ppermute(x, axis, [(0, 1), (1, 0)])]
    add x9 -> x5, other arithmetic: 1.96 us -> 0.22 us  [the longest x1 0.06 us: ring_reduce(): blocks[6] + shift(blocks[5], 'z', 1)]
    slice x0 -> x12, local copies, waits for them, and re-layouts: none -> 1.57 us  [the longest x6 0.79 us: merge(): part[:, :16 - 3 * heads]]
    ppermute x3 -> x4, starting transfers between devices: 4.82 us -> 5.45 us  [flip(): return lax.ppermute(x, axis, [(0, 1), (1, 0)])]
  transfers between devices with their start and end apart: 31 -> 32, of which waited for: 16 -> 14; matrix products, arithmetic and copies ran while one was open for 7% -> 9% of each run, Pallas kernels for 0% -> 0%
where the time goes in v2:
time: 142 us
  starting transfers between devices  53.4 us (38%)
  waiting for transfers between devices  37.7 us (27%)
  Pallas kernels  28 us (20%)
  other arithmetic  10.4 us (7%)
  matrix products  5.72 us (4%)
  local copies, waits for them, and re-layouts  4.41 us (3%)
  between operations  1.89 us (1%)
    ppermute x20, starting transfers between devices, shift(): lax.ppermute(x, axis, [(i, (i + distance) % size) for i in range(size)])  32.1 us
    ppermute x20, waiting for transfers between devices, shift(): lax.ppermute(x, axis, [(i, (i + distance) % size) for i in range(size)])  22.7 us
    pallas_call x1, Pallas kernels, block_grads(): pl.pallas_call(functools.partial(grads_kernel, places, counts, heads), gr...  16.4 us
    pallas_call x1, Pallas kernels, block_stats(): pl.pallas_call(functools.partial(stats_kernel, places, counts, heads), gr...  11.5 us
    all_to_all x1, waiting for transfers between devices, shards(): lax.all_to_all(dkv, ('xl', 'y'), 0, 0, tiled=True).astype(f32)  8.55 us
    ppermute x4, starting transfers between devices, swap(): lax.ppermute(x, axis, [(i, i ^ mask) for i in range(lax.axis_size(axis))])  5.84 us
    ppermute x4, waiting for transfers between devices, swap(): lax.ppermute(x, axis, [(i, i ^ mask) for i in range(lax.axis_size(axis))])  5.6 us
    ppermute x4, starting transfers between devices, flip(): return lax.ppermute(x, axis, [(0, 1), (1, 0)])  5.45 us
  transfers between devices with their start and end apart: 32, of which 14 were waited for; matrix products, arithmetic and copies ran while one was open for 9% of the time, Pallas kernels for 0%

profile of v2, /device:TPU:1, one launch (start us, length us, event | category | flops | bytes accessed | tf_op | source)
XLA Modules:
  0.0 141.5 jit_solution(2224526174526011051)
XLA Ops:
  1.9 3.3 %collective-permute-start = (f32[2,128]{1,0:T(2,128)S(1)}, f32[2,128]{1,0:T(2,128)S(1)}, u32[]{:S(2)}, u32[]{:S(2)}) collective-permute-start(f32[2,128]{1,0:T(2,128)S(1)} %multiply_reduce_fusion), channel_id=1, source_target_pairs={{0,1},{1,0},{2,3},{3,2},{4,5},{5,4},{6,7},{7,6},{8,9},{9,8},{10,11... | collective-permute-start | bytes 3080 | tf_op jit(solution)/shard_map/ppermute | solution.py:76
  7.9 2.0 %collective-permute-start.1 = (f32[2,128]{1,0:T(2,128)S(1)}, f32[2,128]{1,0:T(2,128)S(1)}, u32[]{:S(2)}, u32[]{:S(2)}) collective-permute-start(f32[2,128]{1,0:T(2,128)S(1)} %add.95), channel_id=1, source_target_pairs={{0,2},{2,0},{1,3},{3,1},{4,6},{6,4},{5,7},{7,5},{8,10},{10,8},{9,1... | collective-permute-start | bytes 3080 | tf_op jit(solution)/shard_map/ppermute | solution.py:76
  9.9 5.1 %fusion.10 = bf16[128,640]{1,0:T(8,128)(2,1)S(1)} fusion(bf16[640,5120]{1,0:T(8,128)(2,1)} %param.19, bf16[128,5120]{1,0:T(8,128)(2,1)S(1)} %copy-done.4, f32[5120]{0:T(1024)S(1)} %bitcast.62), kind=kOutput, calls=%fused_computation.14 | convolution fusion | flops 840908800 | bytes 8048640 | tf_op jit(solution)/shard_map/dot_general | solution.py:313
  16.4 1.7 %collective-permute-start.2 = (bf16[128,1280]{1,0:T(8,128)(2,1)S(1)}, bf16[128,1280]{1,0:T(8,128)(2,1)S(1)}, u32[]{:S(2)}, u32[]{:S(2)}) collective-permute-start(bf16[128,1280]{1,0:T(8,128)(2,1)S(1)} %pad_maximum_fusion.refs_0_.refs_9_), channel_id=1, source_target_pairs={{0,16},{16,32},{32,48},{48,64},{64,80},{80,96},{96,112},{112,0},{1... | collective-permute-start | bytes 983048 | tf_op jit(solution)/shard_map/ppermute | solution.py:68
  18.1 4.0 %collective-permute-start.6 = (bf16[128,1280]{1,0:T(8,128)(2,1)S(1)}, bf16[128,1280]{1,0:T(8,128)(2,1)S(1)}, u32[]{:S(2)}, u32[]{:S(2)}) collective-permute-start(bf16[128,1280]{1,0:T(8,128)(2,1)S(1)} %pad_maximum_fusion.refs_0_.refs_9_), channel_id=1, source_target_pairs={{0,112},{16,0},{32,16},{48,32},{64,48},{80,64},{96,80},{112,96},{1... | collective-permute-start | bytes 983048 | tf_op jit(solution)/shard_map/ppermute | solution.py:68
  26.0 3.3 %collective-permute-done.2.refs_1_.refs_10_ = bf16[128,1280]{1,0:T(8,128)(2,1)S(1)} collective-permute-done((bf16[128,1280]{1,0:T(8,128)(2,1)S(1)}, bf16[128,1280]{1,0:T(8,128)(2,1)S(1)}, u32[]{:S(2)}, u32[]{:S(2)}) %collective-permute-start.2) | collective-permute-done | bytes 327712 | tf_op jit(solution)/shard_map/ppermute | solution.py:68
  29.3 2.7 %collective-permute-start.7 = (bf16[128,1280]{1,0:T(8,128)(2,1)S(1)}, bf16[128,1280]{1,0:T(8,128)(2,1)S(1)}, u32[]{:S(2)}, u32[]{:S(2)}) collective-permute-start(bf16[128,1280]{1,0:T(8,128)(2,1)S(1)} %collective-permute-done.6.refs_8_.refs_17_), channel_id=1, source_target_pairs={{0,112},{16,0},{32,16},{48,32},{64,48},{80,64},{96,80},{112,96},{1... | collective-permute-start | bytes 983048 | tf_op jit(solution)/shard_map/ppermute | solution.py:68
  32.0 6.3 %collective-permute-done.3.refs_2_.refs_11_ = bf16[128,1280]{1,0:T(8,128)(2,1)S(1)} collective-permute-done((bf16[128,1280]{1,0:T(8,128)(2,1)S(1)}, bf16[128,1280]{1,0:T(8,128)(2,1)S(1)}, u32[]{:S(2)}, u32[]{:S(2)}) %collective-permute-start.3) | collective-permute-done | bytes 327712 | tf_op jit(solution)/shard_map/ppermute | solution.py:68
  38.3 2.7 %collective-permute-start.8 = (bf16[128,1280]{1,0:T(8,128)(2,1)S(1)}, bf16[128,1280]{1,0:T(8,128)(2,1)S(1)}, u32[]{:S(2)}, u32[]{:S(2)}) collective-permute-start(bf16[128,1280]{1,0:T(8,128)(2,1)S(1)} %collective-permute-done.7.refs_7_.refs_16_), channel_id=1, source_target_pairs={{0,112},{16,0},{32,16},{48,32},{64,48},{80,64},{96,80},{112,96},{1... | collective-permute-start | bytes 983048 | tf_op jit(solution)/shard_map/ppermute | solution.py:68
  43.2 1.6 %collective-permute-start.15 = (bf16[128,1280]{1,0:T(8,128)(2,1)}, bf16[128,1280]{1,0:T(8,128)(2,1)}, u32[]{:S(2)}, u32[]{:S(2)}) collective-permute-start(bf16[128,1280]{1,0:T(8,128)(2,1)} %slice.164), channel_id=1, source_target_pairs={{0,12},{4,0},{8,4},{12,8},{1,13},{5,1},{9,5},{13,9},{2,14},{6,2},{... | collective-permute-start | bytes 983048 | tf_op jit(solution)/shard_map/ppermute | solution.py:68
  44.8 1.6 %collective-permute-done.4.refs_3_.refs_12_ = bf16[128,1280]{1,0:T(8,128)(2,1)S(1)} collective-permute-done((bf16[128,1280]{1,0:T(8,128)(2,1)S(1)}, bf16[128,1280]{1,0:T(8,128)(2,1)S(1)}, u32[]{:S(2)}, u32[]{:S(2)}) %collective-permute-start.4) | collective-permute-done | bytes 327712 | tf_op jit(solution)/shard_map/ppermute | solution.py:68
  46.5 2.7 %collective-permute-start.9 = (bf16[64,1280]{1,0:T(8,128)(2,1)S(1)}, bf16[64,1280]{1,0:T(8,128)(2,1)}, u32[]{:S(2)}, u32[]{:S(2)}) collective-permute-start(bf16[64,1280]{1,0:T(8,128)(2,1)S(1)} %slice.162), channel_id=1, source_target_pairs={{0,112},{16,0},{32,16},{48,32},{64,48},{80,64},{96,80},{112,96},{1... | collective-permute-start | bytes 491528 | tf_op jit(solution)/shard_map/ppermute | solution.py:68
  49.9 2.3 %collective-permute-done.5.refs_4_.refs_13_ = bf16[64,1280]{1,0:T(8,128)(2,1)} collective-permute-done((bf16[64,1280]{1,0:T(8,128)(2,1)S(1)}, bf16[64,1280]{1,0:T(8,128)(2,1)}, u32[]{:S(2)}, u32[]{:S(2)}) %collective-permute-start.5) | collective-permute-done | bytes 163872 | tf_op jit(solution)/shard_map/ppermute | solution.py:68
  52.2 11.5 %block_stats.1 = f32[8,16,128]{2,1,0:T(8,128)} custom-call(s32[3]{0:T(128)} %pad_add_fusion.2.index_ref, bf16[128,1280]{1,0:T(8,128)(2,1)} %copy-done.6, bf16[128,1280]{1,0:T(8,128)(2,1)} %copy-done.18, bf16[128,1280]{1,0:T(8,128)(2,1)} %copy-done.20, bf16[128,1280]{1,0:T(8,128)(2,1)} %copy-done.16, ...), custom_call_target="tpu_custom_call" | custom-call | flops 10737418240 | bytes 8388608 | tf_op jit(solution)/shard_map/block_stats/pallas_call | solution.py:238
  65.4 1.8 %collective-permute-done.16 = f32[8,16,128]{2,1,0:T(8,128)S(1)} collective-permute-done((f32[8,16,128]{2,1,0:T(8,128)}, f32[8,16,128]{2,1,0:T(8,128)S(1)}, u32[]{:S(2)}, u32[]{:S(2)}) %collective-permute-start.16) | collective-permute-done | bytes 65568 | tf_op jit(solution)/shard_map/ppermute | solution.py:72
  68.1 2.6 %collective-permute-start.19 = (f32[8,16,128]{2,1,0:T(8,128)S(1)}, f32[8,16,128]{2,1,0:T(8,128)S(1)}, u32[]{:S(2)}, u32[]{:S(2)}) collective-permute-start(f32[8,16,128]{2,1,0:T(8,128)S(1)} %add_select_fusion.1), channel_id=1, source_target_pairs={{0,96},{16,112},{32,64},{48,80},{64,32},{80,48},{96,0},{112,16},{1... | collective-permute-start | bytes 196616 | tf_op jit(solution)/shard_map/ppermute | solution.py:72
  70.7 2.8 %collective-permute-start.18 = (f32[8,16,128]{2,1,0:T(8,128)S(1)}, f32[8,16,128]{2,1,0:T(8,128)S(1)}, u32[]{:S(2)}, u32[]{:S(2)}) collective-permute-start(f32[8,16,128]{2,1,0:T(8,128)S(1)} %add_select_fusion.1), channel_id=1, source_target_pairs={{0,64},{16,80},{32,96},{48,112},{64,0},{80,16},{96,32},{112,48},{1... | collective-permute-start | bytes 196616 | tf_op jit(solution)/shard_map/ppermute | solution.py:72
  73.9 3.8 %collective-permute-done.18 = f32[8,16,128]{2,1,0:T(8,128)S(1)} collective-permute-done((f32[8,16,128]{2,1,0:T(8,128)S(1)}, f32[8,16,128]{2,1,0:T(8,128)S(1)}, u32[]{:S(2)}, u32[]{:S(2)}) %collective-permute-start.18) | collective-permute-done | bytes 65568 | tf_op jit(solution)/shard_map/ppermute | solution.py:72
  78.7 16.4 %block_grads.1 = (bf16[128,640]{1,0:T(8,128)(2,1)}, bf16[128,640]{1,0:T(8,128)(2,1)}, bf16[128,640]{1,0:T(8,128)(2,1)}, bf16[128,640]{1,0:T(8,128)(2,1)}, bf16[1...) custom-call(s32[3]{0:T(128)} %pad_add_fusion.2.index_ref, ...), custom_call_target="tpu_custom_call" | custom-call | flops 13421772800 | bytes 16777216 | tf_op jit(solution)/shard_map/block_grads/pallas_call | solution.py:258
  95.2 5.2 %all-to-all-start = ((bf16[8,2,128,640]{3,2,1,0:T(8,128)(2,1)}), bf16[8,2,128,640]{3,2,1,0:T(8,128)(2,1)}, u32[]{:S(2)}, u32[]{:S(2)}) async-start(bf16[8,2,128,640]{3,2,1,0:T(8,128)(2,1)} %get-tuple-element.28), calls=%async_computation | async-start | bytes 5242880 | tf_op jit(solution)/shard_map/all_to_all | solution.py:334
  100.4 2.2 %collective-permute-start.24 = (bf16[128,640]{1,0:T(8,128)(2,1)S(1)}, bf16[128,640]{1,0:T(8,128)(2,1)S(1)}, u32[]{:S(2)}, u32[]{:S(2)}) collective-permute-start(bf16[128,640]{1,0:T(8,128)(2,1)S(1)} %copy-done.23), channel_id=1, source_target_pairs={{0,16},{16,32},{32,48},{48,64},{64,80},{80,96},{96,112},{112,0},{1... | collective-permute-start | bytes 491528 | tf_op jit(solution)/shard_map/ppermute | solution.py:68
  103.6 2.6 %collective-permute-start.21 = (bf16[64,640]{1,0:T(8,128)(2,1)S(1)}, bf16[64,640]{1,0:T(8,128)(2,1)S(1)}, u32[]{:S(2)}, u32[]{:S(2)}) collective-permute-start(bf16[64,640]{1,0:T(8,128)(2,1)S(1)} %get-tuple-element.43), channel_id=1, source_target_pairs={{0,96},{16,112},{32,0},{48,16},{64,32},{80,48},{96,64},{112,80},{1... | collective-permute-start | bytes 245768 | tf_op jit(solution)/shard_map/ppermute | solution.py:68
  106.3 2.1 %collective-permute-done.25 = bf16[64,640]{1,0:T(8,128)(2,1)S(1)} collective-permute-done((bf16[64,640]{1,0:T(8,128)(2,1)S(1)}, bf16[64,640]{1,0:T(8,128)(2,1)S(1)}, u32[]{:S(2)}, u32[]{:S(2)}) %collective-permute-start.25) | collective-permute-done | bytes 81952 | tf_op jit(solution)/shard_map/ppermute | solution.py:68
  108.8 1.9 %collective-permute-done.20 = bf16[128,640]{1,0:T(8,128)(2,1)S(1)} collective-permute-done((bf16[128,640]{1,0:T(8,128)(2,1)S(1)}, bf16[128,640]{1,0:T(8,128)(2,1)S(1)}, u32[]{:S(2)}, u32[]{:S(2)}) %collective-permute-start.20) | collective-permute-done | bytes 163872 | tf_op jit(solution)/shard_map/ppermute | solution.py:68
  110.8 2.5 %collective-permute-start.22 = (bf16[128,640]{1,0:T(8,128)(2,1)S(1)}, bf16[128,640]{1,0:T(8,128)(2,1)S(1)}, u32[]{:S(2)}, u32[]{:S(2)}) collective-permute-start(bf16[128,640]{1,0:T(8,128)(2,1)S(1)} %pad_add_fusion.1), channel_id=1, source_target_pairs={{0,112},{16,0},{32,16},{48,32},{64,48},{80,64},{96,80},{112,96},{1... | collective-permute-start | bytes 491528 | tf_op jit(solution)/shard_map/ppermute | solution.py:68
  113.3 2.7 %collective-permute-done.26 = bf16[128,640]{1,0:T(8,128)(2,1)S(1)} collective-permute-done((bf16[128,640]{1,0:T(8,128)(2,1)S(1)}, bf16[128,640]{1,0:T(8,128)(2,1)S(1)}, u32[]{:S(2)}, u32[]{:S(2)}) %collective-permute-start.26) | collective-permute-done | bytes 163872 | tf_op jit(solution)/shard_map/ppermute | solution.py:68
  116.2 3.9 %collective-permute-start.23 = (bf16[128,640]{1,0:T(8,128)(2,1)S(1)}, bf16[128,640]{1,0:T(8,128)(2,1)S(1)}, u32[]{:S(2)}, u32[]{:S(2)}) collective-permute-start(bf16[128,640]{1,0:T(8,128)(2,1)S(1)} %add.111), channel_id=1, source_target_pairs={{0,112},{16,0},{32,16},{48,32},{64,48},{80,64},{96,80},{112,96},{1... | collective-permute-start | bytes 491528 | tf_op jit(solution)/shard_map/ppermute | solution.py:68
  120.1 1.8 %collective-permute-done.27 = bf16[128,640]{1,0:T(8,128)(2,1)S(1)} collective-permute-done((bf16[128,640]{1,0:T(8,128)(2,1)S(1)}, bf16[128,640]{1,0:T(8,128)(2,1)S(1)}, u32[]{:S(2)}, u32[]{:S(2)}) %collective-permute-start.27) | collective-permute-done | bytes 163872 | tf_op jit(solution)/shard_map/ppermute | solution.py:68
  122.7 8.5 %all-to-all-done = bf16[8,2,128,640]{3,2,1,0:T(8,128)(2,1)} async-done(((bf16[8,2,128,640]{3,2,1,0:T(8,128)(2,1)}), bf16[8,2,128,640]{3,2,1,0:T(8,128)(2,1)}, u32[]{:S(2)}, u32[]{:S(2)}) %all-to-all-start) | async-done | bytes 2621472 | tf_op jit(solution)/shard_map/all_to_all | solution.py:334
  131.2 2.2 %convert_reduce_fusion = f32[2,128,640]{2,1,0:T(8,128)S(1)} fusion(bf16[8,2,128,640]{3,2,1,0:T(8,128)(2,1)} %all-to-all-done), kind=kLoop, calls=%fused_computation | loop fusion | flops 2457600 | bytes 3276800 | tf_op jit(solution)/shard_map/reduce_sum | solution.py:334
  134.2 2.5 %collective-permute-start.30 = (f32[2,128]{1,0:T(2,128)S(1)}, f32[2,128]{1,0:T(2,128)S(1)}, u32[]{:S(2)}, u32[]{:S(2)}) collective-permute-start(f32[2,128]{1,0:T(2,128)S(1)} %pad_maximum_fusion.7), channel_id=1, source_target_pairs={{0,3},{1,2},{2,1},{3,0},{4,7},{5,6},{6,5},{7,4},{8,11},{9,10},{10,... | collective-permute-start | bytes 3080 | tf_op jit(solution)/shard_map/ppermute | solution.py:82
  136.7 2.4 %collective-permute-start.29 = (f32[2,128]{1,0:T(2,128)S(1)}, f32[2,128]{1,0:T(2,128)S(1)}, u32[]{:S(2)}, u32[]{:S(2)}) collective-permute-start(f32[2,128]{1,0:T(2,128)S(1)} %pad_maximum_fusion.7), channel_id=1, source_target_pairs={{0,2},{1,3},{2,0},{3,1},{4,6},{5,7},{6,4},{7,5},{8,10},{9,11},{10,... | collective-permute-start | bytes 3080 | tf_op jit(solution)/shard_map/ppermute | solution.py:82
  (149 shorter events, 20.9 us)
Async XLA Ops:
  1.9 5.9 %collective-permute-start = (f32[2,128]{1,0:T(2,128)S(1)}, f32[2,128]{1,0:T(2,128)S(1)}, u32[]{:S(2)}, u32[]{:S(2)}) collective-permute-start(f32[2,128]{1,0:T(2,128)S(1)} %multiply_reduce_fusion), channel_id=1, source_target_pairs={{0,1},{1,0},{2,3},{3,2},{4,5},{5,4},{6,7},{7,6},{8,9},{9,8},{10,11... | collective-permute-start | bytes 3080 | tf_op jit(solution)/shard_map/ppermute | solution.py:76
  5.3 16.9 %collective-permute-start.11 = (bf16[128,640]{1,0:T(8,128)(2,1)}, bf16[128,640]{1,0:T(8,128)(2,1)}, u32[]{:S(2)}, u32[]{:S(2)}) collective-permute-start(bf16[128,640]{1,0:T(8,128)(2,1)} %param.16), channel_id=1, source_target_pairs={{0,128},{128,0},{1,129},{129,1},{2,130},{130,2},{3,131},{131,3},{4... | collective-permute-start | bytes 491528 | tf_op jit(solution)/shard_map/ppermute | solution.py:76
  7.9 7.1 %collective-permute-start.1 = (f32[2,128]{1,0:T(2,128)S(1)}, f32[2,128]{1,0:T(2,128)S(1)}, u32[]{:S(2)}, u32[]{:S(2)}) collective-permute-start(f32[2,128]{1,0:T(2,128)S(1)} %add.95), channel_id=1, source_target_pairs={{0,2},{2,0},{1,3},{3,1},{4,6},{6,4},{5,7},{7,5},{8,10},{10,8},{9,1... | collective-permute-start | bytes 3080 | tf_op jit(solution)/shard_map/ppermute | solution.py:76
  16.3 5.9 %collective-permute-start.10 = (bf16[128,640]{1,0:T(8,128)(2,1)S(1)}, bf16[128,640]{1,0:T(8,128)(2,1)S(1)}, u32[]{:S(2)}, u32[]{:S(2)}) collective-permute-start(bf16[128,640]{1,0:T(8,128)(2,1)S(1)} %fusion.9), channel_id=1, source_target_pairs={{0,128},{128,0},{1,129},{129,1},{2,130},{130,2},{3,131},{131,3},{4... | collective-permute-start | bytes 491528 | tf_op jit(solution)/shard_map/ppermute | solution.py:76
  16.4 12.9 %collective-permute-start.2 = (bf16[128,1280]{1,0:T(8,128)(2,1)S(1)}, bf16[128,1280]{1,0:T(8,128)(2,1)S(1)}, u32[]{:S(2)}, u32[]{:S(2)}) collective-permute-start(bf16[128,1280]{1,0:T(8,128)(2,1)S(1)} %pad_maximum_fusion.refs_0_.refs_9_), channel_id=1, source_target_pairs={{0,16},{16,32},{32,48},{48,64},{64,80},{80,96},{96,112},{112,0},{1... | collective-permute-start | bytes 983048 | tf_op jit(solution)/shard_map/ppermute | solution.py:68
  18.1 11.2 %collective-permute-start.6 = (bf16[128,1280]{1,0:T(8,128)(2,1)S(1)}, bf16[128,1280]{1,0:T(8,128)(2,1)S(1)}, u32[]{:S(2)}, u32[]{:S(2)}) collective-permute-start(bf16[128,1280]{1,0:T(8,128)(2,1)S(1)} %pad_maximum_fusion.refs_0_.refs_9_), channel_id=1, source_target_pairs={{0,112},{16,0},{32,16},{48,32},{64,48},{80,64},{96,80},{112,96},{1... | collective-permute-start | bytes 983048 | tf_op jit(solution)/shard_map/ppermute | solution.py:68
  23.1 17.8 %collective-permute-start.12 = (bf16[256,1280]{1,0:T(8,128)(2,1)S(1)}, bf16[256,1280]{1,0:T(8,128)(2,1)S(1)}, u32[]{:S(2)}, u32[]{:S(2)}) collective-permute-start(bf16[256,1280]{1,0:T(8,128)(2,1)S(1)} %maximum_maximum_fusion.refs_18_.refs_23_), channel_id=1, source_target_pairs={{0,4},{4,8},{8,12},{12,0},{1,5},{5,9},{9,13},{13,1},{2,6},{6,10},{... | collective-permute-start | bytes 1966088 | tf_op jit(solution)/shard_map/ppermute | solution.py:68
  24.5 17.9 %collective-permute-start.14 = (bf16[256,1280]{1,0:T(8,128)(2,1)S(1)}, bf16[256,1280]{1,0:T(8,128)(2,1)S(1)}, u32[]{:S(2)}, u32[]{:S(2)}) collective-permute-start(bf16[256,1280]{1,0:T(8,128)(2,1)S(1)} %maximum_maximum_fusion.refs_18_.refs_23_), channel_id=1, source_target_pairs={{0,12},{4,0},{8,4},{12,8},{1,13},{5,1},{9,5},{13,9},{2,14},{6,2},{... | collective-permute-start | bytes 1966088 | tf_op jit(solution)/shard_map/ppermute | solution.py:68
  29.3 9.0 %collective-permute-start.3 = (bf16[128,1280]{1,0:T(8,128)(2,1)S(1)}, bf16[128,1280]{1,0:T(8,128)(2,1)S(1)}, u32[]{:S(2)}, u32[]{:S(2)}) collective-permute-start(bf16[128,1280]{1,0:T(8,128)(2,1)S(1)} %collective-permute-done.2.refs_1_.refs_10_), channel_id=1, source_target_pairs={{0,16},{16,32},{32,48},{48,64},{64,80},{80,96},{96,112},{112,0},{1... | collective-permute-start | bytes 983048 | tf_op jit(solution)/shard_map/ppermute | solution.py:68
  29.3 9.0 %collective-permute-start.7 = (bf16[128,1280]{1,0:T(8,128)(2,1)S(1)}, bf16[128,1280]{1,0:T(8,128)(2,1)S(1)}, u32[]{:S(2)}, u32[]{:S(2)}) collective-permute-start(bf16[128,1280]{1,0:T(8,128)(2,1)S(1)} %collective-permute-done.6.refs_8_.refs_17_), channel_id=1, source_target_pairs={{0,112},{16,0},{32,16},{48,32},{64,48},{80,64},{96,80},{112,96},{1... | collective-permute-start | bytes 983048 | tf_op jit(solution)/shard_map/ppermute | solution.py:68
  38.3 8.1 %collective-permute-start.4 = (bf16[128,1280]{1,0:T(8,128)(2,1)S(1)}, bf16[128,1280]{1,0:T(8,128)(2,1)S(1)}, u32[]{:S(2)}, u32[]{:S(2)}) collective-permute-start(bf16[128,1280]{1,0:T(8,128)(2,1)S(1)} %collective-permute-done.3.refs_2_.refs_11_), channel_id=1, source_target_pairs={{0,16},{16,32},{32,48},{48,64},{64,80},{80,96},{96,112},{112,0},{1... | collective-permute-start | bytes 983048 | tf_op jit(solution)/shard_map/ppermute | solution.py:68
  38.3 8.2 %collective-permute-start.8 = (bf16[128,1280]{1,0:T(8,128)(2,1)S(1)}, bf16[128,1280]{1,0:T(8,128)(2,1)S(1)}, u32[]{:S(2)}, u32[]{:S(2)}) collective-permute-start(bf16[128,1280]{1,0:T(8,128)(2,1)S(1)} %collective-permute-done.7.refs_7_.refs_16_), channel_id=1, source_target_pairs={{0,112},{16,0},{32,16},{48,32},{64,48},{80,64},{96,80},{112,96},{1... | collective-permute-start | bytes 983048 | tf_op jit(solution)/shard_map/ppermute | solution.py:68
  41.0 11.2 %collective-permute-start.13 = (bf16[128,1280]{1,0:T(8,128)(2,1)S(1)}, bf16[128,1280]{1,0:T(8,128)(2,1)}, u32[]{:S(2)}, u32[]{:S(2)}) collective-permute-start(bf16[128,1280]{1,0:T(8,128)(2,1)S(1)} %slice.163), channel_id=1, source_target_pairs={{0,4},{4,8},{8,12},{12,0},{1,5},{5,9},{9,13},{13,1},{2,6},{6,10},{... | collective-permute-start | bytes 983048 | tf_op jit(solution)/shard_map/ppermute | solution.py:68
  43.2 9.0 %collective-permute-start.15 = (bf16[128,1280]{1,0:T(8,128)(2,1)}, bf16[128,1280]{1,0:T(8,128)(2,1)}, u32[]{:S(2)}, u32[]{:S(2)}) collective-permute-start(bf16[128,1280]{1,0:T(8,128)(2,1)} %slice.164), channel_id=1, source_target_pairs={{0,12},{4,0},{8,4},{12,8},{1,13},{5,1},{9,5},{13,9},{2,14},{6,2},{... | collective-permute-start | bytes 983048 | tf_op jit(solution)/shard_map/ppermute | solution.py:68
  46.4 5.8 %collective-permute-start.5 = (bf16[64,1280]{1,0:T(8,128)(2,1)S(1)}, bf16[64,1280]{1,0:T(8,128)(2,1)}, u32[]{:S(2)}, u32[]{:S(2)}) collective-permute-start(bf16[64,1280]{1,0:T(8,128)(2,1)S(1)} %slice.161), channel_id=1, source_target_pairs={{0,16},{16,32},{32,48},{48,64},{64,80},{80,96},{96,112},{112,0},{1... | collective-permute-start | bytes 491528 | tf_op jit(solution)/shard_map/ppermute | solution.py:68
  46.5 5.7 %collective-permute-start.9 = (bf16[64,1280]{1,0:T(8,128)(2,1)S(1)}, bf16[64,1280]{1,0:T(8,128)(2,1)}, u32[]{:S(2)}, u32[]{:S(2)}) collective-permute-start(bf16[64,1280]{1,0:T(8,128)(2,1)S(1)} %slice.162), channel_id=1, source_target_pairs={{0,112},{16,0},{32,16},{48,32},{64,48},{80,64},{96,80},{112,96},{1... | collective-permute-start | bytes 491528 | tf_op jit(solution)/shard_map/ppermute | solution.py:68
  63.7 3.4 %collective-permute-start.16 = (f32[8,16,128]{2,1,0:T(8,128)}, f32[8,16,128]{2,1,0:T(8,128)S(1)}, u32[]{:S(2)}, u32[]{:S(2)}) collective-permute-start(f32[8,16,128]{2,1,0:T(8,128)} %block_stats.1), channel_id=1, source_target_pairs={{0,16},{16,0},{32,48},{48,32},{64,80},{80,64},{96,112},{112,96},{1... | collective-permute-start | bytes 196616 | tf_op jit(solution)/shard_map/ppermute | solution.py:72
  68.1 5.8 %collective-permute-start.19 = (f32[8,16,128]{2,1,0:T(8,128)S(1)}, f32[8,16,128]{2,1,0:T(8,128)S(1)}, u32[]{:S(2)}, u32[]{:S(2)}) collective-permute-start(f32[8,16,128]{2,1,0:T(8,128)S(1)} %add_select_fusion.1), channel_id=1, source_target_pairs={{0,96},{16,112},{32,64},{48,80},{64,32},{80,48},{96,0},{112,16},{1... | collective-permute-start | bytes 196616 | tf_op jit(solution)/shard_map/ppermute | solution.py:72
  70.7 7.1 %collective-permute-start.18 = (f32[8,16,128]{2,1,0:T(8,128)S(1)}, f32[8,16,128]{2,1,0:T(8,128)S(1)}, u32[]{:S(2)}, u32[]{:S(2)}) collective-permute-start(f32[8,16,128]{2,1,0:T(8,128)S(1)} %add_select_fusion.1), channel_id=1, source_target_pairs={{0,64},{16,80},{32,96},{48,112},{64,0},{80,16},{96,32},{112,48},{1... | collective-permute-start | bytes 196616 | tf_op jit(solution)/shard_map/ppermute | solution.py:72
  73.5 4.3 %collective-permute-start.17 = (f32[8,16,128]{2,1,0:T(8,128)S(1)}, f32[8,16,128]{2,1,0:T(8,128)S(1)}, u32[]{:S(2)}, u32[]{:S(2)}) collective-permute-start(f32[8,16,128]{2,1,0:T(8,128)S(1)} %add_select_fusion.1), channel_id=1, source_target_pairs={{0,32},{16,48},{32,0},{48,16},{64,96},{80,112},{96,64},{112,80},{1... | collective-permute-start | bytes 196616 | tf_op jit(solution)/shard_map/ppermute | solution.py:72
  95.2 36.0 %all-to-all-start = ((bf16[8,2,128,640]{3,2,1,0:T(8,128)(2,1)}), bf16[8,2,128,640]{3,2,1,0:T(8,128)(2,1)}, u32[]{:S(2)}, u32[]{:S(2)}) async-start(bf16[8,2,128,640]{3,2,1,0:T(8,128)(2,1)} %get-tuple-element.28), calls=%async_computation | async-start | bytes 5242880 | tf_op jit(solution)/shard_map/all_to_all | solution.py:334
  100.4 8.0 %collective-permute-start.24 = (bf16[128,640]{1,0:T(8,128)(2,1)S(1)}, bf16[128,640]{1,0:T(8,128)(2,1)S(1)}, u32[]{:S(2)}, u32[]{:S(2)}) collective-permute-start(bf16[128,640]{1,0:T(8,128)(2,1)S(1)} %copy-done.23), channel_id=1, source_target_pairs={{0,16},{16,32},{32,48},{48,64},{64,80},{80,96},{96,112},{112,0},{1... | collective-permute-start | bytes 491528 | tf_op jit(solution)/shard_map/ppermute | solution.py:68
  102.6 5.8 %collective-permute-start.25 = (bf16[64,640]{1,0:T(8,128)(2,1)S(1)}, bf16[64,640]{1,0:T(8,128)(2,1)S(1)}, u32[]{:S(2)}, u32[]{:S(2)}) collective-permute-start(bf16[64,640]{1,0:T(8,128)(2,1)S(1)} %get-tuple-element.44), channel_id=1, source_target_pairs={{0,32},{16,48},{32,64},{48,80},{64,96},{80,112},{96,0},{112,16},{1... | collective-permute-start | bytes 245768 | tf_op jit(solution)/shard_map/ppermute | solution.py:68
  103.6 5.1 %collective-permute-start.21 = (bf16[64,640]{1,0:T(8,128)(2,1)S(1)}, bf16[64,640]{1,0:T(8,128)(2,1)S(1)}, u32[]{:S(2)}, u32[]{:S(2)}) collective-permute-start(bf16[64,640]{1,0:T(8,128)(2,1)S(1)} %get-tuple-element.43), channel_id=1, source_target_pairs={{0,96},{16,112},{32,0},{48,16},{64,32},{80,48},{96,64},{112,80},{1... | collective-permute-start | bytes 245768 | tf_op jit(solution)/shard_map/ppermute | solution.py:68
  106.3 4.5 %collective-permute-start.20 = (bf16[128,640]{1,0:T(8,128)(2,1)S(1)}, bf16[128,640]{1,0:T(8,128)(2,1)S(1)}, u32[]{:S(2)}, u32[]{:S(2)}) collective-permute-start(bf16[128,640]{1,0:T(8,128)(2,1)S(1)} %copy-done.22), channel_id=1, source_target_pairs={{0,112},{16,0},{32,16},{48,32},{64,48},{80,64},{96,80},{112,96},{1... | collective-permute-start | bytes 491528 | tf_op jit(solution)/shard_map/ppermute | solution.py:68
  108.4 7.6 %collective-permute-start.26 = (bf16[128,640]{1,0:T(8,128)(2,1)S(1)}, bf16[128,640]{1,0:T(8,128)(2,1)S(1)}, u32[]{:S(2)}, u32[]{:S(2)}) collective-permute-start(bf16[128,640]{1,0:T(8,128)(2,1)S(1)} %pad_add_fusion), channel_id=1, source_target_pairs={{0,16},{16,32},{32,48},{48,64},{64,80},{80,96},{96,112},{112,0},{1... | collective-permute-start | bytes 491528 | tf_op jit(solution)/shard_map/ppermute | solution.py:68
  110.8 5.4 %collective-permute-start.22 = (bf16[128,640]{1,0:T(8,128)(2,1)S(1)}, bf16[128,640]{1,0:T(8,128)(2,1)S(1)}, u32[]{:S(2)}, u32[]{:S(2)}) collective-permute-start(bf16[128,640]{1,0:T(8,128)(2,1)S(1)} %pad_add_fusion.1), channel_id=1, source_target_pairs={{0,112},{16,0},{32,16},{48,32},{64,48},{80,64},{96,80},{112,96},{1... | collective-permute-start | bytes 491528 | tf_op jit(solution)/shard_map/ppermute | solution.py:68
  116.1 5.9 %collective-permute-start.27 = (bf16[128,640]{1,0:T(8,128)(2,1)S(1)}, bf16[128,640]{1,0:T(8,128)(2,1)S(1)}, u32[]{:S(2)}, u32[]{:S(2)}) collective-permute-start(bf16[128,640]{1,0:T(8,128)(2,1)S(1)} %add.115), channel_id=1, source_target_pairs={{0,16},{16,32},{32,48},{48,64},{64,80},{80,96},{96,112},{112,0},{1... | collective-permute-start | bytes 491528 | tf_op jit(solution)/shard_map/ppermute | solution.py:68
  116.2 6.1 %collective-permute-start.23 = (bf16[128,640]{1,0:T(8,128)(2,1)S(1)}, bf16[128,640]{1,0:T(8,128)(2,1)S(1)}, u32[]{:S(2)}, u32[]{:S(2)}) collective-permute-start(bf16[128,640]{1,0:T(8,128)(2,1)S(1)} %add.111), channel_id=1, source_target_pairs={{0,112},{16,0},{32,16},{48,32},{64,48},{80,64},{96,80},{112,96},{1... | collective-permute-start | bytes 491528 | tf_op jit(solution)/shard_map/ppermute | solution.py:68
  134.2 5.5 %collective-permute-start.30 = (f32[2,128]{1,0:T(2,128)S(1)}, f32[2,128]{1,0:T(2,128)S(1)}, u32[]{:S(2)}, u32[]{:S(2)}) collective-permute-start(f32[2,128]{1,0:T(2,128)S(1)} %pad_maximum_fusion.7), channel_id=1, source_target_pairs={{0,3},{1,2},{2,1},{3,0},{4,7},{5,6},{6,5},{7,4},{8,11},{9,10},{10,... | collective-permute-start | bytes 3080 | tf_op jit(solution)/shard_map/ppermute | solution.py:82
  136.7 3.9 %collective-permute-start.29 = (f32[2,128]{1,0:T(2,128)S(1)}, f32[2,128]{1,0:T(2,128)S(1)}, u32[]{:S(2)}, u32[]{:S(2)}) collective-permute-start(f32[2,128]{1,0:T(2,128)S(1)} %pad_maximum_fusion.7), channel_id=1, source_target_pairs={{0,2},{1,3},{2,0},{3,1},{4,6},{5,7},{6,4},{7,5},{8,10},{9,11},{10,... | collective-permute-start | bytes 3080 | tf_op jit(solution)/shard_map/ppermute | solution.py:82
  139.1 1.5 %collective-permute-start.28 = (f32[2,128]{1,0:T(2,128)S(1)}, f32[2,128]{1,0:T(2,128)S(1)}, u32[]{:S(2)}, u32[]{:S(2)}) collective-permute-start(f32[2,128]{1,0:T(2,128)S(1)} %pad_maximum_fusion.7), channel_id=1, source_target_pairs={{0,1},{1,0},{2,3},{3,2},{4,5},{5,4},{6,7},{7,6},{8,9},{9,8},{10,11... | collective-permute-start | bytes 3080 | tf_op jit(solution)/shard_map/ppermute | solution.py:82
  (24 other events, 258.4 us)

commit v3 on v2

--- a/solution.py
+++ b/solution.py
@@ -70,6 +70,13 @@
 
 def swap(x, axis, mask):
     return lax.ppermute(x, axis, [(i, i ^ mask) for i in range(lax.axis_size(axis))])
+
+
+def other_pairs():
+    beside = [(i, (i + 1) % 8 if i % 2 else (i - 1) % 8) for i in range(8)]
+    beyond = [(i, (i + 2) % 8 if i % 2 else (i - 2) % 8) for i in range(8)]
+    opposite = [(i, (i - 5) % 8 if i % 2 else (i + 5) % 8) for i in range(8)]
+    return opposite, beyond, beside
 
 
 def flip(x, axis):
@@ -324,7 +331,7 @@
     places = list(range(8))
     stats = block_stats(index, places, queries, keys, heads)
     stats = merge([stats, swap(stats, "z", 1)], heads)
-    stats = merge([stats] + [swap(stats, "z", mask) for mask in (2, 4, 6)], heads)
+    stats = merge([stats] + [lax.ppermute(stats, "z", perm) for perm in other_pairs()], heads)
     top, total, weight = (stats[:, kind * heads : (kind + 1) * heads] for kind in range(3))
     rest = jnp.zeros((8, 16 - 2 * heads, 128), f32)
     totals = jnp.concatenate([top + jnp.log2(total), weight / total, rest], axis=1)

time: 142 us -> 142 us (level)
    ppermute x4 -> x1, starting transfers between devices: 5.84 us -> 0.09 us  [swap(): lax.ppermute(x, axis, [(i, i ^ mask) for i in range(lax.axis_size(axis))])]
    ppermute x0 -> x3, starting transfers between devices: none -> 5.08 us  [shards(): lax.ppermute(stats, 'z', perm)]
    ppermute x0 -> x3, waiting for transfers between devices: none -> 3.88 us  [shards(): lax.ppermute(stats, 'z', perm)]
    ppermute x4 -> x1, waiting for transfers between devices: 5.6 us -> 1.77 us  [swap(): lax.ppermute(x, axis, [(i, i ^ mask) for i in range(lax.axis_size(axis))])]
where the time goes in v3:
time: 142 us; the launch traced here: 141 us
  starting transfers between devices  53.7 us (38%)
  waiting for transfers between devices  36.8 us (26%)
  Pallas kernels  28 us (20%)
  other arithmetic  10.4 us (7%)
  matrix products  5.72 us (4%)
  local copies, waits for them, and re-layouts  4.41 us (3%)
  between operations  1.84 us (1%)
    ppermute x20, starting transfers between devices, shift(): lax.ppermute(x, axis, [(i, (i + distance) % size) for i in range(size)])  33.2 us
    ppermute x20, waiting for transfers between devices, shift(): lax.ppermute(x, axis, [(i, (i + distance) % size) for i in range(size)])  21.4 us
    pallas_call x1, Pallas kernels, block_grads(): pl.pallas_call(functools.partial(grads_kernel, places, counts, heads), gr...  16.4 us
    pallas_call x1, Pallas kernels, block_stats(): pl.pallas_call(functools.partial(stats_kernel, places, counts, heads), gr...  11.5 us
    all_to_all x1, waiting for transfers between devices, shards(): lax.all_to_all(dkv, ('xl', 'y'), 0, 0, tiled=True).astype(f32)  8.89 us
    ppermute x4, starting transfers between devices, flip(): return lax.ppermute(x, axis, [(0, 1), (1, 0)])  5.45 us
    dot_general x1, matrix products, shards(): lax.dot_general(gated_cot, out_weight, NT, preferred_element_type=f32)  5.08 us
    ppermute x3, starting transfers between devices, shards(): lax.ppermute(stats, 'z', perm)  5.08 us
  transfers between devices with their start and end apart: 32, of which 14 were waited for; matrix products, arithmetic and copies ran while one was open for 9% of the time, Pallas kernels for 0%

profile of v3, /device:TPU:1, one launch (start us, length us, event | category | flops | bytes accessed | tf_op | source)
XLA Modules:
  0.0 140.8 jit_solution(2270676829909192771)
XLA Ops:
  1.9 3.3 %collective-permute-start = (f32[2,128]{1,0:T(2,128)S(1)}, f32[2,128]{1,0:T(2,128)S(1)}, u32[]{:S(2)}, u32[]{:S(2)}) collective-permute-start(f32[2,128]{1,0:T(2,128)S(1)} %multiply_reduce_fusion), channel_id=1, source_target_pairs={{0,1},{1,0},{2,3},{3,2},{4,5},{5,4},{6,7},{7,6},{8,9},{9,8},{10,11... | collective-permute-start | bytes 3080 | tf_op jit(solution)/shard_map/ppermute | solution.py:83
  7.9 2.0 %collective-permute-start.1 = (f32[2,128]{1,0:T(2,128)S(1)}, f32[2,128]{1,0:T(2,128)S(1)}, u32[]{:S(2)}, u32[]{:S(2)}) collective-permute-start(f32[2,128]{1,0:T(2,128)S(1)} %add.95), channel_id=1, source_target_pairs={{0,2},{2,0},{1,3},{3,1},{4,6},{6,4},{5,7},{7,5},{8,10},{10,8},{9,1... | collective-permute-start | bytes 3080 | tf_op jit(solution)/shard_map/ppermute | solution.py:83
  9.9 5.1 %fusion.10 = bf16[128,640]{1,0:T(8,128)(2,1)S(1)} fusion(bf16[640,5120]{1,0:T(8,128)(2,1)} %param.19, bf16[128,5120]{1,0:T(8,128)(2,1)S(1)} %copy-done.4, f32[5120]{0:T(1024)S(1)} %bitcast.62), kind=kOutput, calls=%fused_computation.14 | convolution fusion | flops 840908800 | bytes 8048640 | tf_op jit(solution)/shard_map/dot_general | solution.py:320
  16.4 1.7 %collective-permute-start.2 = (bf16[128,1280]{1,0:T(8,128)(2,1)S(1)}, bf16[128,1280]{1,0:T(8,128)(2,1)S(1)}, u32[]{:S(2)}, u32[]{:S(2)}) collective-permute-start(bf16[128,1280]{1,0:T(8,128)(2,1)S(1)} %pad_maximum_fusion.refs_0_.refs_9_), channel_id=1, source_target_pairs={{0,16},{16,32},{32,48},{48,64},{64,80},{80,96},{96,112},{112,0},{1... | collective-permute-start | bytes 983048 | tf_op jit(solution)/shard_map/ppermute | solution.py:68
  18.1 4.0 %collective-permute-start.6 = (bf16[128,1280]{1,0:T(8,128)(2,1)S(1)}, bf16[128,1280]{1,0:T(8,128)(2,1)S(1)}, u32[]{:S(2)}, u32[]{:S(2)}) collective-permute-start(bf16[128,1280]{1,0:T(8,128)(2,1)S(1)} %pad_maximum_fusion.refs_0_.refs_9_), channel_id=1, source_target_pairs={{0,112},{16,0},{32,16},{48,32},{64,48},{80,64},{96,80},{112,96},{1... | collective-permute-start | bytes 983048 | tf_op jit(solution)/shard_map/ppermute | solution.py:68
  26.0 3.3 %collective-permute-done.2.refs_1_.refs_10_ = bf16[128,1280]{1,0:T(8,128)(2,1)S(1)} collective-permute-done((bf16[128,1280]{1,0:T(8,128)(2,1)S(1)}, bf16[128,1280]{1,0:T(8,128)(2,1)S(1)}, u32[]{:S(2)}, u32[]{:S(2)}) %collective-permute-start.2) | collective-permute-done | bytes 327712 | tf_op jit(solution)/shard_map/ppermute | solution.py:68
  29.3 2.7 %collective-permute-start.7 = (bf16[128,1280]{1,0:T(8,128)(2,1)S(1)}, bf16[128,1280]{1,0:T(8,128)(2,1)S(1)}, u32[]{:S(2)}, u32[]{:S(2)}) collective-permute-start(bf16[128,1280]{1,0:T(8,128)(2,1)S(1)} %collective-permute-done.6.refs_8_.refs_17_), channel_id=1, source_target_pairs={{0,112},{16,0},{32,16},{48,32},{64,48},{80,64},{96,80},{112,96},{1... | collective-permute-start | bytes 983048 | tf_op jit(solution)/shard_map/ppermute | solution.py:68
  32.0 6.3 %collective-permute-done.3.refs_2_.refs_11_ = bf16[128,1280]{1,0:T(8,128)(2,1)S(1)} collective-permute-done((bf16[128,1280]{1,0:T(8,128)(2,1)S(1)}, bf16[128,1280]{1,0:T(8,128)(2,1)S(1)}, u32[]{:S(2)}, u32[]{:S(2)}) %collective-permute-start.3) | collective-permute-done | bytes 327712 | tf_op jit(solution)/shard_map/ppermute | solution.py:68
  38.3 2.7 %collective-permute-start.8 = (bf16[128,1280]{1,0:T(8,128)(2,1)S(1)}, bf16[128,1280]{1,0:T(8,128)(2,1)S(1)}, u32[]{:S(2)}, u32[]{:S(2)}) collective-permute-start(bf16[128,1280]{1,0:T(8,128)(2,1)S(1)} %collective-permute-done.7.refs_7_.refs_16_), channel_id=1, source_target_pairs={{0,112},{16,0},{32,16},{48,32},{64,48},{80,64},{96,80},{112,96},{1... | collective-permute-start | bytes 983048 | tf_op jit(solution)/shard_map/ppermute | solution.py:68
  43.2 1.6 %collective-permute-start.15 = (bf16[128,1280]{1,0:T(8,128)(2,1)}, bf16[128,1280]{1,0:T(8,128)(2,1)}, u32[]{:S(2)}, u32[]{:S(2)}) collective-permute-start(bf16[128,1280]{1,0:T(8,128)(2,1)} %slice.164), channel_id=1, source_target_pairs={{0,12},{4,0},{8,4},{12,8},{1,13},{5,1},{9,5},{13,9},{2,14},{6,2},{... | collective-permute-start | bytes 983048 | tf_op jit(solution)/shard_map/ppermute | solution.py:68
  44.8 1.6 %collective-permute-done.4.refs_3_.refs_12_ = bf16[128,1280]{1,0:T(8,128)(2,1)S(1)} collective-permute-done((bf16[128,1280]{1,0:T(8,128)(2,1)S(1)}, bf16[128,1280]{1,0:T(8,128)(2,1)S(1)}, u32[]{:S(2)}, u32[]{:S(2)}) %collective-permute-start.4) | collective-permute-done | bytes 327712 | tf_op jit(solution)/shard_map/ppermute | solution.py:68
  46.5 2.7 %collective-permute-start.9 = (bf16[64,1280]{1,0:T(8,128)(2,1)S(1)}, bf16[64,1280]{1,0:T(8,128)(2,1)}, u32[]{:S(2)}, u32[]{:S(2)}) collective-permute-start(bf16[64,1280]{1,0:T(8,128)(2,1)S(1)} %slice.162), channel_id=1, source_target_pairs={{0,112},{16,0},{32,16},{48,32},{64,48},{80,64},{96,80},{112,96},{1... | collective-permute-start | bytes 491528 | tf_op jit(solution)/shard_map/ppermute | solution.py:68
  49.9 2.3 %collective-permute-done.5.refs_4_.refs_13_ = bf16[64,1280]{1,0:T(8,128)(2,1)} collective-permute-done((bf16[64,1280]{1,0:T(8,128)(2,1)S(1)}, bf16[64,1280]{1,0:T(8,128)(2,1)}, u32[]{:S(2)}, u32[]{:S(2)}) %collective-permute-start.5) | collective-permute-done | bytes 163872 | tf_op jit(solution)/shard_map/ppermute | solution.py:68
  52.2 11.5 %block_stats.1 = f32[8,16,128]{2,1,0:T(8,128)} custom-call(s32[3]{0:T(128)} %pad_add_fusion.2.index_ref, bf16[128,1280]{1,0:T(8,128)(2,1)} %copy-done.6, bf16[128,1280]{1,0:T(8,128)(2,1)} %copy-done.18, bf16[128,1280]{1,0:T(8,128)(2,1)} %copy-done.20, bf16[128,1280]{1,0:T(8,128)(2,1)} %copy-done.16, ...), custom_call_target="tpu_custom_call" | custom-call | flops 10737418240 | bytes 8388608 | tf_op jit(solution)/shard_map/block_stats/pallas_call | solution.py:245
  65.4 1.8 %collective-permute-done.16 = f32[8,16,128]{2,1,0:T(8,128)S(1)} collective-permute-done((f32[8,16,128]{2,1,0:T(8,128)}, f32[8,16,128]{2,1,0:T(8,128)S(1)}, u32[]{:S(2)}, u32[]{:S(2)}) %collective-permute-start.16) | collective-permute-done | bytes 65568 | tf_op jit(solution)/shard_map/ppermute | solution.py:72
  68.1 2.9 %collective-permute-start.19 = (f32[8,16,128]{2,1,0:T(8,128)S(1)}, f32[8,16,128]{2,1,0:T(8,128)S(1)}, u32[]{:S(2)}, u32[]{:S(2)}) collective-permute-start(f32[8,16,128]{2,1,0:T(8,128)S(1)} %add_select_fusion.1), channel_id=1, source_target_pairs={{0,112},{16,32},{32,16},{48,64},{64,48},{80,96},{96,80},{112,0},{1... | collective-permute-start | bytes 196616 | tf_op jit(solution)/shard_map/ppermute | solution.py:334
  71.0 2.2 %collective-permute-start.17 = (f32[8,16,128]{2,1,0:T(8,128)S(1)}, f32[8,16,128]{2,1,0:T(8,128)S(1)}, u32[]{:S(2)}, u32[]{:S(2)}) collective-permute-start(f32[8,16,128]{2,1,0:T(8,128)S(1)} %add_select_fusion.1), channel_id=1, source_target_pairs={{0,80},{16,64},{32,112},{48,96},{64,16},{80,0},{96,48},{112,32},{1... | collective-permute-start | bytes 196616 | tf_op jit(solution)/shard_map/ppermute | solution.py:334
  73.3 1.7 %collective-permute-done.18 = f32[8,16,128]{2,1,0:T(8,128)S(1)} collective-permute-done((f32[8,16,128]{2,1,0:T(8,128)S(1)}, f32[8,16,128]{2,1,0:T(8,128)S(1)}, u32[]{:S(2)}, u32[]{:S(2)}) %collective-permute-start.18) | collective-permute-done | bytes 65568 | tf_op jit(solution)/shard_map/ppermute | solution.py:334
  75.0 2.1 %collective-permute-done.17 = f32[8,16,128]{2,1,0:T(8,128)S(1)} collective-permute-done((f32[8,16,128]{2,1,0:T(8,128)S(1)}, f32[8,16,128]{2,1,0:T(8,128)S(1)}, u32[]{:S(2)}, u32[]{:S(2)}) %collective-permute-start.17) | collective-permute-done | bytes 65568 | tf_op jit(solution)/shard_map/ppermute | solution.py:334
  78.0 16.4 %block_grads.1 = (bf16[128,640]{1,0:T(8,128)(2,1)}, bf16[128,640]{1,0:T(8,128)(2,1)}, bf16[128,640]{1,0:T(8,128)(2,1)}, bf16[128,640]{1,0:T(8,128)(2,1)}, bf16[1...) custom-call(s32[3]{0:T(128)} %pad_add_fusion.2.index_ref, ...), custom_call_target="tpu_custom_call" | custom-call | flops 13421772800 | bytes 16777216 | tf_op jit(solution)/shard_map/block_grads/pallas_call | solution.py:265
  94.5 5.1 %all-to-all-start = ((bf16[8,2,128,640]{3,2,1,0:T(8,128)(2,1)}), bf16[8,2,128,640]{3,2,1,0:T(8,128)(2,1)}, u32[]{:S(2)}, u32[]{:S(2)}) async-start(bf16[8,2,128,640]{3,2,1,0:T(8,128)(2,1)} %get-tuple-element.28), calls=%async_computation | async-start | bytes 5242880 | tf_op jit(solution)/shard_map/all_to_all | solution.py:341
  100.5 2.1 %collective-permute-start.25 = (bf16[64,640]{1,0:T(8,128)(2,1)S(1)}, bf16[64,640]{1,0:T(8,128)(2,1)S(1)}, u32[]{:S(2)}, u32[]{:S(2)}) collective-permute-start(bf16[64,640]{1,0:T(8,128)(2,1)S(1)} %get-tuple-element.44), channel_id=1, source_target_pairs={{0,32},{16,48},{32,64},{48,80},{64,96},{80,112},{96,0},{112,16},{1... | collective-permute-start | bytes 245768 | tf_op jit(solution)/shard_map/ppermute | solution.py:68
  105.3 1.6 %collective-permute-done.25 = bf16[64,640]{1,0:T(8,128)(2,1)S(1)} collective-permute-done((bf16[64,640]{1,0:T(8,128)(2,1)S(1)}, bf16[64,640]{1,0:T(8,128)(2,1)S(1)}, u32[]{:S(2)}, u32[]{:S(2)}) %collective-permute-start.25) | collective-permute-done | bytes 81952 | tf_op jit(solution)/shard_map/ppermute | solution.py:68
  107.0 2.1 %collective-permute-start.26 = (bf16[128,640]{1,0:T(8,128)(2,1)S(1)}, bf16[128,640]{1,0:T(8,128)(2,1)S(1)}, u32[]{:S(2)}, u32[]{:S(2)}) collective-permute-start(bf16[128,640]{1,0:T(8,128)(2,1)S(1)} %pad_add_fusion), channel_id=1, source_target_pairs={{0,16},{16,32},{32,48},{48,64},{64,80},{80,96},{96,112},{112,0},{1... | collective-permute-start | bytes 491528 | tf_op jit(solution)/shard_map/ppermute | solution.py:68
  111.7 1.6 %collective-permute-done.26 = bf16[128,640]{1,0:T(8,128)(2,1)S(1)} collective-permute-done((bf16[128,640]{1,0:T(8,128)(2,1)S(1)}, bf16[128,640]{1,0:T(8,128)(2,1)S(1)}, u32[]{:S(2)}, u32[]{:S(2)}) %collective-permute-start.26) | collective-permute-done | bytes 163872 | tf_op jit(solution)/shard_map/ppermute | solution.py:68
  113.4 2.0 %collective-permute-start.27 = (bf16[128,640]{1,0:T(8,128)(2,1)S(1)}, bf16[128,640]{1,0:T(8,128)(2,1)S(1)}, u32[]{:S(2)}, u32[]{:S(2)}) collective-permute-start(bf16[128,640]{1,0:T(8,128)(2,1)S(1)} %add.115), channel_id=1, source_target_pairs={{0,16},{16,32},{32,48},{48,64},{64,80},{80,96},{96,112},{112,0},{1... | collective-permute-start | bytes 491528 | tf_op jit(solution)/shard_map/ppermute | solution.py:68
  115.5 2.2 %collective-permute-start.23 = (bf16[128,640]{1,0:T(8,128)(2,1)S(1)}, bf16[128,640]{1,0:T(8,128)(2,1)S(1)}, u32[]{:S(2)}, u32[]{:S(2)}) collective-permute-start(bf16[128,640]{1,0:T(8,128)(2,1)S(1)} %add.111), channel_id=1, source_target_pairs={{0,112},{16,0},{32,16},{48,32},{64,48},{80,64},{96,80},{112,96},{1... | collective-permute-start | bytes 491528 | tf_op jit(solution)/shard_map/ppermute | solution.py:68
  119.2 2.0 %collective-permute-done.23 = bf16[128,640]{1,0:T(8,128)(2,1)S(1)} collective-permute-done((bf16[128,640]{1,0:T(8,128)(2,1)S(1)}, bf16[128,640]{1,0:T(8,128)(2,1)S(1)}, u32[]{:S(2)}, u32[]{:S(2)}) %collective-permute-start.23) | collective-permute-done | bytes 163872 | tf_op jit(solution)/shard_map/ppermute | solution.py:68
  121.6 8.9 %all-to-all-done = bf16[8,2,128,640]{3,2,1,0:T(8,128)(2,1)} async-done(((bf16[8,2,128,640]{3,2,1,0:T(8,128)(2,1)}), bf16[8,2,128,640]{3,2,1,0:T(8,128)(2,1)}, u32[]{:S(2)}, u32[]{:S(2)}) %all-to-all-start) | async-done | bytes 2621472 | tf_op jit(solution)/shard_map/all_to_all | solution.py:341
  130.5 2.2 %convert_reduce_fusion = f32[2,128,640]{2,1,0:T(8,128)S(1)} fusion(bf16[8,2,128,640]{3,2,1,0:T(8,128)(2,1)} %all-to-all-done), kind=kLoop, calls=%fused_computation | loop fusion | flops 2457600 | bytes 3276800 | tf_op jit(solution)/shard_map/reduce_sum | solution.py:341
  133.5 2.4 %collective-permute-start.30 = (f32[2,128]{1,0:T(2,128)S(1)}, f32[2,128]{1,0:T(2,128)S(1)}, u32[]{:S(2)}, u32[]{:S(2)}) collective-permute-start(f32[2,128]{1,0:T(2,128)S(1)} %pad_maximum_fusion.7), channel_id=1, source_target_pairs={{0,3},{1,2},{2,1},{3,0},{4,7},{5,6},{6,5},{7,4},{8,11},{9,10},{10,... | collective-permute-start | bytes 3080 | tf_op jit(solution)/shard_map/ppermute | solution.py:89
  135.9 2.4 %collective-permute-start.29 = (f32[2,128]{1,0:T(2,128)S(1)}, f32[2,128]{1,0:T(2,128)S(1)}, u32[]{:S(2)}, u32[]{:S(2)}) collective-permute-start(f32[2,128]{1,0:T(2,128)S(1)} %pad_maximum_fusion.7), channel_id=1, source_target_pairs={{0,2},{1,3},{2,0},{3,1},{4,6},{5,7},{6,4},{7,5},{8,10},{9,11},{10,... | collective-permute-start | bytes 3080 | tf_op jit(solution)/shard_map/ppermute | solution.py:89
  (149 shorter events, 26.4 us)
Async XLA Ops:
  1.9 5.9 %collective-permute-start = (f32[2,128]{1,0:T(2,128)S(1)}, f32[2,128]{1,0:T(2,128)S(1)}, u32[]{:S(2)}, u32[]{:S(2)}) collective-permute-start(f32[2,128]{1,0:T(2,128)S(1)} %multiply_reduce_fusion), channel_id=1, source_target_pairs={{0,1},{1,0},{2,3},{3,2},{4,5},{5,4},{6,7},{7,6},{8,9},{9,8},{10,11... | collective-permute-start | bytes 3080 | tf_op jit(solution)/shard_map/ppermute | solution.py:83
  5.3 16.9 %collective-permute-start.11 = (bf16[128,640]{1,0:T(8,128)(2,1)}, bf16[128,640]{1,0:T(8,128)(2,1)}, u32[]{:S(2)}, u32[]{:S(2)}) collective-permute-start(bf16[128,640]{1,0:T(8,128)(2,1)} %param.16), channel_id=1, source_target_pairs={{0,128},{128,0},{1,129},{129,1},{2,130},{130,2},{3,131},{131,3},{4... | collective-permute-start | bytes 491528 | tf_op jit(solution)/shard_map/ppermute | solution.py:83
  7.9 7.1 %collective-permute-start.1 = (f32[2,128]{1,0:T(2,128)S(1)}, f32[2,128]{1,0:T(2,128)S(1)}, u32[]{:S(2)}, u32[]{:S(2)}) collective-permute-start(f32[2,128]{1,0:T(2,128)S(1)} %add.95), channel_id=1, source_target_pairs={{0,2},{2,0},{1,3},{3,1},{4,6},{6,4},{5,7},{7,5},{8,10},{10,8},{9,1... | collective-permute-start | bytes 3080 | tf_op jit(solution)/shard_map/ppermute | solution.py:83
  16.3 5.9 %collective-permute-start.10 = (bf16[128,640]{1,0:T(8,128)(2,1)S(1)}, bf16[128,640]{1,0:T(8,128)(2,1)S(1)}, u32[]{:S(2)}, u32[]{:S(2)}) collective-permute-start(bf16[128,640]{1,0:T(8,128)(2,1)S(1)} %fusion.9), channel_id=1, source_target_pairs={{0,128},{128,0},{1,129},{129,1},{2,130},{130,2},{3,131},{131,3},{4... | collective-permute-start | bytes 491528 | tf_op jit(solution)/shard_map/ppermute | solution.py:83
  16.4 12.9 %collective-permute-start.2 = (bf16[128,1280]{1,0:T(8,128)(2,1)S(1)}, bf16[128,1280]{1,0:T(8,128)(2,1)S(1)}, u32[]{:S(2)}, u32[]{:S(2)}) collective-permute-start(bf16[128,1280]{1,0:T(8,128)(2,1)S(1)} %pad_maximum_fusion.refs_0_.refs_9_), channel_id=1, source_target_pairs={{0,16},{16,32},{32,48},{48,64},{64,80},{80,96},{96,112},{112,0},{1... | collective-permute-start | bytes 983048 | tf_op jit(solution)/shard_map/ppermute | solution.py:68
  18.1 11.2 %collective-permute-start.6 = (bf16[128,1280]{1,0:T(8,128)(2,1)S(1)}, bf16[128,1280]{1,0:T(8,128)(2,1)S(1)}, u32[]{:S(2)}, u32[]{:S(2)}) collective-permute-start(bf16[128,1280]{1,0:T(8,128)(2,1)S(1)} %pad_maximum_fusion.refs_0_.refs_9_), channel_id=1, source_target_pairs={{0,112},{16,0},{32,16},{48,32},{64,48},{80,64},{96,80},{112,96},{1... | collective-permute-start | bytes 983048 | tf_op jit(solution)/shard_map/ppermute | solution.py:68
  23.1 17.8 %collective-permute-start.12 = (bf16[256,1280]{1,0:T(8,128)(2,1)S(1)}, bf16[256,1280]{1,0:T(8,128)(2,1)S(1)}, u32[]{:S(2)}, u32[]{:S(2)}) collective-permute-start(bf16[256,1280]{1,0:T(8,128)(2,1)S(1)} %maximum_maximum_fusion.refs_18_.refs_23_), channel_id=1, source_target_pairs={{0,4},{4,8},{8,12},{12,0},{1,5},{5,9},{9,13},{13,1},{2,6},{6,10},{... | collective-permute-start | bytes 1966088 | tf_op jit(solution)/shard_map/ppermute | solution.py:68
  24.5 17.9 %collective-permute-start.14 = (bf16[256,1280]{1,0:T(8,128)(2,1)S(1)}, bf16[256,1280]{1,0:T(8,128)(2,1)S(1)}, u32[]{:S(2)}, u32[]{:S(2)}) collective-permute-start(bf16[256,1280]{1,0:T(8,128)(2,1)S(1)} %maximum_maximum_fusion.refs_18_.refs_23_), channel_id=1, source_target_pairs={{0,12},{4,0},{8,4},{12,8},{1,13},{5,1},{9,5},{13,9},{2,14},{6,2},{... | collective-permute-start | bytes 1966088 | tf_op jit(solution)/shard_map/ppermute | solution.py:68
  29.3 9.0 %collective-permute-start.3 = (bf16[128,1280]{1,0:T(8,128)(2,1)S(1)}, bf16[128,1280]{1,0:T(8,128)(2,1)S(1)}, u32[]{:S(2)}, u32[]{:S(2)}) collective-permute-start(bf16[128,1280]{1,0:T(8,128)(2,1)S(1)} %collective-permute-done.2.refs_1_.refs_10_), channel_id=1, source_target_pairs={{0,16},{16,32},{32,48},{48,64},{64,80},{80,96},{96,112},{112,0},{1... | collective-permute-start | bytes 983048 | tf_op jit(solution)/shard_map/ppermute | solution.py:68
  29.3 9.0 %collective-permute-start.7 = (bf16[128,1280]{1,0:T(8,128)(2,1)S(1)}, bf16[128,1280]{1,0:T(8,128)(2,1)S(1)}, u32[]{:S(2)}, u32[]{:S(2)}) collective-permute-start(bf16[128,1280]{1,0:T(8,128)(2,1)S(1)} %collective-permute-done.6.refs_8_.refs_17_), channel_id=1, source_target_pairs={{0,112},{16,0},{32,16},{48,32},{64,48},{80,64},{96,80},{112,96},{1... | collective-permute-start | bytes 983048 | tf_op jit(solution)/shard_map/ppermute | solution.py:68
  38.3 8.1 %collective-permute-start.4 = (bf16[128,1280]{1,0:T(8,128)(2,1)S(1)}, bf16[128,1280]{1,0:T(8,128)(2,1)S(1)}, u32[]{:S(2)}, u32[]{:S(2)}) collective-permute-start(bf16[128,1280]{1,0:T(8,128)(2,1)S(1)} %collective-permute-done.3.refs_2_.refs_11_), channel_id=1, source_target_pairs={{0,16},{16,32},{32,48},{48,64},{64,80},{80,96},{96,112},{112,0},{1... | collective-permute-start | bytes 983048 | tf_op jit(solution)/shard_map/ppermute | solution.py:68
  38.3 8.2 %collective-permute-start.8 = (bf16[128,1280]{1,0:T(8,128)(2,1)S(1)}, bf16[128,1280]{1,0:T(8,128)(2,1)S(1)}, u32[]{:S(2)}, u32[]{:S(2)}) collective-permute-start(bf16[128,1280]{1,0:T(8,128)(2,1)S(1)} %collective-permute-done.7.refs_7_.refs_16_), channel_id=1, source_target_pairs={{0,112},{16,0},{32,16},{48,32},{64,48},{80,64},{96,80},{112,96},{1... | collective-permute-start | bytes 983048 | tf_op jit(solution)/shard_map/ppermute | solution.py:68
  41.0 11.2 %collective-permute-start.13 = (bf16[128,1280]{1,0:T(8,128)(2,1)S(1)}, bf16[128,1280]{1,0:T(8,128)(2,1)}, u32[]{:S(2)}, u32[]{:S(2)}) collective-permute-start(bf16[128,1280]{1,0:T(8,128)(2,1)S(1)} %slice.163), channel_id=1, source_target_pairs={{0,4},{4,8},{8,12},{12,0},{1,5},{5,9},{9,13},{13,1},{2,6},{6,10},{... | collective-permute-start | bytes 983048 | tf_op jit(solution)/shard_map/ppermute | solution.py:68
  43.2 9.0 %collective-permute-start.15 = (bf16[128,1280]{1,0:T(8,128)(2,1)}, bf16[128,1280]{1,0:T(8,128)(2,1)}, u32[]{:S(2)}, u32[]{:S(2)}) collective-permute-start(bf16[128,1280]{1,0:T(8,128)(2,1)} %slice.164), channel_id=1, source_target_pairs={{0,12},{4,0},{8,4},{12,8},{1,13},{5,1},{9,5},{13,9},{2,14},{6,2},{... | collective-permute-start | bytes 983048 | tf_op jit(solution)/shard_map/ppermute | solution.py:68
  46.4 5.8 %collective-permute-start.5 = (bf16[64,1280]{1,0:T(8,128)(2,1)S(1)}, bf16[64,1280]{1,0:T(8,128)(2,1)}, u32[]{:S(2)}, u32[]{:S(2)}) collective-permute-start(bf16[64,1280]{1,0:T(8,128)(2,1)S(1)} %slice.161), channel_id=1, source_target_pairs={{0,16},{16,32},{32,48},{48,64},{64,80},{80,96},{96,112},{112,0},{1... | collective-permute-start | bytes 491528 | tf_op jit(solution)/shard_map/ppermute | solution.py:68
  46.5 5.7 %collective-permute-start.9 = (bf16[64,1280]{1,0:T(8,128)(2,1)S(1)}, bf16[64,1280]{1,0:T(8,128)(2,1)}, u32[]{:S(2)}, u32[]{:S(2)}) collective-permute-start(bf16[64,1280]{1,0:T(8,128)(2,1)S(1)} %slice.162), channel_id=1, source_target_pairs={{0,112},{16,0},{32,16},{48,32},{64,48},{80,64},{96,80},{112,96},{1... | collective-permute-start | bytes 491528 | tf_op jit(solution)/shard_map/ppermute | solution.py:68
  63.7 3.4 %collective-permute-start.16 = (f32[8,16,128]{2,1,0:T(8,128)}, f32[8,16,128]{2,1,0:T(8,128)S(1)}, u32[]{:S(2)}, u32[]{:S(2)}) collective-permute-start(f32[8,16,128]{2,1,0:T(8,128)} %block_stats.1), channel_id=1, source_target_pairs={{0,16},{16,0},{32,48},{48,32},{64,80},{80,64},{96,112},{112,96},{1... | collective-permute-start | bytes 196616 | tf_op jit(solution)/shard_map/ppermute | solution.py:72
  68.1 5.2 %collective-permute-start.19 = (f32[8,16,128]{2,1,0:T(8,128)S(1)}, f32[8,16,128]{2,1,0:T(8,128)S(1)}, u32[]{:S(2)}, u32[]{:S(2)}) collective-permute-start(f32[8,16,128]{2,1,0:T(8,128)S(1)} %add_select_fusion.1), channel_id=1, source_target_pairs={{0,112},{16,32},{32,16},{48,64},{64,48},{80,96},{96,80},{112,0},{1... | collective-permute-start | bytes 196616 | tf_op jit(solution)/shard_map/ppermute | solution.py:334
  71.0 4.0 %collective-permute-start.18 = (f32[8,16,128]{2,1,0:T(8,128)S(1)}, f32[8,16,128]{2,1,0:T(8,128)S(1)}, u32[]{:S(2)}, u32[]{:S(2)}) collective-permute-start(f32[8,16,128]{2,1,0:T(8,128)S(1)} %add_select_fusion.1), channel_id=1, source_target_pairs={{0,96},{16,48},{32,0},{48,80},{64,32},{80,112},{96,64},{112,16},{1... | collective-permute-start | bytes 196616 | tf_op jit(solution)/shard_map/ppermute | solution.py:334
  71.0 6.2 %collective-permute-start.17 = (f32[8,16,128]{2,1,0:T(8,128)S(1)}, f32[8,16,128]{2,1,0:T(8,128)S(1)}, u32[]{:S(2)}, u32[]{:S(2)}) collective-permute-start(f32[8,16,128]{2,1,0:T(8,128)S(1)} %add_select_fusion.1), channel_id=1, source_target_pairs={{0,80},{16,64},{32,112},{48,96},{64,16},{80,0},{96,48},{112,32},{1... | collective-permute-start | bytes 196616 | tf_op jit(solution)/shard_map/ppermute | solution.py:334
  94.5 35.9 %all-to-all-start = ((bf16[8,2,128,640]{3,2,1,0:T(8,128)(2,1)}), bf16[8,2,128,640]{3,2,1,0:T(8,128)(2,1)}, u32[]{:S(2)}, u32[]{:S(2)}) async-start(bf16[8,2,128,640]{3,2,1,0:T(8,128)(2,1)} %get-tuple-element.28), calls=%async_computation | async-start | bytes 5242880 | tf_op jit(solution)/shard_map/all_to_all | solution.py:341
  99.6 7.3 %collective-permute-start.24 = (bf16[128,640]{1,0:T(8,128)(2,1)S(1)}, bf16[128,640]{1,0:T(8,128)(2,1)S(1)}, u32[]{:S(2)}, u32[]{:S(2)}) collective-permute-start(bf16[128,640]{1,0:T(8,128)(2,1)S(1)} %copy-done.23), channel_id=1, source_target_pairs={{0,16},{16,32},{32,48},{48,64},{64,80},{80,96},{96,112},{112,0},{1... | collective-permute-start | bytes 491528 | tf_op jit(solution)/shard_map/ppermute | solution.py:68
  100.5 6.4 %collective-permute-start.25 = (bf16[64,640]{1,0:T(8,128)(2,1)S(1)}, bf16[64,640]{1,0:T(8,128)(2,1)S(1)}, u32[]{:S(2)}, u32[]{:S(2)}) collective-permute-start(bf16[64,640]{1,0:T(8,128)(2,1)S(1)} %get-tuple-element.44), channel_id=1, source_target_pairs={{0,32},{16,48},{32,64},{48,80},{64,96},{80,112},{96,0},{112,16},{1... | collective-permute-start | bytes 245768 | tf_op jit(solution)/shard_map/ppermute | solution.py:68
  102.7 6.4 %collective-permute-start.21 = (bf16[64,640]{1,0:T(8,128)(2,1)S(1)}, bf16[64,640]{1,0:T(8,128)(2,1)S(1)}, u32[]{:S(2)}, u32[]{:S(2)}) collective-permute-start(bf16[64,640]{1,0:T(8,128)(2,1)S(1)} %get-tuple-element.43), channel_id=1, source_target_pairs={{0,96},{16,112},{32,0},{48,16},{64,32},{80,48},{96,64},{112,80},{1... | collective-permute-start | bytes 245768 | tf_op jit(solution)/shard_map/ppermute | solution.py:68
  104.2 5.9 %collective-permute-start.20 = (bf16[128,640]{1,0:T(8,128)(2,1)S(1)}, bf16[128,640]{1,0:T(8,128)(2,1)S(1)}, u32[]{:S(2)}, u32[]{:S(2)}) collective-permute-start(bf16[128,640]{1,0:T(8,128)(2,1)S(1)} %copy-done.22), channel_id=1, source_target_pairs={{0,112},{16,0},{32,16},{48,32},{64,48},{80,64},{96,80},{112,96},{1... | collective-permute-start | bytes 491528 | tf_op jit(solution)/shard_map/ppermute | solution.py:68
  107.0 6.3 %collective-permute-start.26 = (bf16[128,640]{1,0:T(8,128)(2,1)S(1)}, bf16[128,640]{1,0:T(8,128)(2,1)S(1)}, u32[]{:S(2)}, u32[]{:S(2)}) collective-permute-start(bf16[128,640]{1,0:T(8,128)(2,1)S(1)} %pad_add_fusion), channel_id=1, source_target_pairs={{0,16},{16,32},{32,48},{48,64},{64,80},{80,96},{96,112},{112,0},{1... | collective-permute-start | bytes 491528 | tf_op jit(solution)/shard_map/ppermute | solution.py:68
  110.2 5.2 %collective-permute-start.22 = (bf16[128,640]{1,0:T(8,128)(2,1)S(1)}, bf16[128,640]{1,0:T(8,128)(2,1)S(1)}, u32[]{:S(2)}, u32[]{:S(2)}) collective-permute-start(bf16[128,640]{1,0:T(8,128)(2,1)S(1)} %pad_add_fusion.1), channel_id=1, source_target_pairs={{0,112},{16,0},{32,16},{48,32},{64,48},{80,64},{96,80},{112,96},{1... | collective-permute-start | bytes 491528 | tf_op jit(solution)/shard_map/ppermute | solution.py:68
  113.4 5.9 %collective-permute-start.27 = (bf16[128,640]{1,0:T(8,128)(2,1)S(1)}, bf16[128,640]{1,0:T(8,128)(2,1)S(1)}, u32[]{:S(2)}, u32[]{:S(2)}) collective-permute-start(bf16[128,640]{1,0:T(8,128)(2,1)S(1)} %add.115), channel_id=1, source_target_pairs={{0,16},{16,32},{32,48},{48,64},{64,80},{80,96},{96,112},{112,0},{1... | collective-permute-start | bytes 491528 | tf_op jit(solution)/shard_map/ppermute | solution.py:68
  115.5 5.8 %collective-permute-start.23 = (bf16[128,640]{1,0:T(8,128)(2,1)S(1)}, bf16[128,640]{1,0:T(8,128)(2,1)S(1)}, u32[]{:S(2)}, u32[]{:S(2)}) collective-permute-start(bf16[128,640]{1,0:T(8,128)(2,1)S(1)} %add.111), channel_id=1, source_target_pairs={{0,112},{16,0},{32,16},{48,32},{64,48},{80,64},{96,80},{112,96},{1... | collective-permute-start | bytes 491528 | tf_op jit(solution)/shard_map/ppermute | solution.py:68
  133.5 5.5 %collective-permute-start.30 = (f32[2,128]{1,0:T(2,128)S(1)}, f32[2,128]{1,0:T(2,128)S(1)}, u32[]{:S(2)}, u32[]{:S(2)}) collective-permute-start(f32[2,128]{1,0:T(2,128)S(1)} %pad_maximum_fusion.7), channel_id=1, source_target_pairs={{0,3},{1,2},{2,1},{3,0},{4,7},{5,6},{6,5},{7,4},{8,11},{9,10},{10,... | collective-permute-start | bytes 3080 | tf_op jit(solution)/shard_map/ppermute | solution.py:89
  135.9 3.9 %collective-permute-start.29 = (f32[2,128]{1,0:T(2,128)S(1)}, f32[2,128]{1,0:T(2,128)S(1)}, u32[]{:S(2)}, u32[]{:S(2)}) collective-permute-start(f32[2,128]{1,0:T(2,128)S(1)} %pad_maximum_fusion.7), channel_id=1, source_target_pairs={{0,2},{1,3},{2,0},{3,1},{4,6},{5,7},{6,4},{7,5},{8,10},{9,11},{10,... | collective-permute-start | bytes 3080 | tf_op jit(solution)/shard_map/ppermute | solution.py:89
  138.3 1.5 %collective-permute-start.28 = (f32[2,128]{1,0:T(2,128)S(1)}, f32[2,128]{1,0:T(2,128)S(1)}, u32[]{:S(2)}, u32[]{:S(2)}) collective-permute-start(f32[2,128]{1,0:T(2,128)S(1)} %pad_maximum_fusion.7), channel_id=1, source_target_pairs={{0,1},{1,0},{2,3},{3,2},{4,5},{5,4},{6,7},{7,6},{8,9},{9,8},{10,11... | collective-permute-start | bytes 3080 | tf_op jit(solution)/shard_map/ppermute | solution.py:89
  (24 other events, 252.5 us)

commit v4 on v3

--- a/solution.py
+++ b/solution.py
@@ -187,9 +187,9 @@
     q_ref, c_ref, k_ref, v_ref = scratch
     k_turned = k_ref[...].astype(jnp.float32).T.astype(jnp.bfloat16)
     h = pl.program_id(0)
-    for t in range(0, len(places), 2):
-        cols = slice(t * 128, t * 128 + 256)
-        owners = [owner_of(index_ref, place) for place in places[t : t + 2]]
+    for t in (0, 4):
+        cols = slice(t * 128, t * 128 + 512)
+        owners = [owner_of(index_ref, place) for place in places[t : t + 4]]
         log_total, delta = (
             jnp.concatenate(
                 [totals_ref[owner, pl.ds(heads * kind + h, 1), :] for owner in owners], axis=1
@@ -206,17 +206,17 @@
             dv_ref[...] = dv
             dk_ref[...] = dk
         else:
-            dv_ref[...] += dv
-            dk_ref[...] += dk
+            dv = (dv_ref[...] + dv).astype(jnp.bfloat16)
+            dk = ((dk_ref[...] + dk) * SCALING).astype(jnp.bfloat16)
+            for place in range(8):
+                owner = key_owner_of(index_ref, place)
+                rows = slice(place * 128, place * 128 + 128)
+                dkv_ref[owner, 0] = dk[rows]
+                dkv_ref[owner, 1] = dv[rows]
         dq = jnp.dot(k_turned, ds, preferred_element_type=jnp.float32)
         dq = (dq / LOG2E).T.astype(jnp.bfloat16)
-        dq_refs[t][...] = dq[:128]
-        dq_refs[t + 1][...] = dq[128:]
-    for place in range(8):
-        owner = key_owner_of(index_ref, place)
-        rows = slice(place * 128, place * 128 + 128)
-        dkv_ref[owner, 0] = (dk_ref[rows, :] * SCALING).astype(jnp.bfloat16)
-        dkv_ref[owner, 1] = dv_ref[rows, :].astype(jnp.bfloat16)
+        for side in range(4):
+            dq_refs[t + side][...] = dq[side * 128 : side * 128 + 128]
 
 
 SMEM_SPEC = pl.BlockSpec(memory_space=pltpu.SMEM)

time: 142 us -> 142 us (level)
  no operation moved by 1% of the time
where the time goes in v4:
time: 142 us; the launch traced here: 141 us
  starting transfers between devices  53.7 us (38%)
  waiting for transfers between devices  36.8 us (26%)
  Pallas kernels  27.9 us (20%)
  other arithmetic  10.4 us (7%)
  matrix products  5.72 us (4%)
  local copies, waits for them, and re-layouts  4.41 us (3%)
  between operations  1.84 us (1%)
    ppermute x20, starting transfers between devices, shift(): lax.ppermute(x, axis, [(i, (i + distance) % size) for i in range(size)])  33.2 us
    ppermute x20, waiting for transfers between devices, shift(): lax.ppermute(x, axis, [(i, (i + distance) % size) for i in range(size)])  21.4 us
    pallas_call x1, Pallas kernels, block_grads(): pl.pallas_call(functools.partial(grads_kernel, places, counts, heads), gr...  16.3 us
    pallas_call x1, Pallas kernels, block_stats(): pl.pallas_call(functools.partial(stats_kernel, places, counts, heads), gr...  11.5 us
    all_to_all x1, waiting for transfers between devices, shards(): lax.all_to_all(dkv, ('xl', 'y'), 0, 0, tiled=True).astype(f32)  8.89 us
    ppermute x4, starting transfers between devices, flip(): return lax.ppermute(x, axis, [(0, 1), (1, 0)])  5.45 us
    dot_general x1, matrix products, shards(): lax.dot_general(gated_cot, out_weight, NT, preferred_element_type=f32)  5.08 us
    ppermute x3, starting transfers between devices, shards(): lax.ppermute(stats, 'z', perm)  5.08 us
  transfers between devices with their start and end apart: 32, of which 14 were waited for; matrix products, arithmetic and copies ran while one was open for 9% of the time, Pallas kernels for 0%

profile of v4, /device:TPU:1, one launch (start us, length us, event | category | flops | bytes accessed | tf_op | source)
XLA Modules:
  0.0 140.6 jit_solution(15101169016040321187)
XLA Ops:
  1.9 3.3 %collective-permute-start = (f32[2,128]{1,0:T(2,128)S(1)}, f32[2,128]{1,0:T(2,128)S(1)}, u32[]{:S(2)}, u32[]{:S(2)}) collective-permute-start(f32[2,128]{1,0:T(2,128)S(1)} %multiply_reduce_fusion), channel_id=1, source_target_pairs={{0,1},{1,0},{2,3},{3,2},{4,5},{5,4},{6,7},{7,6},{8,9},{9,8},{10,11... | collective-permute-start | bytes 3080 | tf_op jit(solution)/shard_map/ppermute | solution.py:83
  7.9 2.0 %collective-permute-start.1 = (f32[2,128]{1,0:T(2,128)S(1)}, f32[2,128]{1,0:T(2,128)S(1)}, u32[]{:S(2)}, u32[]{:S(2)}) collective-permute-start(f32[2,128]{1,0:T(2,128)S(1)} %add.95), channel_id=1, source_target_pairs={{0,2},{2,0},{1,3},{3,1},{4,6},{6,4},{5,7},{7,5},{8,10},{10,8},{9,1... | collective-permute-start | bytes 3080 | tf_op jit(solution)/shard_map/ppermute | solution.py:83
  9.9 5.1 %fusion.10 = bf16[128,640]{1,0:T(8,128)(2,1)S(1)} fusion(bf16[640,5120]{1,0:T(8,128)(2,1)} %param.19, bf16[128,5120]{1,0:T(8,128)(2,1)S(1)} %copy-done.4, f32[5120]{0:T(1024)S(1)} %bitcast.62), kind=kOutput, calls=%fused_computation.14 | convolution fusion | flops 840908800 | bytes 8048640 | tf_op jit(solution)/shard_map/dot_general | solution.py:320
  16.4 1.7 %collective-permute-start.2 = (bf16[128,1280]{1,0:T(8,128)(2,1)S(1)}, bf16[128,1280]{1,0:T(8,128)(2,1)S(1)}, u32[]{:S(2)}, u32[]{:S(2)}) collective-permute-start(bf16[128,1280]{1,0:T(8,128)(2,1)S(1)} %pad_maximum_fusion.refs_0_.refs_9_), channel_id=1, source_target_pairs={{0,16},{16,32},{32,48},{48,64},{64,80},{80,96},{96,112},{112,0},{1... | collective-permute-start | bytes 983048 | tf_op jit(solution)/shard_map/ppermute | solution.py:68
  18.1 4.0 %collective-permute-start.6 = (bf16[128,1280]{1,0:T(8,128)(2,1)S(1)}, bf16[128,1280]{1,0:T(8,128)(2,1)S(1)}, u32[]{:S(2)}, u32[]{:S(2)}) collective-permute-start(bf16[128,1280]{1,0:T(8,128)(2,1)S(1)} %pad_maximum_fusion.refs_0_.refs_9_), channel_id=1, source_target_pairs={{0,112},{16,0},{32,16},{48,32},{64,48},{80,64},{96,80},{112,96},{1... | collective-permute-start | bytes 983048 | tf_op jit(solution)/shard_map/ppermute | solution.py:68
  26.0 3.3 %collective-permute-done.2.refs_1_.refs_10_ = bf16[128,1280]{1,0:T(8,128)(2,1)S(1)} collective-permute-done((bf16[128,1280]{1,0:T(8,128)(2,1)S(1)}, bf16[128,1280]{1,0:T(8,128)(2,1)S(1)}, u32[]{:S(2)}, u32[]{:S(2)}) %collective-permute-start.2) | collective-permute-done | bytes 327712 | tf_op jit(solution)/shard_map/ppermute | solution.py:68
  29.3 2.7 %collective-permute-start.7 = (bf16[128,1280]{1,0:T(8,128)(2,1)S(1)}, bf16[128,1280]{1,0:T(8,128)(2,1)S(1)}, u32[]{:S(2)}, u32[]{:S(2)}) collective-permute-start(bf16[128,1280]{1,0:T(8,128)(2,1)S(1)} %collective-permute-done.6.refs_8_.refs_17_), channel_id=1, source_target_pairs={{0,112},{16,0},{32,16},{48,32},{64,48},{80,64},{96,80},{112,96},{1... | collective-permute-start | bytes 983048 | tf_op jit(solution)/shard_map/ppermute | solution.py:68
  32.0 6.3 %collective-permute-done.3.refs_2_.refs_11_ = bf16[128,1280]{1,0:T(8,128)(2,1)S(1)} collective-permute-done((bf16[128,1280]{1,0:T(8,128)(2,1)S(1)}, bf16[128,1280]{1,0:T(8,128)(2,1)S(1)}, u32[]{:S(2)}, u32[]{:S(2)}) %collective-permute-start.3) | collective-permute-done | bytes 327712 | tf_op jit(solution)/shard_map/ppermute | solution.py:68
  38.3 2.7 %collective-permute-start.8 = (bf16[128,1280]{1,0:T(8,128)(2,1)S(1)}, bf16[128,1280]{1,0:T(8,128)(2,1)S(1)}, u32[]{:S(2)}, u32[]{:S(2)}) collective-permute-start(bf16[128,1280]{1,0:T(8,128)(2,1)S(1)} %collective-permute-done.7.refs_7_.refs_16_), channel_id=1, source_target_pairs={{0,112},{16,0},{32,16},{48,32},{64,48},{80,64},{96,80},{112,96},{1... | collective-permute-start | bytes 983048 | tf_op jit(solution)/shard_map/ppermute | solution.py:68
  44.8 1.6 %collective-permute-done.4.refs_3_.refs_12_ = bf16[128,1280]{1,0:T(8,128)(2,1)S(1)} collective-permute-done((bf16[128,1280]{1,0:T(8,128)(2,1)S(1)}, bf16[128,1280]{1,0:T(8,128)(2,1)S(1)}, u32[]{:S(2)}, u32[]{:S(2)}) %collective-permute-start.4) | collective-permute-done | bytes 327712 | tf_op jit(solution)/shard_map/ppermute | solution.py:68
  46.5 2.7 %collective-permute-start.9 = (bf16[64,1280]{1,0:T(8,128)(2,1)S(1)}, bf16[64,1280]{1,0:T(8,128)(2,1)}, u32[]{:S(2)}, u32[]{:S(2)}) collective-permute-start(bf16[64,1280]{1,0:T(8,128)(2,1)S(1)} %slice.162), channel_id=1, source_target_pairs={{0,112},{16,0},{32,16},{48,32},{64,48},{80,64},{96,80},{112,96},{1... | collective-permute-start | bytes 491528 | tf_op jit(solution)/shard_map/ppermute | solution.py:68
  49.9 2.3 %collective-permute-done.5.refs_4_.refs_13_ = bf16[64,1280]{1,0:T(8,128)(2,1)} collective-permute-done((bf16[64,1280]{1,0:T(8,128)(2,1)S(1)}, bf16[64,1280]{1,0:T(8,128)(2,1)}, u32[]{:S(2)}, u32[]{:S(2)}) %collective-permute-start.5) | collective-permute-done | bytes 163872 | tf_op jit(solution)/shard_map/ppermute | solution.py:68
  52.2 11.5 %block_stats.1 = f32[8,16,128]{2,1,0:T(8,128)} custom-call(s32[3]{0:T(128)} %pad_add_fusion.2.index_ref, bf16[128,1280]{1,0:T(8,128)(2,1)} %copy-done.6, bf16[128,1280]{1,0:T(8,128)(2,1)} %copy-done.18, bf16[128,1280]{1,0:T(8,128)(2,1)} %copy-done.20, bf16[128,1280]{1,0:T(8,128)(2,1)} %copy-done.16, ...), custom_call_target="tpu_custom_call" | custom-call | flops 10737418240 | bytes 8388608 | tf_op jit(solution)/shard_map/block_stats/pallas_call | solution.py:245
  65.4 1.8 %collective-permute-done.16 = f32[8,16,128]{2,1,0:T(8,128)S(1)} collective-permute-done((f32[8,16,128]{2,1,0:T(8,128)}, f32[8,16,128]{2,1,0:T(8,128)S(1)}, u32[]{:S(2)}, u32[]{:S(2)}) %collective-permute-start.16) | collective-permute-done | bytes 65568 | tf_op jit(solution)/shard_map/ppermute | solution.py:72
  68.1 2.9 %collective-permute-start.19 = (f32[8,16,128]{2,1,0:T(8,128)S(1)}, f32[8,16,128]{2,1,0:T(8,128)S(1)}, u32[]{:S(2)}, u32[]{:S(2)}) collective-permute-start(f32[8,16,128]{2,1,0:T(8,128)S(1)} %add_select_fusion.1), channel_id=1, source_target_pairs={{0,112},{16,32},{32,16},{48,64},{64,48},{80,96},{96,80},{112,0},{1... | collective-permute-start | bytes 196616 | tf_op jit(solution)/shard_map/ppermute | solution.py:334
  71.0 2.2 %collective-permute-start.17 = (f32[8,16,128]{2,1,0:T(8,128)S(1)}, f32[8,16,128]{2,1,0:T(8,128)S(1)}, u32[]{:S(2)}, u32[]{:S(2)}) collective-permute-start(f32[8,16,128]{2,1,0:T(8,128)S(1)} %add_select_fusion.1), channel_id=1, source_target_pairs={{0,80},{16,64},{32,112},{48,96},{64,16},{80,0},{96,48},{112,32},{1... | collective-permute-start | bytes 196616 | tf_op jit(solution)/shard_map/ppermute | solution.py:334
  73.3 1.7 %collective-permute-done.18 = f32[8,16,128]{2,1,0:T(8,128)S(1)} collective-permute-done((f32[8,16,128]{2,1,0:T(8,128)S(1)}, f32[8,16,128]{2,1,0:T(8,128)S(1)}, u32[]{:S(2)}, u32[]{:S(2)}) %collective-permute-start.18) | collective-permute-done | bytes 65568 | tf_op jit(solution)/shard_map/ppermute | solution.py:334
  75.0 2.1 %collective-permute-done.17 = f32[8,16,128]{2,1,0:T(8,128)S(1)} collective-permute-done((f32[8,16,128]{2,1,0:T(8,128)S(1)}, f32[8,16,128]{2,1,0:T(8,128)S(1)}, u32[]{:S(2)}, u32[]{:S(2)}) %collective-permute-start.17) | collective-permute-done | bytes 65568 | tf_op jit(solution)/shard_map/ppermute | solution.py:334
  78.0 16.3 %block_grads.1 = (bf16[128,640]{1,0:T(8,128)(2,1)}, bf16[128,640]{1,0:T(8,128)(2,1)}, bf16[128,640]{1,0:T(8,128)(2,1)}, bf16[128,640]{1,0:T(8,128)(2,1)}, bf16[1...) custom-call(s32[3]{0:T(128)} %pad_add_fusion.2.index_ref, ...), custom_call_target="tpu_custom_call" | custom-call | flops 13421772800 | bytes 16777216 | tf_op jit(solution)/shard_map/block_grads/pallas_call | solution.py:265
  94.4 5.1 %all-to-all-start = ((bf16[8,2,128,640]{3,2,1,0:T(8,128)(2,1)}), bf16[8,2,128,640]{3,2,1,0:T(8,128)(2,1)}, u32[]{:S(2)}, u32[]{:S(2)}) async-start(bf16[8,2,128,640]{3,2,1,0:T(8,128)(2,1)} %get-tuple-element.28), calls=%async_computation | async-start | bytes 5242880 | tf_op jit(solution)/shard_map/all_to_all | solution.py:341
  100.5 2.1 %collective-permute-start.25 = (bf16[64,640]{1,0:T(8,128)(2,1)S(1)}, bf16[64,640]{1,0:T(8,128)(2,1)S(1)}, u32[]{:S(2)}, u32[]{:S(2)}) collective-permute-start(bf16[64,640]{1,0:T(8,128)(2,1)S(1)} %get-tuple-element.44), channel_id=1, source_target_pairs={{0,32},{16,48},{32,64},{48,80},{64,96},{80,112},{96,0},{112,16},{1... | collective-permute-start | bytes 245768 | tf_op jit(solution)/shard_map/ppermute | solution.py:68
  105.2 1.6 %collective-permute-done.25 = bf16[64,640]{1,0:T(8,128)(2,1)S(1)} collective-permute-done((bf16[64,640]{1,0:T(8,128)(2,1)S(1)}, bf16[64,640]{1,0:T(8,128)(2,1)S(1)}, u32[]{:S(2)}, u32[]{:S(2)}) %collective-permute-start.25) | collective-permute-done | bytes 81952 | tf_op jit(solution)/shard_map/ppermute | solution.py:68
  106.9 2.1 %collective-permute-start.26 = (bf16[128,640]{1,0:T(8,128)(2,1)S(1)}, bf16[128,640]{1,0:T(8,128)(2,1)S(1)}, u32[]{:S(2)}, u32[]{:S(2)}) collective-permute-start(bf16[128,640]{1,0:T(8,128)(2,1)S(1)} %pad_add_fusion), channel_id=1, source_target_pairs={{0,16},{16,32},{32,48},{48,64},{64,80},{80,96},{96,112},{112,0},{1... | collective-permute-start | bytes 491528 | tf_op jit(solution)/shard_map/ppermute | solution.py:68
  111.6 1.6 %collective-permute-done.26 = bf16[128,640]{1,0:T(8,128)(2,1)S(1)} collective-permute-done((bf16[128,640]{1,0:T(8,128)(2,1)S(1)}, bf16[128,640]{1,0:T(8,128)(2,1)S(1)}, u32[]{:S(2)}, u32[]{:S(2)}) %collective-permute-start.26) | collective-permute-done | bytes 163872 | tf_op jit(solution)/shard_map/ppermute | solution.py:68
  113.3 2.0 %collective-permute-start.27 = (bf16[128,640]{1,0:T(8,128)(2,1)S(1)}, bf16[128,640]{1,0:T(8,128)(2,1)S(1)}, u32[]{:S(2)}, u32[]{:S(2)}) collective-permute-start(bf16[128,640]{1,0:T(8,128)(2,1)S(1)} %add.115), channel_id=1, source_target_pairs={{0,16},{16,32},{32,48},{48,64},{64,80},{80,96},{96,112},{112,0},{1... | collective-permute-start | bytes 491528 | tf_op jit(solution)/shard_map/ppermute | solution.py:68
  115.4 2.2 %collective-permute-start.23 = (bf16[128,640]{1,0:T(8,128)(2,1)S(1)}, bf16[128,640]{1,0:T(8,128)(2,1)S(1)}, u32[]{:S(2)}, u32[]{:S(2)}) collective-permute-start(bf16[128,640]{1,0:T(8,128)(2,1)S(1)} %add.111), channel_id=1, source_target_pairs={{0,112},{16,0},{32,16},{48,32},{64,48},{80,64},{96,80},{112,96},{1... | collective-permute-start | bytes 491528 | tf_op jit(solution)/shard_map/ppermute | solution.py:68
  117.5 1.6 %collective-permute-done.27 = bf16[128,640]{1,0:T(8,128)(2,1)S(1)} collective-permute-done((bf16[128,640]{1,0:T(8,128)(2,1)S(1)}, bf16[128,640]{1,0:T(8,128)(2,1)S(1)}, u32[]{:S(2)}, u32[]{:S(2)}) %collective-permute-start.27) | collective-permute-done | bytes 163872 | tf_op jit(solution)/shard_map/ppermute | solution.py:68
  119.1 2.0 %collective-permute-done.23 = bf16[128,640]{1,0:T(8,128)(2,1)S(1)} collective-permute-done((bf16[128,640]{1,0:T(8,128)(2,1)S(1)}, bf16[128,640]{1,0:T(8,128)(2,1)S(1)}, u32[]{:S(2)}, u32[]{:S(2)}) %collective-permute-start.23) | collective-permute-done | bytes 163872 | tf_op jit(solution)/shard_map/ppermute | solution.py:68
  121.5 8.9 %all-to-all-done = bf16[8,2,128,640]{3,2,1,0:T(8,128)(2,1)} async-done(((bf16[8,2,128,640]{3,2,1,0:T(8,128)(2,1)}), bf16[8,2,128,640]{3,2,1,0:T(8,128)(2,1)}, u32[]{:S(2)}, u32[]{:S(2)}) %all-to-all-start) | async-done | bytes 2621472 | tf_op jit(solution)/shard_map/all_to_all | solution.py:341
  130.3 2.2 %convert_reduce_fusion = f32[2,128,640]{2,1,0:T(8,128)S(1)} fusion(bf16[8,2,128,640]{3,2,1,0:T(8,128)(2,1)} %all-to-all-done), kind=kLoop, calls=%fused_computation | loop fusion | flops 2457600 | bytes 3276800 | tf_op jit(solution)/shard_map/reduce_sum | solution.py:341
  133.4 2.4 %collective-permute-start.30 = (f32[2,128]{1,0:T(2,128)S(1)}, f32[2,128]{1,0:T(2,128)S(1)}, u32[]{:S(2)}, u32[]{:S(2)}) collective-permute-start(f32[2,128]{1,0:T(2,128)S(1)} %pad_maximum_fusion.7), channel_id=1, source_target_pairs={{0,3},{1,2},{2,1},{3,0},{4,7},{5,6},{6,5},{7,4},{8,11},{9,10},{10,... | collective-permute-start | bytes 3080 | tf_op jit(solution)/shard_map/ppermute | solution.py:89
  135.8 2.4 %collective-permute-start.29 = (f32[2,128]{1,0:T(2,128)S(1)}, f32[2,128]{1,0:T(2,128)S(1)}, u32[]{:S(2)}, u32[]{:S(2)}) collective-permute-start(f32[2,128]{1,0:T(2,128)S(1)} %pad_maximum_fusion.7), channel_id=1, source_target_pairs={{0,2},{1,3},{2,0},{3,1},{4,6},{5,7},{6,4},{7,5},{8,10},{9,11},{10,... | collective-permute-start | bytes 3080 | tf_op jit(solution)/shard_map/ppermute | solution.py:89
  (149 shorter events, 26.4 us)
Async XLA Ops:
  1.9 5.9 %collective-permute-start = (f32[2,128]{1,0:T(2,128)S(1)}, f32[2,128]{1,0:T(2,128)S(1)}, u32[]{:S(2)}, u32[]{:S(2)}) collective-permute-start(f32[2,128]{1,0:T(2,128)S(1)} %multiply_reduce_fusion), channel_id=1, source_target_pairs={{0,1},{1,0},{2,3},{3,2},{4,5},{5,4},{6,7},{7,6},{8,9},{9,8},{10,11... | collective-permute-start | bytes 3080 | tf_op jit(solution)/shard_map/ppermute | solution.py:83
  5.3 16.9 %collective-permute-start.11 = (bf16[128,640]{1,0:T(8,128)(2,1)}, bf16[128,640]{1,0:T(8,128)(2,1)}, u32[]{:S(2)}, u32[]{:S(2)}) collective-permute-start(bf16[128,640]{1,0:T(8,128)(2,1)} %param.16), channel_id=1, source_target_pairs={{0,128},{128,0},{1,129},{129,1},{2,130},{130,2},{3,131},{131,3},{4... | collective-permute-start | bytes 491528 | tf_op jit(solution)/shard_map/ppermute | solution.py:83
  7.9 7.1 %collective-permute-start.1 = (f32[2,128]{1,0:T(2,128)S(1)}, f32[2,128]{1,0:T(2,128)S(1)}, u32[]{:S(2)}, u32[]{:S(2)}) collective-permute-start(f32[2,128]{1,0:T(2,128)S(1)} %add.95), channel_id=1, source_target_pairs={{0,2},{2,0},{1,3},{3,1},{4,6},{6,4},{5,7},{7,5},{8,10},{10,8},{9,1... | collective-permute-start | bytes 3080 | tf_op jit(solution)/shard_map/ppermute | solution.py:83
  16.3 5.9 %collective-permute-start.10 = (bf16[128,640]{1,0:T(8,128)(2,1)S(1)}, bf16[128,640]{1,0:T(8,128)(2,1)S(1)}, u32[]{:S(2)}, u32[]{:S(2)}) collective-permute-start(bf16[128,640]{1,0:T(8,128)(2,1)S(1)} %fusion.9), channel_id=1, source_target_pairs={{0,128},{128,0},{1,129},{129,1},{2,130},{130,2},{3,131},{131,3},{4... | collective-permute-start | bytes 491528 | tf_op jit(solution)/shard_map/ppermute | solution.py:83
  16.4 12.9 %collective-permute-start.2 = (bf16[128,1280]{1,0:T(8,128)(2,1)S(1)}, bf16[128,1280]{1,0:T(8,128)(2,1)S(1)}, u32[]{:S(2)}, u32[]{:S(2)}) collective-permute-start(bf16[128,1280]{1,0:T(8,128)(2,1)S(1)} %pad_maximum_fusion.refs_0_.refs_9_), channel_id=1, source_target_pairs={{0,16},{16,32},{32,48},{48,64},{64,80},{80,96},{96,112},{112,0},{1... | collective-permute-start | bytes 983048 | tf_op jit(solution)/shard_map/ppermute | solution.py:68
  18.1 11.2 %collective-permute-start.6 = (bf16[128,1280]{1,0:T(8,128)(2,1)S(1)}, bf16[128,1280]{1,0:T(8,128)(2,1)S(1)}, u32[]{:S(2)}, u32[]{:S(2)}) collective-permute-start(bf16[128,1280]{1,0:T(8,128)(2,1)S(1)} %pad_maximum_fusion.refs_0_.refs_9_), channel_id=1, source_target_pairs={{0,112},{16,0},{32,16},{48,32},{64,48},{80,64},{96,80},{112,96},{1... | collective-permute-start | bytes 983048 | tf_op jit(solution)/shard_map/ppermute | solution.py:68
  23.1 17.8 %collective-permute-start.12 = (bf16[256,1280]{1,0:T(8,128)(2,1)S(1)}, bf16[256,1280]{1,0:T(8,128)(2,1)S(1)}, u32[]{:S(2)}, u32[]{:S(2)}) collective-permute-start(bf16[256,1280]{1,0:T(8,128)(2,1)S(1)} %maximum_maximum_fusion.refs_18_.refs_23_), channel_id=1, source_target_pairs={{0,4},{4,8},{8,12},{12,0},{1,5},{5,9},{9,13},{13,1},{2,6},{6,10},{... | collective-permute-start | bytes 1966088 | tf_op jit(solution)/shard_map/ppermute | solution.py:68
  24.5 17.9 %collective-permute-start.14 = (bf16[256,1280]{1,0:T(8,128)(2,1)S(1)}, bf16[256,1280]{1,0:T(8,128)(2,1)S(1)}, u32[]{:S(2)}, u32[]{:S(2)}) collective-permute-start(bf16[256,1280]{1,0:T(8,128)(2,1)S(1)} %maximum_maximum_fusion.refs_18_.refs_23_), channel_id=1, source_target_pairs={{0,12},{4,0},{8,4},{12,8},{1,13},{5,1},{9,5},{13,9},{2,14},{6,2},{... | collective-permute-start | bytes 1966088 | tf_op jit(solution)/shard_map/ppermute | solution.py:68
  29.3 9.0 %collective-permute-start.3 = (bf16[128,1280]{1,0:T(8,128)(2,1)S(1)}, bf16[128,1280]{1,0:T(8,128)(2,1)S(1)}, u32[]{:S(2)}, u32[]{:S(2)}) collective-permute-start(bf16[128,1280]{1,0:T(8,128)(2,1)S(1)} %collective-permute-done.2.refs_1_.refs_10_), channel_id=1, source_target_pairs={{0,16},{16,32},{32,48},{48,64},{64,80},{80,96},{96,112},{112,0},{1... | collective-permute-start | bytes 983048 | tf_op jit(solution)/shard_map/ppermute | solution.py:68
  29.3 9.0 %collective-permute-start.7 = (bf16[128,1280]{1,0:T(8,128)(2,1)S(1)}, bf16[128,1280]{1,0:T(8,128)(2,1)S(1)}, u32[]{:S(2)}, u32[]{:S(2)}) collective-permute-start(bf16[128,1280]{1,0:T(8,128)(2,1)S(1)} %collective-permute-done.6.refs_8_.refs_17_), channel_id=1, source_target_pairs={{0,112},{16,0},{32,16},{48,32},{64,48},{80,64},{96,80},{112,96},{1... | collective-permute-start | bytes 983048 | tf_op jit(solution)/shard_map/ppermute | solution.py:68
  38.3 8.1 %collective-permute-start.4 = (bf16[128,1280]{1,0:T(8,128)(2,1)S(1)}, bf16[128,1280]{1,0:T(8,128)(2,1)S(1)}, u32[]{:S(2)}, u32[]{:S(2)}) collective-permute-start(bf16[128,1280]{1,0:T(8,128)(2,1)S(1)} %collective-permute-done.3.refs_2_.refs_11_), channel_id=1, source_target_pairs={{0,16},{16,32},{32,48},{48,64},{64,80},{80,96},{96,112},{112,0},{1... | collective-permute-start | bytes 983048 | tf_op jit(solution)/shard_map/ppermute | solution.py:68
  38.3 8.2 %collective-permute-start.8 = (bf16[128,1280]{1,0:T(8,128)(2,1)S(1)}, bf16[128,1280]{1,0:T(8,128)(2,1)S(1)}, u32[]{:S(2)}, u32[]{:S(2)}) collective-permute-start(bf16[128,1280]{1,0:T(8,128)(2,1)S(1)} %collective-permute-done.7.refs_7_.refs_16_), channel_id=1, source_target_pairs={{0,112},{16,0},{32,16},{48,32},{64,48},{80,64},{96,80},{112,96},{1... | collective-permute-start | bytes 983048 | tf_op jit(solution)/shard_map/ppermute | solution.py:68
  41.0 11.2 %collective-permute-start.13 = (bf16[128,1280]{1,0:T(8,128)(2,1)S(1)}, bf16[128,1280]{1,0:T(8,128)(2,1)}, u32[]{:S(2)}, u32[]{:S(2)}) collective-permute-start(bf16[128,1280]{1,0:T(8,128)(2,1)S(1)} %slice.163), channel_id=1, source_target_pairs={{0,4},{4,8},{8,12},{12,0},{1,5},{5,9},{9,13},{13,1},{2,6},{6,10},{... | collective-permute-start | bytes 983048 | tf_op jit(solution)/shard_map/ppermute | solution.py:68
  43.2 9.0 %collective-permute-start.15 = (bf16[128,1280]{1,0:T(8,128)(2,1)}, bf16[128,1280]{1,0:T(8,128)(2,1)}, u32[]{:S(2)}, u32[]{:S(2)}) collective-permute-start(bf16[128,1280]{1,0:T(8,128)(2,1)} %slice.164), channel_id=1, source_target_pairs={{0,12},{4,0},{8,4},{12,8},{1,13},{5,1},{9,5},{13,9},{2,14},{6,2},{... | collective-permute-start | bytes 983048 | tf_op jit(solution)/shard_map/ppermute | solution.py:68
  46.4 5.8 %collective-permute-start.5 = (bf16[64,1280]{1,0:T(8,128)(2,1)S(1)}, bf16[64,1280]{1,0:T(8,128)(2,1)}, u32[]{:S(2)}, u32[]{:S(2)}) collective-permute-start(bf16[64,1280]{1,0:T(8,128)(2,1)S(1)} %slice.161), channel_id=1, source_target_pairs={{0,16},{16,32},{32,48},{48,64},{64,80},{80,96},{96,112},{112,0},{1... | collective-permute-start | bytes 491528 | tf_op jit(solution)/shard_map/ppermute | solution.py:68
  46.5 5.7 %collective-permute-start.9 = (bf16[64,1280]{1,0:T(8,128)(2,1)S(1)}, bf16[64,1280]{1,0:T(8,128)(2,1)}, u32[]{:S(2)}, u32[]{:S(2)}) collective-permute-start(bf16[64,1280]{1,0:T(8,128)(2,1)S(1)} %slice.162), channel_id=1, source_target_pairs={{0,112},{16,0},{32,16},{48,32},{64,48},{80,64},{96,80},{112,96},{1... | collective-permute-start | bytes 491528 | tf_op jit(solution)/shard_map/ppermute | solution.py:68
  63.7 3.4 %collective-permute-start.16 = (f32[8,16,128]{2,1,0:T(8,128)}, f32[8,16,128]{2,1,0:T(8,128)S(1)}, u32[]{:S(2)}, u32[]{:S(2)}) collective-permute-start(f32[8,16,128]{2,1,0:T(8,128)} %block_stats.1), channel_id=1, source_target_pairs={{0,16},{16,0},{32,48},{48,32},{64,80},{80,64},{96,112},{112,96},{1... | collective-permute-start | bytes 196616 | tf_op jit(solution)/shard_map/ppermute | solution.py:72
  68.1 5.2 %collective-permute-start.19 = (f32[8,16,128]{2,1,0:T(8,128)S(1)}, f32[8,16,128]{2,1,0:T(8,128)S(1)}, u32[]{:S(2)}, u32[]{:S(2)}) collective-permute-start(f32[8,16,128]{2,1,0:T(8,128)S(1)} %add_select_fusion.1), channel_id=1, source_target_pairs={{0,112},{16,32},{32,16},{48,64},{64,48},{80,96},{96,80},{112,0},{1... | collective-permute-start | bytes 196616 | tf_op jit(solution)/shard_map/ppermute | solution.py:334
  71.0 4.0 %collective-permute-start.18 = (f32[8,16,128]{2,1,0:T(8,128)S(1)}, f32[8,16,128]{2,1,0:T(8,128)S(1)}, u32[]{:S(2)}, u32[]{:S(2)}) collective-permute-start(f32[8,16,128]{2,1,0:T(8,128)S(1)} %add_select_fusion.1), channel_id=1, source_target_pairs={{0,96},{16,48},{32,0},{48,80},{64,32},{80,112},{96,64},{112,16},{1... | collective-permute-start | bytes 196616 | tf_op jit(solution)/shard_map/ppermute | solution.py:334
  71.0 6.2 %collective-permute-start.17 = (f32[8,16,128]{2,1,0:T(8,128)S(1)}, f32[8,16,128]{2,1,0:T(8,128)S(1)}, u32[]{:S(2)}, u32[]{:S(2)}) collective-permute-start(f32[8,16,128]{2,1,0:T(8,128)S(1)} %add_select_fusion.1), channel_id=1, source_target_pairs={{0,80},{16,64},{32,112},{48,96},{64,16},{80,0},{96,48},{112,32},{1... | collective-permute-start | bytes 196616 | tf_op jit(solution)/shard_map/ppermute | solution.py:334
  94.4 35.9 %all-to-all-start = ((bf16[8,2,128,640]{3,2,1,0:T(8,128)(2,1)}), bf16[8,2,128,640]{3,2,1,0:T(8,128)(2,1)}, u32[]{:S(2)}, u32[]{:S(2)}) async-start(bf16[8,2,128,640]{3,2,1,0:T(8,128)(2,1)} %get-tuple-element.28), calls=%async_computation | async-start | bytes 5242880 | tf_op jit(solution)/shard_map/all_to_all | solution.py:341
  99.5 7.3 %collective-permute-start.24 = (bf16[128,640]{1,0:T(8,128)(2,1)S(1)}, bf16[128,640]{1,0:T(8,128)(2,1)S(1)}, u32[]{:S(2)}, u32[]{:S(2)}) collective-permute-start(bf16[128,640]{1,0:T(8,128)(2,1)S(1)} %copy-done.23), channel_id=1, source_target_pairs={{0,16},{16,32},{32,48},{48,64},{64,80},{80,96},{96,112},{112,0},{1... | collective-permute-start | bytes 491528 | tf_op jit(solution)/shard_map/ppermute | solution.py:68
  100.5 6.4 %collective-permute-start.25 = (bf16[64,640]{1,0:T(8,128)(2,1)S(1)}, bf16[64,640]{1,0:T(8,128)(2,1)S(1)}, u32[]{:S(2)}, u32[]{:S(2)}) collective-permute-start(bf16[64,640]{1,0:T(8,128)(2,1)S(1)} %get-tuple-element.44), channel_id=1, source_target_pairs={{0,32},{16,48},{32,64},{48,80},{64,96},{80,112},{96,0},{112,16},{1... | collective-permute-start | bytes 245768 | tf_op jit(solution)/shard_map/ppermute | solution.py:68
  102.6 6.4 %collective-permute-start.21 = (bf16[64,640]{1,0:T(8,128)(2,1)S(1)}, bf16[64,640]{1,0:T(8,128)(2,1)S(1)}, u32[]{:S(2)}, u32[]{:S(2)}) collective-permute-start(bf16[64,640]{1,0:T(8,128)(2,1)S(1)} %get-tuple-element.43), channel_id=1, source_target_pairs={{0,96},{16,112},{32,0},{48,16},{64,32},{80,48},{96,64},{112,80},{1... | collective-permute-start | bytes 245768 | tf_op jit(solution)/shard_map/ppermute | solution.py:68
  104.1 5.9 %collective-permute-start.20 = (bf16[128,640]{1,0:T(8,128)(2,1)S(1)}, bf16[128,640]{1,0:T(8,128)(2,1)S(1)}, u32[]{:S(2)}, u32[]{:S(2)}) collective-permute-start(bf16[128,640]{1,0:T(8,128)(2,1)S(1)} %copy-done.22), channel_id=1, source_target_pairs={{0,112},{16,0},{32,16},{48,32},{64,48},{80,64},{96,80},{112,96},{1... | collective-permute-start | bytes 491528 | tf_op jit(solution)/shard_map/ppermute | solution.py:68
  106.9 6.3 %collective-permute-start.26 = (bf16[128,640]{1,0:T(8,128)(2,1)S(1)}, bf16[128,640]{1,0:T(8,128)(2,1)S(1)}, u32[]{:S(2)}, u32[]{:S(2)}) collective-permute-start(bf16[128,640]{1,0:T(8,128)(2,1)S(1)} %pad_add_fusion), channel_id=1, source_target_pairs={{0,16},{16,32},{32,48},{48,64},{64,80},{80,96},{96,112},{112,0},{1... | collective-permute-start | bytes 491528 | tf_op jit(solution)/shard_map/ppermute | solution.py:68
  110.1 5.2 %collective-permute-start.22 = (bf16[128,640]{1,0:T(8,128)(2,1)S(1)}, bf16[128,640]{1,0:T(8,128)(2,1)S(1)}, u32[]{:S(2)}, u32[]{:S(2)}) collective-permute-start(bf16[128,640]{1,0:T(8,128)(2,1)S(1)} %pad_add_fusion.1), channel_id=1, source_target_pairs={{0,112},{16,0},{32,16},{48,32},{64,48},{80,64},{96,80},{112,96},{1... | collective-permute-start | bytes 491528 | tf_op jit(solution)/shard_map/ppermute | solution.py:68
  113.3 5.9 %collective-permute-start.27 = (bf16[128,640]{1,0:T(8,128)(2,1)S(1)}, bf16[128,640]{1,0:T(8,128)(2,1)S(1)}, u32[]{:S(2)}, u32[]{:S(2)}) collective-permute-start(bf16[128,640]{1,0:T(8,128)(2,1)S(1)} %add.115), channel_id=1, source_target_pairs={{0,16},{16,32},{32,48},{48,64},{64,80},{80,96},{96,112},{112,0},{1... | collective-permute-start | bytes 491528 | tf_op jit(solution)/shard_map/ppermute | solution.py:68
  115.4 5.8 %collective-permute-start.23 = (bf16[128,640]{1,0:T(8,128)(2,1)S(1)}, bf16[128,640]{1,0:T(8,128)(2,1)S(1)}, u32[]{:S(2)}, u32[]{:S(2)}) collective-permute-start(bf16[128,640]{1,0:T(8,128)(2,1)S(1)} %add.111), channel_id=1, source_target_pairs={{0,112},{16,0},{32,16},{48,32},{64,48},{80,64},{96,80},{112,96},{1... | collective-permute-start | bytes 491528 | tf_op jit(solution)/shard_map/ppermute | solution.py:68
  133.4 5.5 %collective-permute-start.30 = (f32[2,128]{1,0:T(2,128)S(1)}, f32[2,128]{1,0:T(2,128)S(1)}, u32[]{:S(2)}, u32[]{:S(2)}) collective-permute-start(f32[2,128]{1,0:T(2,128)S(1)} %pad_maximum_fusion.7), channel_id=1, source_target_pairs={{0,3},{1,2},{2,1},{3,0},{4,7},{5,6},{6,5},{7,4},{8,11},{9,10},{10,... | collective-permute-start | bytes 3080 | tf_op jit(solution)/shard_map/ppermute | solution.py:89
  135.8 3.9 %collective-permute-start.29 = (f32[2,128]{1,0:T(2,128)S(1)}, f32[2,128]{1,0:T(2,128)S(1)}, u32[]{:S(2)}, u32[]{:S(2)}) collective-permute-start(f32[2,128]{1,0:T(2,128)S(1)} %pad_maximum_fusion.7), channel_id=1, source_target_pairs={{0,2},{1,3},{2,0},{3,1},{4,6},{5,7},{6,4},{7,5},{8,10},{9,11},{10,... | collective-permute-start | bytes 3080 | tf_op jit(solution)/shard_map/ppermute | solution.py:89
  138.2 1.5 %collective-permute-start.28 = (f32[2,128]{1,0:T(2,128)S(1)}, f32[2,128]{1,0:T(2,128)S(1)}, u32[]{:S(2)}, u32[]{:S(2)}) collective-permute-start(f32[2,128]{1,0:T(2,128)S(1)} %pad_maximum_fusion.7), channel_id=1, source_target_pairs={{0,1},{1,0},{2,3},{3,2},{4,5},{5,4},{6,7},{7,6},{8,9},{9,8},{10,11... | collective-permute-start | bytes 3080 | tf_op jit(solution)/shard_map/ppermute | solution.py:89
  (24 other events, 252.5 us)
